TPU v7x, 32 devices: a whole 2x2x4 slice. The times are simulated.
32 devices in a mesh: tm: 4 (over z), space: 8 (over y, x, core).
Axes of the slice: x: 2, y: 2, z: 4, core: 2. Of those that a mesh axis runs over, the one named last changes fastest.
Arguments:
- starts: float32 [4, 4, 32, 64, 128], P('tm', None, 'space'), may hold values from -46 to 46
- flags: int32 [32, 64, 128], P('space'), may hold values from 0 to 2
Outputs:
- next_states: float32 [4, 4, 32, 64, 128], P('tm', None, 'space')
Inputs may be any that keep to these rules, and one draw needn't show every extreme that they name: `flags`: 0 marks a fluid cell, 1 a wall cell, 2 a free-surface cell.
All inputs are finite; a program needn't handle non-finite values.
Results may differ from a plain program's by a relative error of at most 0.0001.
Values sent between devices are 32-bit elements; how exact they have to be, the bound alone decides.
No kernel may reach another device: no remote copies, remote signals or barrier semaphores. Data moves between devices by JAX's collectives and lax.ppermute only.
A program may use at most 64 MiB of HBM per device.

v0:
```python
import jax
import jax.numpy as jnp
from jax import lax
from jax.sharding import PartitionSpec as P

FINE_STEPS = 8
COARSE_STEPS = 2


fine_dt = 0.12
coarse_dt = 0.48
coupling = 0.5


def extended(block, sides, width):
    for axis, dim in sides:
        count = lax.axis_size(axis)
        forward = [(i, i + 1) for i in range(count - 1)]
        backward = [(target, source) for source, target in forward]
        low = lax.ppermute(
            lax.slice_in_dim(block, block.shape[dim] - width, None, axis=dim), axis, forward
        )
        high = lax.ppermute(lax.slice_in_dim(block, 0, width, axis=dim), axis, backward)
        block = jnp.concatenate([low, block, high], axis=dim)
    return block


def from_behind(block, axis, distance):
    devices = range(lax.axis_size(axis))
    route = [(i - distance, i) for i in devices if i - distance in devices]
    return lax.ppermute(block, axis, route)


def offset_cut(values, along, offset):
    bounds = [slice(1, -1)] * 3
    bounds[along] = slice(1 + offset, values.shape[along] - 1 + offset)
    return values[tuple(bounds)]


def central(values, along, spacing):
    return (offset_cut(values, along, 1) - offset_cut(values, along, -1)) / (2.0 * spacing)


def laplace(values, spacings, middle):
    total = jnp.zeros_like(middle)
    for along in range(3):
        total = (
            total
            + (offset_cut(values, along, 1) + offset_cut(values, along, -1) - 2.0 * middle)
            / spacings[along] ** 2
        )
    return total


def advance(padded, keep_velocity, keep_shear, delta, spacings, layout):
    axis_x, axis_y, axis_z = layout
    velocity, shear_x, shear_y, normal = (padded[0], padded[1], padded[2], padded[3])
    mids = [offset_cut(padded[k], 0, 0) for k in range(4)]
    grad_x = central(velocity, axis_x, spacings[axis_x])
    grad_y = central(velocity, axis_y, spacings[axis_y])
    grad_z = central(velocity, axis_z, spacings[axis_z])
    diverge = (
        central(shear_x, axis_x, spacings[axis_x])
        + central(shear_y, axis_y, spacings[axis_y])
        + central(normal, axis_z, spacings[axis_z])
    )
    new_velocity = mids[0] + delta * (laplace(velocity, spacings, mids[0]) + coupling * diverge)
    new_shear_x = mids[1] + delta * (
        grad_x + mids[1] * grad_z - mids[1] + laplace(shear_x, spacings, mids[1])
    )
    new_shear_y = mids[2] + delta * (
        grad_y + mids[2] * grad_z - mids[2] + laplace(shear_y, spacings, mids[2])
    )
    new_normal = mids[3] + delta * (
        2.0 * (grad_x * mids[1] + grad_y * mids[2] + grad_z * mids[3])
        - (mids[3] - 1.0)
        + laplace(normal, spacings, mids[3])
    )
    return jnp.stack(
        [
            new_velocity * keep_velocity,
            new_shear_x * keep_shear,
            new_shear_y * keep_shear,
            new_normal,
        ]
    )


def side_pad(fields):
    return jnp.pad(fields, ((0, 0), (0, 0), (1, 1), (1, 1)))


def coarse_step_padded(padded):
    return advance(side_pad(padded), 1.0, 1.0, coarse_dt, (2.0, 16.0, 2.0), (0, 2, 1))


def coarse_spread(fields):
    for _ in range(COARSE_STEPS):
        padded = extended(fields, (("space", 1),), 1)
        fields = coarse_step_padded(padded)
    return fields


def restrict(fields):
    count, xs, ys, zs = fields.shape
    blocks = fields.reshape(count, xs // 2, 2, ys // 2, 2, zs // 16, 16)
    return jnp.transpose(jnp.mean(blocks, axis=(2, 4, 6)), (0, 1, 3, 2))


def prolong(coarse, fine_shape):
    count, xs, ys, zs = fine_shape
    grid = jnp.transpose(coarse, (0, 1, 3, 2))
    wide = jnp.broadcast_to(
        grid[:, :, None, :, None, :, None], (count, xs // 2, 2, ys // 2, 2, zs // 16, 16)
    )
    return wide.reshape(fine_shape)


def local(starts, flags):
    keep_velocity = (flags != 1).astype(jnp.float32)
    keep_shear = (flags != 2).astype(jnp.float32)
    opening = starts[0]
    fields = opening
    for _ in range(FINE_STEPS):
        padded = extended(fields, (("space", 1),), 1)
        fields = advance(
            side_pad(padded), keep_velocity, keep_shear, fine_dt, (1.0, 1.0, 1.0), (0, 1, 2)
        )
    coarse_start = restrict(opening)
    coarse_end = restrict(fields)
    first_time = lax.axis_index("tm") == 0
    guess_old = coarse_spread(coarse_start)
    incoming = coarse_start
    for _ in range(lax.axis_size("tm") - 1):
        outgoing = coarse_spread(incoming) + (coarse_end - guess_old)
        received = from_behind(outgoing, "tm", 1)
        incoming = jnp.where(first_time, coarse_start, received)
    change = coarse_spread(incoming) - guess_old
    return (fields + prolong(change, fields.shape))[None]


def solution(mesh):
    return jax.shard_map(
        local,
        mesh=mesh,
        in_specs=(P("tm", None, "space", None, None), P("space", None, None)),
        out_specs=P("tm", None, "space", None, None),
        check_vma=False,
    )
```

profile of v0, /device:TPU:11, one launch (start us, length us, event | category | flops | bytes accessed | tf_op | source)
XLA Modules:
  0.0 195.9 jit_solution(13459829161188613332)
XLA Ops:
  0.0 3.7 %reshape_squeeze.3 = f32[4,2,2,32,2,8,16]{6,5,4,3,2,1,0:T(8,128)} reshape(f32[1,4,4,64,128]{4,3,2,1,0:T(8,128)} %param.2) | data formatting | bytes 1048576 | tf_op jit(solution)/shard_map/reshape;squeeze | solution.py:106
  6.5 3.7 %collective-permute-start.16 = (f32[4,1,8,32]{3,2,1,0:T(8,128)S(1)}, f32[4,1,8,32]{3,2,1,0:T(8,128)S(1)}, u32[]{:S(2)}, u32[]{:S(2)}) collective-permute-start(f32[4,1,8,32]{3,2,1,0:T(8,128)S(1)} %get-tuple-element.103), channel_id=1, source_target_pairs={{0,1},{1,2},{2,3},{3,4},{4,5},{5,6},{6,7},{8,9},{9,10},{10,11},{11... | collective-permute-start | bytes 12296 | tf_op jit(solution)/shard_map/ppermute | solution.py:20
  12.1 4.5 %collective-permute-start = (f32[4,1,64,128]{3,2,1,0:T(8,128)S(1)}, f32[4,1,64,128]{3,2,1,0:T(8,128)S(1)}, u32[]{:S(2)}, u32[]{:S(2)}) collective-permute-start(f32[4,1,64,128]{3,2,1,0:T(8,128)S(1)} %get-tuple-element.55), channel_id=1, source_target_pairs={{0,1},{1,2},{2,3},{3,4},{4,5},{5,6},{6,7},{8,9},{9,10},{10,11},{11... | collective-permute-start | bytes 393224 | tf_op jit(solution)/shard_map/ppermute | solution.py:20
  19.1 4.8 %collective-permute-done.1 = f32[4,1,64,128]{3,2,1,0:T(8,128)S(1)} collective-permute-done((f32[4,1,64,128]{3,2,1,0:T(8,128)S(1)}, f32[4,1,64,128]{3,2,1,0:T(8,128)S(1)}, u32[]{:S(2)}, u32[]{:S(2)}) %collective-permute-start.1) | collective-permute-done | bytes 131104 | tf_op jit(solution)/shard_map/ppermute | solution.py:23
  31.2 4.6 %collective-permute-done.3 = f32[4,1,64,128]{3,2,1,0:T(8,128)S(1)} collective-permute-done((f32[4,1,64,128]{3,2,1,0:T(8,128)S(1)}, f32[4,1,64,128]{3,2,1,0:T(8,128)S(1)}, u32[]{:S(2)}, u32[]{:S(2)}) %collective-permute-start.3) | collective-permute-done | bytes 131104 | tf_op jit(solution)/shard_map/ppermute | solution.py:23
  42.7 4.1 %collective-permute-start.18 = (f32[4,1,8,32]{3,2,1,0:T(8,128)S(1)}, f32[4,1,8,32]{3,2,1,0:T(8,128)S(1)}, u32[]{:S(2)}, u32[]{:S(2)}) collective-permute-start(f32[4,1,8,32]{3,2,1,0:T(8,128)S(1)} %get-tuple-element.101), channel_id=1, source_target_pairs={{0,1},{1,2},{2,3},{3,4},{4,5},{5,6},{6,7},{8,9},{9,10},{10,11},{11... | collective-permute-start | bytes 12296 | tf_op jit(solution)/shard_map/ppermute | solution.py:20
  48.7 4.0 %collective-permute-done.19 = f32[4,1,8,32]{3,2,1,0:T(8,128)S(1)} collective-permute-done((f32[4,1,8,32]{3,2,1,0:T(8,128)S(1)}, f32[4,1,8,32]{3,2,1,0:T(8,128)S(1)}, u32[]{:S(2)}, u32[]{:S(2)}) %collective-permute-start.19) | collective-permute-done | bytes 4128 | tf_op jit(solution)/shard_map/ppermute | solution.py:23
  59.9 4.6 %collective-permute-done.7 = f32[4,1,64,128]{3,2,1,0:T(8,128)S(1)} collective-permute-done((f32[4,1,64,128]{3,2,1,0:T(8,128)S(1)}, f32[4,1,64,128]{3,2,1,0:T(8,128)S(1)}, u32[]{:S(2)}, u32[]{:S(2)}) %collective-permute-start.7) | collective-permute-done | bytes 131104 | tf_op jit(solution)/shard_map/ppermute | solution.py:23
  71.4 4.7 %collective-permute-done.9 = f32[4,1,64,128]{3,2,1,0:T(8,128)S(1)} collective-permute-done((f32[4,1,64,128]{3,2,1,0:T(8,128)S(1)}, f32[4,1,64,128]{3,2,1,0:T(8,128)S(1)}, u32[]{:S(2)}, u32[]{:S(2)}) %collective-permute-start.9) | collective-permute-done | bytes 131104 | tf_op jit(solution)/shard_map/ppermute | solution.py:23
  83.0 4.7 %collective-permute-done.11 = f32[4,1,64,128]{3,2,1,0:T(8,128)S(1)} collective-permute-done((f32[4,1,64,128]{3,2,1,0:T(8,128)S(1)}, f32[4,1,64,128]{3,2,1,0:T(8,128)S(1)}, u32[]{:S(2)}, u32[]{:S(2)}) %collective-permute-start.11) | collective-permute-done | bytes 131104 | tf_op jit(solution)/shard_map/ppermute | solution.py:23
  95.2 4.1 %collective-permute-done.13 = f32[4,1,64,128]{3,2,1,0:T(8,128)S(1)} collective-permute-done((f32[4,1,64,128]{3,2,1,0:T(8,128)S(1)}, f32[4,1,64,128]{3,2,1,0:T(8,128)S(1)}, u32[]{:S(2)}, u32[]{:S(2)}) %collective-permute-start.13) | collective-permute-done | bytes 131104 | tf_op jit(solution)/shard_map/ppermute | solution.py:23
  107.0 3.9 %collective-permute-done.15 = f32[4,1,64,128]{3,2,1,0:T(8,128)S(1)} collective-permute-done((f32[4,1,64,128]{3,2,1,0:T(8,128)S(1)}, f32[4,1,64,128]{3,2,1,0:T(8,128)S(1)}, u32[]{:S(2)}, u32[]{:S(2)}) %collective-permute-start.15) | collective-permute-done | bytes 131104 | tf_op jit(solution)/shard_map/ppermute | solution.py:23
  120.4 3.2 %collective-permute-start.20 = (f32[4,2,8,32]{3,2,1,0:T(8,128)S(1)}, f32[4,2,8,32]{3,2,1,0:T(8,128)S(1)}, u32[]{:S(2)}, u32[]{:S(2)}) collective-permute-start(f32[4,2,8,32]{3,2,1,0:T(8,128)S(1)} %fusion.212), channel_id=1, source_target_pairs={{0,8},{8,16},{16,24},{1,9},{9,17},{17,25},{2,10},{10,18},{18,26},{... | collective-permute-start | bytes 24584 | tf_op jit(solution)/shard_map/ppermute | solution.py:31
  130.7 4.0 %collective-permute-done.22 = f32[4,1,8,32]{3,2,1,0:T(8,128)S(1)} collective-permute-done((f32[4,1,8,32]{3,2,1,0:T(8,128)S(1)}, f32[4,1,8,32]{3,2,1,0:T(8,128)S(1)}, u32[]{:S(2)}, u32[]{:S(2)}) %collective-permute-start.22) | collective-permute-done | bytes 4128 | tf_op jit(solution)/shard_map/ppermute | solution.py:23
  139.7 3.5 %collective-permute-done.24 = f32[4,1,8,32]{3,2,1,0:T(8,128)S(1)} collective-permute-done((f32[4,1,8,32]{3,2,1,0:T(8,128)S(1)}, f32[4,1,8,32]{3,2,1,0:T(8,128)S(1)}, u32[]{:S(2)}, u32[]{:S(2)}) %collective-permute-start.24) | collective-permute-done | bytes 4128 | tf_op jit(solution)/shard_map/ppermute | solution.py:23
  143.8 3.2 %collective-permute-start.25 = (f32[4,2,8,32]{3,2,1,0:T(8,128)S(1)}, f32[4,2,8,32]{3,2,1,0:T(8,128)S(1)}, u32[]{:S(2)}, u32[]{:S(2)}) collective-permute-start(f32[4,2,8,32]{3,2,1,0:T(8,128)S(1)} %maximum_add_fusion.1), channel_id=1, source_target_pairs={{0,8},{8,16},{16,24},{1,9},{9,17},{17,25},{2,10},{10,18},{18,26},{... | collective-permute-start | bytes 24584 | tf_op jit(solution)/shard_map/ppermute | solution.py:31
  148.5 3.1 %collective-permute-start.26 = (f32[4,1,8,32]{3,2,1,0:T(8,128)S(1)}, f32[4,1,8,32]{3,2,1,0:T(8,128)S(1)}, u32[]{:S(2)}, u32[]{:S(2)}) collective-permute-start(f32[4,1,8,32]{3,2,1,0:T(8,128)S(1)} %get-tuple-element.95), channel_id=1, source_target_pairs={{0,1},{1,2},{2,3},{3,4},{4,5},{5,6},{6,7},{8,9},{9,10},{10,11},{11... | collective-permute-start | bytes 12296 | tf_op jit(solution)/shard_map/ppermute | solution.py:20
  153.5 4.0 %collective-permute-done.27 = f32[4,1,8,32]{3,2,1,0:T(8,128)S(1)} collective-permute-done((f32[4,1,8,32]{3,2,1,0:T(8,128)S(1)}, f32[4,1,8,32]{3,2,1,0:T(8,128)S(1)}, u32[]{:S(2)}, u32[]{:S(2)}) %collective-permute-start.27) | collective-permute-done | bytes 4128 | tf_op jit(solution)/shard_map/ppermute | solution.py:23
  162.4 3.5 %collective-permute-done.29 = f32[4,1,8,32]{3,2,1,0:T(8,128)S(1)} collective-permute-done((f32[4,1,8,32]{3,2,1,0:T(8,128)S(1)}, f32[4,1,8,32]{3,2,1,0:T(8,128)S(1)}, u32[]{:S(2)}, u32[]{:S(2)}) %collective-permute-start.29) | collective-permute-done | bytes 4128 | tf_op jit(solution)/shard_map/ppermute | solution.py:23
  166.6 3.2 %collective-permute-start.30 = (f32[4,2,8,32]{3,2,1,0:T(8,128)S(1)}, f32[4,2,8,32]{3,2,1,0:T(8,128)S(1)}, u32[]{:S(2)}, u32[]{:S(2)}) collective-permute-start(f32[4,2,8,32]{3,2,1,0:T(8,128)S(1)} %maximum_add_fusion.2), channel_id=1, source_target_pairs={{0,8},{8,16},{16,24},{1,9},{9,17},{17,25},{2,10},{10,18},{18,26},{... | collective-permute-start | bytes 24584 | tf_op jit(solution)/shard_map/ppermute | solution.py:31
  171.2 3.1 %collective-permute-start.31 = (f32[4,1,8,32]{3,2,1,0:T(8,128)S(1)}, f32[4,1,8,32]{3,2,1,0:T(8,128)S(1)}, u32[]{:S(2)}, u32[]{:S(2)}) collective-permute-start(f32[4,1,8,32]{3,2,1,0:T(8,128)S(1)} %get-tuple-element.91), channel_id=1, source_target_pairs={{0,1},{1,2},{2,3},{3,4},{4,5},{5,6},{6,7},{8,9},{9,10},{10,11},{11... | collective-permute-start | bytes 12296 | tf_op jit(solution)/shard_map/ppermute | solution.py:20
  176.3 4.0 %collective-permute-done.32 = f32[4,1,8,32]{3,2,1,0:T(8,128)S(1)} collective-permute-done((f32[4,1,8,32]{3,2,1,0:T(8,128)S(1)}, f32[4,1,8,32]{3,2,1,0:T(8,128)S(1)}, u32[]{:S(2)}, u32[]{:S(2)}) %collective-permute-start.32) | collective-permute-done | bytes 4128 | tf_op jit(solution)/shard_map/ppermute | solution.py:23
  185.2 3.5 %collective-permute-done.34 = f32[4,1,8,32]{3,2,1,0:T(8,128)S(1)} collective-permute-done((f32[4,1,8,32]{3,2,1,0:T(8,128)S(1)}, f32[4,1,8,32]{3,2,1,0:T(8,128)S(1)}, u32[]{:S(2)}, u32[]{:S(2)}) %collective-permute-start.34) | collective-permute-done | bytes 4128 | tf_op jit(solution)/shard_map/ppermute | solution.py:23
  191.7 3.3 %reshape.79 = f32[1,4,4,64,128]{4,3,2,1,0:T(8,128)S(1)} reshape(f32[4,2,2,32,2,8,16]{6,5,4,3,2,1,0:T(8,128)} %broadcast_in_dim.2) | data formatting | bytes 1048576 | tf_op jit(solution)/shard_map/reshape | solution.py:116
  (199 shorter events, 101.5 us)
Async XLA Ops:
  6.5 12.1 %collective-permute-start.16 = (f32[4,1,8,32]{3,2,1,0:T(8,128)S(1)}, f32[4,1,8,32]{3,2,1,0:T(8,128)S(1)}, u32[]{:S(2)}, u32[]{:S(2)}) collective-permute-start(f32[4,1,8,32]{3,2,1,0:T(8,128)S(1)} %get-tuple-element.103), channel_id=1, source_target_pairs={{0,1},{1,2},{2,3},{3,4},{4,5},{5,6},{6,7},{8,9},{9,10},{10,11},{11... | collective-permute-start | bytes 12296 | tf_op jit(solution)/shard_map/ppermute | solution.py:20
  10.2 8.5 %collective-permute-start.17 = (f32[4,1,8,32]{3,2,1,0:T(8,128)S(1)}, f32[4,1,8,32]{3,2,1,0:T(8,128)S(1)}, u32[]{:S(2)}, u32[]{:S(2)}) collective-permute-start(f32[4,1,8,32]{3,2,1,0:T(8,128)S(1)} %get-tuple-element.104), channel_id=1, source_target_pairs={{1,0},{2,1},{3,2},{4,3},{5,4},{6,5},{7,6},{9,8},{10,9},{11,10},{12... | collective-permute-start | bytes 12296 | tf_op jit(solution)/shard_map/ppermute | solution.py:23
  12.1 6.9 %collective-permute-start = (f32[4,1,64,128]{3,2,1,0:T(8,128)S(1)}, f32[4,1,64,128]{3,2,1,0:T(8,128)S(1)}, u32[]{:S(2)}, u32[]{:S(2)}) collective-permute-start(f32[4,1,64,128]{3,2,1,0:T(8,128)S(1)} %get-tuple-element.55), channel_id=1, source_target_pairs={{0,1},{1,2},{2,3},{3,4},{4,5},{5,6},{6,7},{8,9},{9,10},{10,11},{11... | collective-permute-start | bytes 393224 | tf_op jit(solution)/shard_map/ppermute | solution.py:20
  16.7 7.2 %collective-permute-start.1 = (f32[4,1,64,128]{3,2,1,0:T(8,128)S(1)}, f32[4,1,64,128]{3,2,1,0:T(8,128)S(1)}, u32[]{:S(2)}, u32[]{:S(2)}) collective-permute-start(f32[4,1,64,128]{3,2,1,0:T(8,128)S(1)} %get-tuple-element.56), channel_id=1, source_target_pairs={{1,0},{2,1},{3,2},{4,3},{5,4},{6,5},{7,6},{9,8},{10,9},{11,10},{12... | collective-permute-start | bytes 393224 | tf_op jit(solution)/shard_map/ppermute | solution.py:23
  28.6 7.2 %collective-permute-start.3 = (f32[4,1,64,128]{3,2,1,0:T(8,128)S(1)}, f32[4,1,64,128]{3,2,1,0:T(8,128)S(1)}, u32[]{:S(2)}, u32[]{:S(2)}) collective-permute-start(f32[4,1,64,128]{3,2,1,0:T(8,128)S(1)} %get-tuple-element.54), channel_id=1, source_target_pairs={{1,0},{2,1},{3,2},{4,3},{5,4},{6,5},{7,6},{9,8},{10,9},{11,10},{12... | collective-permute-start | bytes 393224 | tf_op jit(solution)/shard_map/ppermute | solution.py:23
  38.3 14.5 %collective-permute-start.4 = (f32[4,1,64,128]{3,2,1,0:T(8,128)S(1)}, f32[4,1,64,128]{3,2,1,0:T(8,128)S(1)}, u32[]{:S(2)}, u32[]{:S(2)}) collective-permute-start(f32[4,1,64,128]{3,2,1,0:T(8,128)S(1)} %get-tuple-element.51), channel_id=1, source_target_pairs={{0,1},{1,2},{2,3},{3,4},{4,5},{5,6},{6,7},{8,9},{9,10},{10,11},{11... | collective-permute-start | bytes 393224 | tf_op jit(solution)/shard_map/ppermute | solution.py:20
  40.2 12.6 %collective-permute-start.5 = (f32[4,1,64,128]{3,2,1,0:T(8,128)S(1)}, f32[4,1,64,128]{3,2,1,0:T(8,128)S(1)}, u32[]{:S(2)}, u32[]{:S(2)}) collective-permute-start(f32[4,1,64,128]{3,2,1,0:T(8,128)S(1)} %get-tuple-element.52), channel_id=1, source_target_pairs={{1,0},{2,1},{3,2},{4,3},{5,4},{6,5},{7,6},{9,8},{10,9},{11,10},{12... | collective-permute-start | bytes 393224 | tf_op jit(solution)/shard_map/ppermute | solution.py:23
  42.7 6.0 %collective-permute-start.18 = (f32[4,1,8,32]{3,2,1,0:T(8,128)S(1)}, f32[4,1,8,32]{3,2,1,0:T(8,128)S(1)}, u32[]{:S(2)}, u32[]{:S(2)}) collective-permute-start(f32[4,1,8,32]{3,2,1,0:T(8,128)S(1)} %get-tuple-element.101), channel_id=1, source_target_pairs={{0,1},{1,2},{2,3},{3,4},{4,5},{5,6},{6,7},{8,9},{9,10},{10,11},{11... | collective-permute-start | bytes 12296 | tf_op jit(solution)/shard_map/ppermute | solution.py:20
  46.7 6.0 %collective-permute-start.19 = (f32[4,1,8,32]{3,2,1,0:T(8,128)S(1)}, f32[4,1,8,32]{3,2,1,0:T(8,128)S(1)}, u32[]{:S(2)}, u32[]{:S(2)}) collective-permute-start(f32[4,1,8,32]{3,2,1,0:T(8,128)S(1)} %get-tuple-element.102), channel_id=1, source_target_pairs={{1,0},{2,1},{3,2},{4,3},{5,4},{6,5},{7,6},{9,8},{10,9},{11,10},{12... | collective-permute-start | bytes 12296 | tf_op jit(solution)/shard_map/ppermute | solution.py:23
  57.3 7.2 %collective-permute-start.7 = (f32[4,1,64,128]{3,2,1,0:T(8,128)S(1)}, f32[4,1,64,128]{3,2,1,0:T(8,128)S(1)}, u32[]{:S(2)}, u32[]{:S(2)}) collective-permute-start(f32[4,1,64,128]{3,2,1,0:T(8,128)S(1)} %get-tuple-element.50), channel_id=1, source_target_pairs={{1,0},{2,1},{3,2},{4,3},{5,4},{6,5},{7,6},{9,8},{10,9},{11,10},{12... | collective-permute-start | bytes 393224 | tf_op jit(solution)/shard_map/ppermute | solution.py:23
  68.9 7.2 %collective-permute-start.9 = (f32[4,1,64,128]{3,2,1,0:T(8,128)S(1)}, f32[4,1,64,128]{3,2,1,0:T(8,128)S(1)}, u32[]{:S(2)}, u32[]{:S(2)}) collective-permute-start(f32[4,1,64,128]{3,2,1,0:T(8,128)S(1)} %get-tuple-element.48), channel_id=1, source_target_pairs={{1,0},{2,1},{3,2},{4,3},{5,4},{6,5},{7,6},{9,8},{10,9},{11,10},{12... | collective-permute-start | bytes 393224 | tf_op jit(solution)/shard_map/ppermute | solution.py:23
  80.5 7.2 %collective-permute-start.11 = (f32[4,1,64,128]{3,2,1,0:T(8,128)S(1)}, f32[4,1,64,128]{3,2,1,0:T(8,128)S(1)}, u32[]{:S(2)}, u32[]{:S(2)}) collective-permute-start(f32[4,1,64,128]{3,2,1,0:T(8,128)S(1)} %get-tuple-element.46), channel_id=1, source_target_pairs={{1,0},{2,1},{3,2},{4,3},{5,4},{6,5},{7,6},{9,8},{10,9},{11,10},{12... | collective-permute-start | bytes 393224 | tf_op jit(solution)/shard_map/ppermute | solution.py:23
  90.1 5.0 %collective-permute-start.12 = (f32[4,1,64,128]{3,2,1,0:T(8,128)S(1)}, f32[4,1,64,128]{3,2,1,0:T(8,128)S(1)}, u32[]{:S(2)}, u32[]{:S(2)}) collective-permute-start(f32[4,1,64,128]{3,2,1,0:T(8,128)S(1)} %get-tuple-element.43), channel_id=1, source_target_pairs={{0,1},{1,2},{2,3},{3,4},{4,5},{5,6},{6,7},{8,9},{9,10},{10,11},{11... | collective-permute-start | bytes 393224 | tf_op jit(solution)/shard_map/ppermute | solution.py:20
  92.1 7.2 %collective-permute-start.13 = (f32[4,1,64,128]{3,2,1,0:T(8,128)S(1)}, f32[4,1,64,128]{3,2,1,0:T(8,128)S(1)}, u32[]{:S(2)}, u32[]{:S(2)}) collective-permute-start(f32[4,1,64,128]{3,2,1,0:T(8,128)S(1)} %get-tuple-element.44), channel_id=1, source_target_pairs={{1,0},{2,1},{3,2},{4,3},{5,4},{6,5},{7,6},{9,8},{10,9},{11,10},{12... | collective-permute-start | bytes 393224 | tf_op jit(solution)/shard_map/ppermute | solution.py:23
  101.7 5.3 %collective-permute-start.14 = (f32[4,1,64,128]{3,2,1,0:T(8,128)S(1)}, f32[4,1,64,128]{3,2,1,0:T(8,128)S(1)}, u32[]{:S(2)}, u32[]{:S(2)}) collective-permute-start(f32[4,1,64,128]{3,2,1,0:T(8,128)S(1)} %get-tuple-element.41), channel_id=1, source_target_pairs={{0,1},{1,2},{2,3},{3,4},{4,5},{5,6},{6,7},{8,9},{9,10},{10,11},{11... | collective-permute-start | bytes 393224 | tf_op jit(solution)/shard_map/ppermute | solution.py:20
  103.7 7.2 %collective-permute-start.15 = (f32[4,1,64,128]{3,2,1,0:T(8,128)S(1)}, f32[4,1,64,128]{3,2,1,0:T(8,128)S(1)}, u32[]{:S(2)}, u32[]{:S(2)}) collective-permute-start(f32[4,1,64,128]{3,2,1,0:T(8,128)S(1)} %get-tuple-element.42), channel_id=1, source_target_pairs={{1,0},{2,1},{3,2},{4,3},{5,4},{6,5},{7,6},{9,8},{10,9},{11,10},{12... | collective-permute-start | bytes 393224 | tf_op jit(solution)/shard_map/ppermute | solution.py:23
  128.8 6.0 %collective-permute-start.22 = (f32[4,1,8,32]{3,2,1,0:T(8,128)S(1)}, f32[4,1,8,32]{3,2,1,0:T(8,128)S(1)}, u32[]{:S(2)}, u32[]{:S(2)}) collective-permute-start(f32[4,1,8,32]{3,2,1,0:T(8,128)S(1)} %get-tuple-element.100), channel_id=1, source_target_pairs={{1,0},{2,1},{3,2},{4,3},{5,4},{6,5},{7,6},{9,8},{10,9},{11,10},{12... | collective-permute-start | bytes 12296 | tf_op jit(solution)/shard_map/ppermute | solution.py:23
  137.3 6.0 %collective-permute-start.24 = (f32[4,1,8,32]{3,2,1,0:T(8,128)S(1)}, f32[4,1,8,32]{3,2,1,0:T(8,128)S(1)}, u32[]{:S(2)}, u32[]{:S(2)}) collective-permute-start(f32[4,1,8,32]{3,2,1,0:T(8,128)S(1)} %get-tuple-element.98), channel_id=1, source_target_pairs={{1,0},{2,1},{3,2},{4,3},{5,4},{6,5},{7,6},{9,8},{10,9},{11,10},{12... | collective-permute-start | bytes 12296 | tf_op jit(solution)/shard_map/ppermute | solution.py:23
  148.5 5.0 %collective-permute-start.26 = (f32[4,1,8,32]{3,2,1,0:T(8,128)S(1)}, f32[4,1,8,32]{3,2,1,0:T(8,128)S(1)}, u32[]{:S(2)}, u32[]{:S(2)}) collective-permute-start(f32[4,1,8,32]{3,2,1,0:T(8,128)S(1)} %get-tuple-element.95), channel_id=1, source_target_pairs={{0,1},{1,2},{2,3},{3,4},{4,5},{5,6},{6,7},{8,9},{9,10},{10,11},{11... | collective-permute-start | bytes 12296 | tf_op jit(solution)/shard_map/ppermute | solution.py:20
  151.6 6.0 %collective-permute-start.27 = (f32[4,1,8,32]{3,2,1,0:T(8,128)S(1)}, f32[4,1,8,32]{3,2,1,0:T(8,128)S(1)}, u32[]{:S(2)}, u32[]{:S(2)}) collective-permute-start(f32[4,1,8,32]{3,2,1,0:T(8,128)S(1)} %get-tuple-element.96), channel_id=1, source_target_pairs={{1,0},{2,1},{3,2},{4,3},{5,4},{6,5},{7,6},{9,8},{10,9},{11,10},{12... | collective-permute-start | bytes 12296 | tf_op jit(solution)/shard_map/ppermute | solution.py:23
  160.0 6.0 %collective-permute-start.29 = (f32[4,1,8,32]{3,2,1,0:T(8,128)S(1)}, f32[4,1,8,32]{3,2,1,0:T(8,128)S(1)}, u32[]{:S(2)}, u32[]{:S(2)}) collective-permute-start(f32[4,1,8,32]{3,2,1,0:T(8,128)S(1)} %get-tuple-element.94), channel_id=1, source_target_pairs={{1,0},{2,1},{3,2},{4,3},{5,4},{6,5},{7,6},{9,8},{10,9},{11,10},{12... | collective-permute-start | bytes 12296 | tf_op jit(solution)/shard_map/ppermute | solution.py:23
  171.2 5.0 %collective-permute-start.31 = (f32[4,1,8,32]{3,2,1,0:T(8,128)S(1)}, f32[4,1,8,32]{3,2,1,0:T(8,128)S(1)}, u32[]{:S(2)}, u32[]{:S(2)}) collective-permute-start(f32[4,1,8,32]{3,2,1,0:T(8,128)S(1)} %get-tuple-element.91), channel_id=1, source_target_pairs={{0,1},{1,2},{2,3},{3,4},{4,5},{5,6},{6,7},{8,9},{9,10},{10,11},{11... | collective-permute-start | bytes 12296 | tf_op jit(solution)/shard_map/ppermute | solution.py:20
  174.3 6.0 %collective-permute-start.32 = (f32[4,1,8,32]{3,2,1,0:T(8,128)S(1)}, f32[4,1,8,32]{3,2,1,0:T(8,128)S(1)}, u32[]{:S(2)}, u32[]{:S(2)}) collective-permute-start(f32[4,1,8,32]{3,2,1,0:T(8,128)S(1)} %get-tuple-element.92), channel_id=1, source_target_pairs={{1,0},{2,1},{3,2},{4,3},{5,4},{6,5},{7,6},{9,8},{10,9},{11,10},{12... | collective-permute-start | bytes 12296 | tf_op jit(solution)/shard_map/ppermute | solution.py:23
  182.8 6.0 %collective-permute-start.34 = (f32[4,1,8,32]{3,2,1,0:T(8,128)S(1)}, f32[4,1,8,32]{3,2,1,0:T(8,128)S(1)}, u32[]{:S(2)}, u32[]{:S(2)}) collective-permute-start(f32[4,1,8,32]{3,2,1,0:T(8,128)S(1)} %get-tuple-element.90), channel_id=1, source_target_pairs={{1,0},{2,1},{3,2},{4,3},{5,4},{6,5},{7,6},{9,8},{10,9},{11,10},{12... | collective-permute-start | bytes 12296 | tf_op jit(solution)/shard_map/ppermute | solution.py:23
  (19 other events, 161.0 us)
where the time goes:
time: 197 us; the launch traced here: 196 us
  starting transfers between devices  86.2 us (44%)
  waiting for transfers between devices  62.3 us (32%)
  other arithmetic  30.8 us (16%)
  local copies, waits for them, and re-layouts  15.2 us (8%)
    ppermute x16, waiting for transfers between devices, extended(): lax.ppermute(lax.slice_in_dim(block, 0, width, axis=dim), axis, backward)  58 us
    ppermute x16, starting transfers between devices, extended(): lax.ppermute(lax.slice_in_dim(block, block.shape[dim] - width, None, axis...  40.6 us
    ppermute x16, starting transfers between devices, extended(): lax.ppermute(lax.slice_in_dim(block, 0, width, axis=dim), axis, backward)  35.9 us
    another operation x64, other arithmetic, advance(): jnp.stack([new_velocity * keep_velocity, new_shear_x * keep_shear, new_sh...  16.4 us
    ppermute x3, starting transfers between devices, from_behind(): return lax.ppermute(block, axis, route)  9.61 us
    concatenate x16, other arithmetic, extended(): block = jnp.concatenate([low, block, high], axis=dim)  5.09 us
    reduce_sum x2, other arithmetic, restrict(): return jnp.transpose(jnp.mean(blocks, axis=(2, 4, 6)), (0, 1, 3, 2))  5.01 us
    ppermute x3, waiting for transfers between devices, from_behind(): return lax.ppermute(block, axis, route)  4.33 us
  transfers between devices with their start and end apart: 35, of which 17 were waited for; matrix products, arithmetic and copies ran while one was open for 1% of the time, Pallas kernels for 0%

commit v1 on v0

v1 whole, which is shorter than its diff:
```python
import functools

import jax
import jax.numpy as jnp
from jax import lax
from jax.experimental import pallas as pl
from jax.experimental.pallas import tpu as pltpu
from jax.sharding import PartitionSpec as P

FINE_STEPS = 8
COARSE_STEPS = 2

fine_dt = 0.12
coarse_dt = 0.48

FIELDS = 4
PLANES = 4
NY = 64
NZ = 128
REACH = FINE_STEPS // PLANES
BLOCKS = 2 * REACH + 1
WINDOW = BLOCKS * PLANES
TOP = 8
CHUNK = 16
F32 = jnp.float32
HIGHEST = lax.Precision.HIGHEST
VMEM = pl.BlockSpec(memory_space=pltpu.VMEM)
ANY = pl.BlockSpec(memory_space=pl.ANY)
LIMIT = 48 * 2**20


def iota(shape, dim):
    return lax.broadcasted_iota(jnp.int32, shape, dim)


def pick_rows(shape):
    return ((iota(shape, 0) % NY) // 2 % 16 == iota(shape, 1) // 8).astype(F32)


def packed_mean(pairs):
    stacked = jnp.concatenate(pairs, axis=0)
    gather = (iota((NZ, NZ), 0) // 16 == iota((NZ, NZ), 1) % 8).astype(F32)
    sums = jnp.dot(stacked, gather, precision=HIGHEST, preferred_element_type=F32)
    sums = sums * pick_rows(sums.shape)
    rows = sums.shape[0] // 32
    return jnp.sum(sums.reshape(rows, 32, NZ), axis=1) * (1.0 / 64.0)


def restrict_kernel(starts, packed):
    pairs = [starts[0, f, 2 * x] + starts[0, f, 2 * x + 1] for f in range(FIELDS) for x in range(PLANES // 2)]
    packed[...] = packed_mean(pairs)


def fine_step(src, keep, plane, store):
    beta = 1.0 / fine_dt - 7.0
    alpha = 1.0 / fine_dt - 6.0
    for r0 in range(0, NY, CHUNK):
        lane = iota((CHUNK, NZ), 1)
        mid, lo_x, hi_x, lo_y, hi_y, lo_z, hi_z = [], [], [], [], [], [], []
        for f in range(FIELDS):
            v = src[f, plane, pl.ds(TOP + r0, CHUNK), :]
            mid.append(v)
            lo_x.append(src[f, plane - 1, pl.ds(TOP + r0, CHUNK), :])
            hi_x.append(src[f, plane + 1, pl.ds(TOP + r0, CHUNK), :])
            lo_y.append(src[f, plane, pl.ds(TOP + r0 - 1, CHUNK), :])
            hi_y.append(src[f, plane, pl.ds(TOP + r0 + 1, CHUNK), :])
            lo_z.append(jnp.where(lane == 0, 0.0, pltpu.roll(v, 1, 1)))
            hi_z.append(jnp.where(lane == NZ - 1, 0.0, pltpu.roll(v, NZ - 1, 1)))
        total = [
            ((lo_x[f] + hi_x[f]) + (lo_y[f] + hi_y[f])) + (lo_z[f] + hi_z[f]) for f in range(FIELDS)
        ]
        w, a, b, c = mid
        gx = hi_x[0] - lo_x[0]
        gy = hi_y[0] - lo_y[0]
        gz = hi_z[0] - lo_z[0]
        diverge = (hi_x[1] - lo_x[1]) + (hi_y[2] - lo_y[2]) + (hi_z[3] - lo_z[3])
        kv = keep[0, plane, pl.ds(r0, CHUNK), :]
        ks = keep[1, plane, pl.ds(r0, CHUNK), :]
        stretch = gz + beta
        new_w = kv * ((total[0] + 0.125 * diverge) + alpha * w)
        new_a = ks * ((total[1] + gx) + a * stretch)
        new_b = ks * ((total[2] + gy) + b * stretch)
        new_c = fine_dt * ((total[3] + 2.0 * (gx * a + gy * b)) + ((stretch + gz) * c + 1.0))
        for f, value in enumerate((new_w, new_a, new_b, new_c)):
            store(f, r0, value)


def fine_kernel(space_size, own, own_flags, near, near_flags, fine_end, packed, even, odd, flags, keep, sems):
    place = lax.axis_index("space")
    gathered = near.shape[0] == space_size

    def in_range(j):
        return (place + (j - REACH) >= 0) & (place + (j - REACH) < space_size)

    def source(j):
        if gathered:
            return jnp.clip(place + (j - REACH), 0, space_size - 1)
        return j

    def copies(j):
        into = even.at[:, pl.ds(j * PLANES, PLANES), pl.ds(TOP, NY), :]
        into_flags = flags.at[pl.ds(j * PLANES, PLANES)]
        if j == REACH:
            return [
                pltpu.make_async_copy(own.at[0], into, sems.at[0, j]),
                pltpu.make_async_copy(own_flags, into_flags, sems.at[1, j]),
            ]
        return [
            pltpu.make_async_copy(near.at[source(j)], into, sems.at[0, j]),
            pltpu.make_async_copy(near_flags.at[source(j)], into_flags, sems.at[1, j]),
        ]

    for j in range(BLOCKS):
        for copy in copies(j):
            copy.start()

    def clear_edges(p, carry):
        for buffer in (even, odd):
            for f in range(FIELDS):
                buffer[f, p, pl.ds(0, TOP), :] = jnp.zeros((TOP, NZ), F32)
                buffer[f, p, pl.ds(TOP + NY, TOP), :] = jnp.zeros((TOP, NZ), F32)
        return carry

    lax.fori_loop(0, WINDOW, clear_edges, 0)
    for j in range(BLOCKS):
        for copy in copies(j):
            copy.wait()
    for j in range(BLOCKS):
        if j == REACH:
            continue

        @pl.when(jnp.logical_not(in_range(j)))
        def _():
            def clear(p, carry):
                for buffer in (even, odd):
                    for f in range(FIELDS):
                        buffer[f, p, pl.ds(TOP, NY), :] = jnp.zeros((NY, NZ), F32)
                return carry

            lax.fori_loop(j * PLANES, (j + 1) * PLANES, clear, 0)

    def prepare(p, carry):
        even[0, p, pl.ds(TOP, NY), :] = even[0, p, pl.ds(TOP, NY), :] * 0.5
        kind = flags[p]
        keep[0, p] = jnp.where(kind != 1, fine_dt, 0.0).astype(F32)
        keep[1, p] = jnp.where(kind != 2, fine_dt, 0.0).astype(F32)
        return carry

    lax.fori_loop(0, WINDOW, prepare, 0)

    first = (REACH - place) * PLANES
    last = (space_size + REACH - place) * PLANES
    for t in range(FINE_STEPS - 1):
        src, dst = (even, odd) if t % 2 == 0 else (odd, even)

        def body(p, carry, src=src, dst=dst):
            def store(f, r0, value):
                dst[f, p, pl.ds(TOP + r0, CHUNK), :] = value

            fine_step(src, keep, p, store)
            return carry

        lax.fori_loop(jnp.maximum(1 + t, first), jnp.minimum(WINDOW - 1 - t, last), body, 0)

    src = even if FINE_STEPS % 2 == 1 else odd
    begin = REACH * PLANES

    def final(p, carry):
        def store(f, r0, value):
            fine_end[f, p - begin, pl.ds(r0, CHUNK), :] = value * 2.0 if f == 0 else value

        fine_step(src, keep, p, store)
        return carry

    lax.fori_loop(begin, begin + PLANES, final, 0)
    pairs = [
        fine_end[f, 2 * x] + fine_end[f, 2 * x + 1] for f in range(FIELDS) for x in range(PLANES // 2)
    ]
    packed[...] = packed_mean(pairs)


def row_shift(v, by):
    rows = v.shape[0]
    row = iota(v.shape, 0)
    rolled = pltpu.roll(v, (-by) % rows, 0)
    return jnp.where((row + by >= 0) & (row + by < rows), rolled, 0.0)


def coarse_neighbours(v):
    row = iota(v.shape, 0)
    lane = iota(v.shape, 1)
    lo_x, hi_x = row_shift(v, -2), row_shift(v, 2)
    up = pltpu.roll(v, NZ - 8, 1)
    hi_y = jnp.where(lane < NZ - 8, up, jnp.where(row % 2 == 0, row_shift(up, 1), 0.0))
    down = pltpu.roll(v, 8, 1)
    lo_y = jnp.where(lane >= 8, down, jnp.where(row % 2 == 1, row_shift(down, -1), 0.0))
    hi_z = jnp.where(lane % 8 == 7, 0.0, pltpu.roll(v, NZ - 1, 1))
    lo_z = jnp.where(lane % 8 == 0, 0.0, pltpu.roll(v, 1, 1))
    return lo_x, hi_x, lo_y, hi_y, lo_z, hi_z


def coarse_step(state):
    near = [coarse_neighbours(v) for v in state]
    w, a, b, c = state

    def lap(f):
        lo_x, hi_x, lo_y, hi_y, lo_z, hi_z = near[f]
        middle = state[f]
        return (
            0.25 * ((lo_x + hi_x) + (lo_y + hi_y)) + (1.0 / 256.0) * (lo_z + hi_z)
        ) - (1.0 + 2.0 / 256.0) * middle

    def grad(f, k):
        return (near[f][2 * k + 1] - near[f][2 * k]) * (1.0 / 32.0 if k == 2 else 0.25)

    gx, gy, gz = grad(0, 0), grad(0, 1), grad(0, 2)
    diverge = grad(1, 0) + grad(2, 1) + grad(3, 2)
    new_w = w + coarse_dt * (lap(0) + 0.5 * diverge)
    new_a = a + coarse_dt * (gx + a * gz - a + lap(1))
    new_b = b + coarse_dt * (gy + b * gz - b + lap(2))
    new_c = c + coarse_dt * (2.0 * (gx * a + gy * b + gz * c) - (c - 1.0) + lap(3))
    return new_w, new_a, new_b, new_c


def coarse_run(state):
    for _ in range(COARSE_STEPS):
        state = coarse_step(state)
    return state


def unpack(packed, grids, count):
    for m in count:
        for s in range(packed.shape[1]):
            for f in range(FIELDS):
                grids[m, f, pl.ds(4 * s, 4), :] = packed[m, s, pl.ds(4 * f, 4), :]


def guess_kernel(packed, guesses, grids):
    slices = packed.shape[0]
    unpack(packed, grids, range(1, slices))
    for m in range(1, slices):
        ended = coarse_run(tuple(grids[m, f] for f in range(FIELDS)))
        for f in range(FIELDS):
            guesses[m, f] = ended[f]


def correct_kernel(packed, guesses, fine_end, out, grids, change):
    slices = packed.shape[0]
    mine = lax.axis_index("tm")
    place = lax.axis_index("space")
    unpack(packed, grids, range(slices - 1))
    state = tuple(grids[0, f] for f in range(FIELDS))
    kept = tuple(jnp.zeros_like(v) for v in state)
    for m in range(1, slices):
        ended = coarse_run(state)
        moved = [ended[f] - guesses[m, f] for f in range(FIELDS)]
        kept = [jnp.where(mine == m, moved[f], kept[f]) for f in range(FIELDS)]
        if m < slices - 1:
            state = tuple(moved[f] + grids[m, f] for f in range(FIELDS))
    for f in range(FIELDS):
        change[f] = kept[f]
    pieces = []
    for f in range(FIELDS):
        for x in range(PLANES // 2):
            for half in range(2):
                line = change[f, pl.ds(4 * place + 2 * x + half, 1), :]
                pieces.append(jnp.broadcast_to(line, (32, NZ)))
    stacked = jnp.concatenate(pieces, axis=0)
    stacked = stacked * pick_rows(stacked.shape)
    spread = (iota((NZ, NZ), 0) % 8 == iota((NZ, NZ), 1) // 16).astype(F32)
    wide = jnp.dot(stacked, spread, precision=HIGHEST, preferred_element_type=F32)
    for f in range(FIELDS):
        for x in range(PLANES // 2):
            k = (f * 2 + x) * NY
            for i in range(2):
                out[0, f, 2 * x + i] = fine_end[f, 2 * x + i] + wide[k : k + NY]


def params():
    return pltpu.CompilerParams(vmem_limit_bytes=LIMIT)


def window(block, axis, size):
    if size <= 8:
        return lax.all_gather(block, axis)
    parts = []
    for j in range(-REACH, REACH + 1):
        if j == 0:
            parts.append(block)
            continue
        route = [(i, i - j) for i in range(size) if 0 <= i - j < size]
        parts.append(lax.ppermute(block, axis, route))
    return jnp.stack(parts)


def local(slices, space_size, starts, flags):
    near = window(starts[0], "space", space_size)
    near_flags = window(flags, "space", space_size)
    packed_shape = jax.ShapeDtypeStruct((FIELDS * 4, NZ), F32)
    begin = pl.pallas_call(
        restrict_kernel, out_shape=packed_shape, in_specs=[VMEM], out_specs=VMEM, compiler_params=params(),
        name="restrict_starts",
    )(starts)
    begin_all = lax.all_gather(begin, ("tm", "space")).reshape(slices, space_size, FIELDS * 4, NZ)

    fine_end, packed = pl.pallas_call(
        functools.partial(fine_kernel, space_size),
        out_shape=(jax.ShapeDtypeStruct((FIELDS, PLANES, NY, NZ), F32), packed_shape),
        in_specs=[ANY] * 4,
        out_specs=(VMEM, VMEM),
        scratch_shapes=[
            pltpu.VMEM((FIELDS, WINDOW, NY + 2 * TOP, NZ), F32),
            pltpu.VMEM((FIELDS, WINDOW, NY + 2 * TOP, NZ), F32),
            pltpu.VMEM((WINDOW, NY, NZ), jnp.int32),
            pltpu.VMEM((2, WINDOW, NY, NZ), F32),
            pltpu.SemaphoreType.DMA((2, BLOCKS)),
        ],
        compiler_params=params(),
        name="fine_steps",
    )(starts, flags, near, near_flags)

    end_all = lax.all_gather(packed, ("tm", "space")).reshape(slices, space_size, FIELDS * 4, NZ)

    grid_shape = (slices, FIELDS, space_size * 4, NZ)
    guesses = pl.pallas_call(
        guess_kernel,
        out_shape=jax.ShapeDtypeStruct(grid_shape, F32),
        in_specs=[VMEM],
        out_specs=VMEM,
        scratch_shapes=[pltpu.VMEM(grid_shape, F32)],
        compiler_params=params(),
        name="guess_old",
    )(begin_all)

    return pl.pallas_call(
        correct_kernel,
        out_shape=jax.ShapeDtypeStruct((1, FIELDS, PLANES, NY, NZ), F32),
        in_specs=[VMEM] * 3,
        out_specs=VMEM,
        scratch_shapes=[pltpu.VMEM(grid_shape, F32), pltpu.VMEM(grid_shape[1:], F32)],
        compiler_params=params(),
        name="correct",
    )(end_all, guesses, fine_end)


def solution(mesh):
    return jax.shard_map(
        functools.partial(local, mesh.shape["tm"], mesh.shape["space"]),
        mesh=mesh,
        in_specs=(P("tm", None, "space", None, None), P("space", None, None)),
        out_specs=P("tm", None, "space", None, None),
        check_vma=False,
    )
```

time: 197 us -> 144 us (0.73)
  the two profiles are of different devices: /device:TPU:11 before, /device:TPU:0 now
where the time goes in v1:
time: 144 us; the launch traced here: 143 us
  blocking collectives  88.8 us (62%)
  waiting for transfers between devices  21.5 us (15%)
  Pallas kernels  15.5 us (11%)
  between operations  13.4 us (9%)
  local copies, waits for them, and re-layouts  4.21 us (3%)
    all_gather x1, blocking collectives, local(): lax.all_gather(packed, ('tm', 'space'))  44.7 us
    all_gather x1, blocking collectives, local(): lax.all_gather(begin, ('tm', 'space'))  44.2 us
    all_gather x2, waiting for transfers between devices, window(): return lax.all_gather(block, axis)  20.1 us
    pallas_call x1, Pallas kernels, local(): pl.pallas_call(functools.partial(fine_kernel, space_size), out_shape=(jax...  12.3 us
    unnamed x8, local copies, waits for them, and re-layouts  4.21 us
  transfers between devices with their start and end apart: 2, of which 1 were waited for; matrix products, arithmetic and copies ran while one was open for 0% of the time, Pallas kernels for 1%

profile of v1, /device:TPU:0, one launch (start us, length us, event | category | flops | bytes accessed | tf_op | source)
XLA Modules:
  0.0 143.5 jit_solution(10758133918228383673)
XLA Ops:
  6.5 0.0 all-gather.8.cloned.1.call-start
  6.5 0.7 all-gather.8.cloned.1.call-update
  7.3 0.0 all-gather.6.cloned.1.call-start
  7.3 0.7 all-gather.6.cloned.1.call-update
  8.0 0.0 copy-start
  8.0 1.0 copy-done
  9.1 0.4 restrict_starts.1
  9.4 44.2 %all-gather.2 = f32[512,128]{1,0:T(8,128)S(1)} all-gather(f32[16,128]{1,0:T(8,128)S(1)} %restrict_starts.1), channel_id=4, replica_groups=mesh['tm'=4,'space'=8] {'tm','space'}, dimensions={0}, use_global_device_ids=true | all-gather | bytes 270336 | tf_op jit(solution)/shard_map/all_gather | solution.py:304
  53.6 0.7 guess_old.1.guesses
  54.3 0.0 all-gather.8.cloned.1.call-done
  54.3 20.1 %all-gather.6.cloned.1.call-done.near = f32[8,4,4,64,128]{4,3,2,1,0:T(8,128)} async-done(((f32[1,4,4,64,128]{4,3,2,1,0:T(8,128)}), f32[8,4,4,64,128]{4,3,2,1,0:T(8,128)}) %all-gather.6.cloned.1.call-update) | async-done | bytes 4194320 | tf_op jit(solution)/shard_map/all_gather | solution.py:285
  74.4 0.0 copy-start.1
  74.4 1.0 copy-done.1
  75.5 0.0 copy-start.2
  75.5 1.2 copy-done.2
  76.7 0.0 copy-start.3
  76.7 0.9 copy-done.3
  77.6 12.3 %fine_steps.1 = (f32[4,4,64,128]{3,2,1,0:T(8,128)S(1)}, f32[16,128]{1,0:T(8,128)S(1)}) custom-call(f32[1,4,4,64,128]{4,3,2,1,0:T(8,128)S(1)} %copy-done.1, s32[4,64,128]{2,1,0:T(8,128)S(1)} %copy-done.3, f32[8,4,4,64,128]{4,3,2,1,0:T(8,128)} %all-gather.6.cloned.1.call-done.near, s32[8,4,64,128]{3,2,1,0:T(8,128)S(1)} %bitcast.5), custom_call_target="tpu_custom_call" | custom-call | tf_op jit(solution)/shard_map/fine_steps/pallas_call | solution.py:306
  89.9 44.7 %all-gather.1 = f32[512,128]{1,0:T(8,128)S(1)} all-gather(f32[16,128]{1,0:T(8,128)S(1)} %get-tuple-element.7), channel_id=3, replica_groups=mesh['tm'=4,'space'=8] {'tm','space'}, dimensions={0}, use_global_device_ids=true | all-gather | bytes 270336 | tf_op jit(solution)/shard_map/all_gather | solution.py:322
  134.5 2.1 %correct.1 = f32[1,4,4,64,128]{4,3,2,1,0:T(8,128)} custom-call(f32[4,8,16,128]{3,2,1,0:T(8,128)S(1)} %bitcast.4, f32[4,4,32,128]{3,2,1,0:T(8,128)S(1)} %guess_old.1.guesses, f32[4,4,64,128]{3,2,1,0:T(8,128)S(1)} %get-tuple-element.8.fine_end), custom_call_target="tpu_custom_call" | custom-call | tf_op jit(solution)/shard_map/correct/pallas_call | solution.py:335
Async XLA Ops:
  6.5 47.8 %all-gather.8.cloned.1.call-start = ((), (), s32[]{:S(2)}) async-start(), calls=%async_computation.1 | async-start | bytes 1179648 | tf_op jit(solution)/shard_map/all_gather | solution.py:285
  7.3 67.2 %all-gather.6.cloned.1.call-start = ((), (), s32[]{:S(2)}) async-start(), calls=%async_computation | async-start | bytes 4718592 | tf_op jit(solution)/shard_map/all_gather | solution.py:285
  8.0 1.0 copy-start
  74.4 1.0 copy-start.1
  75.5 1.2 copy-start.2
  76.7 0.9 copy-start.3
Sparse Core Ops, SparseCore 0:
  9.2 26.6 all-gather.7
  37.9 36.5 all-gather.5

commit v2 on v0

v2 whole, which is shorter than its diff:
```python
import functools

import jax
import jax.numpy as jnp
from jax import lax
from jax.experimental import pallas as pl
from jax.experimental.pallas import tpu as pltpu
from jax.sharding import PartitionSpec as P

FINE_STEPS = 8
COARSE_STEPS = 2

fine_dt = 0.12
coarse_dt = 0.48

FIELDS = 4
PLANES = 4
NY = 64
NZ = 128
ROUND = 4
WINDOW = 3 * PLANES
TILES = NY // 8
PACKED = FIELDS * PLANES
F32 = jnp.float32
HIGHEST = lax.Precision.HIGHEST
VMEM = pl.BlockSpec(memory_space=pltpu.VMEM)
LIMIT = 48 * 2**20


def iota(shape, dim):
    return lax.broadcasted_iota(jnp.int32, shape, dim)


def params():
    return pltpu.CompilerParams(vmem_limit_bytes=LIMIT)


def prepare_kernel(starts, flags, sent):
    for f in range(FIELDS):
        for x in range(PLANES):
            for t in range(TILES):
                v = starts[0, f, x, pl.ds(t, 8, stride=8), :]
                sent[f * PLANES + x, t] = v * 0.5 if f == 0 else v
    for x in range(PLANES):
        for t in range(TILES):
            sent[PACKED + x, t] = flags[x, pl.ds(t, 8, stride=8), :].astype(F32)


def fine_plane(src, keep, p, store):
    beta = 1.0 / fine_dt - 7.0
    alpha = 1.0 / fine_dt - 6.0
    lane = iota((8, NZ), 1)
    low_lane, high_lane = lane == 0, lane == NZ - 1
    fields = range(FIELDS)
    lo_y = [src[f, p, 0] for f in fields]
    mid = [src[f, p, 1] for f in fields]
    for t in range(TILES):
        hi_y = [src[f, p, t + 2] for f in fields]
        lo_x = [src[f, p - 1, t + 1] for f in fields]
        hi_x = [src[f, p + 1, t + 1] for f in fields]
        lo_z = [jnp.where(low_lane, 0.0, pltpu.roll(v, 1, 1)) for v in mid]
        hi_z = [jnp.where(high_lane, 0.0, pltpu.roll(v, NZ - 1, 1)) for v in mid]
        total = [((lo_x[f] + hi_x[f]) + (lo_y[f] + hi_y[f])) + (lo_z[f] + hi_z[f]) for f in fields]
        w, a, b, c = mid
        gx = hi_x[0] - lo_x[0]
        gy = hi_y[0] - lo_y[0]
        gz = hi_z[0] - lo_z[0]
        diverge = (hi_x[1] - lo_x[1]) + (hi_y[2] - lo_y[2]) + (hi_z[3] - lo_z[3])
        kv = keep[0, p, t]
        ks = keep[1, p, t]
        stretch = gz + beta
        new_w = kv * ((total[0] + 0.125 * diverge) + alpha * w)
        new_a = ks * ((total[1] + gx) + a * stretch)
        new_b = ks * ((total[2] + gy) + b * stretch)
        new_c = fine_dt * ((total[3] + 2.0 * (gx * a + gy * b)) + ((stretch + gz) * c + 1.0))
        for f, value in enumerate((new_w, new_a, new_b, new_c)):
            store(f, t, value)
        lo_y, mid = mid, hi_y


def put_tile(buffer, f, p, t, value):
    buffer[f, p, t + 1] = value
    row = iota((8, NZ), 0)
    if t == 0:
        buffer[f, p, TILES + 1] = jnp.where(row == 7, 0.0, pltpu.roll(value, 7, 0))
    if t == TILES - 1:
        buffer[f, p, 0] = jnp.where(row == 0, 0.0, pltpu.roll(value, 1, 0))


def fine_round(space_size, place, parts, kinds, even, odd, keep, finish):
    for j, part in enumerate(parts):

        def load(x, carry, j=j, part=part):
            for f in range(FIELDS):
                for t in range(TILES):
                    put_tile(even, f, j * PLANES + x, t, part[f * PLANES + x, t])
            return carry

        lax.fori_loop(0, PLANES, load, 0)

        def convert(x, carry, j=j, kind=kinds[j]):
            v = kind[PACKED + x]
            keep[0, j * PLANES + x] = jnp.where(v != 1.0, fine_dt, 0.0).astype(F32)
            keep[1, j * PLANES + x] = jnp.where(v != 2.0, fine_dt, 0.0).astype(F32)
            return carry

        lax.fori_loop(0, PLANES, convert, 0)

    for edge, outside in ((PLANES - 1, place == 0), (2 * PLANES, place == space_size - 1)):

        @pl.when(outside)
        def _(edge=edge):
            for f in range(FIELDS):
                odd[f, edge] = jnp.zeros((TILES + 2, 8, NZ), F32)

    first = jnp.where(place == 0, PLANES, 0)
    last = jnp.where(place == space_size - 1, 2 * PLANES, WINDOW)
    for step in range(ROUND - 1):
        src, dst = (even, odd) if step % 2 == 0 else (odd, even)

        def body(p, carry, src=src, dst=dst):
            fine_plane(src, keep, p, lambda f, t, value: put_tile(dst, f, p, t, value))
            return carry

        lax.fori_loop(jnp.maximum(1 + step, first), jnp.minimum(WINDOW - 1 - step, last), body, 0)

    src = even if ROUND % 2 == 1 else odd

    def final(p, carry):
        fine_plane(src, keep, p, lambda f, t, value: finish(f, p - PLANES, t, value))
        return carry

    lax.fori_loop(PLANES, 2 * PLANES, final, 0)


def first_kernel(space_size, left, own, right, sent, even, odd, keep):
    parts = (left, own, right)

    def finish(f, x, t, value):
        sent[f * PLANES + x, t] = value

    fine_round(space_size, lax.axis_index("space"), parts, parts, even, odd, keep, finish)


def coarse_rows(pair_of, count):
    pairs = count // 2
    pieces = []
    for k in range(pairs):
        v = pair_of(k)
        for i in range(TILES // 2):
            pieces.append(v[2 * i] + v[2 * i + 1])
    stacked = jnp.concatenate(pieces, axis=0)
    gather = (iota((NZ, NZ), 0) // 16 == iota((NZ, NZ), 1) % 8).astype(F32)
    sums = jnp.dot(stacked, gather, precision=HIGHEST, preferred_element_type=F32)
    sums = sums * pick_rows(sums.shape)
    sums = sums.reshape(pairs, TILES // 2, 8, NZ)
    sums = (sums[:, 0] + sums[:, 1]) + (sums[:, 2] + sums[:, 3])
    return sums.reshape(pairs * 8, NZ)


def pick_rows(shape):
    row = iota(shape, 0)
    return (row % 8 % 4 * 4 + row // 8 % 4 == iota(shape, 1) // 8).astype(F32)


def halves(sums, rows):
    shape = (rows, sums.shape[0])
    add = (iota(shape, 0) == iota(shape, 1) // 4).astype(F32) * (1.0 / 64.0)
    return jnp.dot(add, sums, precision=HIGHEST, preferred_element_type=F32)


def row_shift(v, by):
    rows = v.shape[0]
    row = iota(v.shape, 0)
    rolled = pltpu.roll(v, (-by) % rows, 0)
    return jnp.where((row + by >= 0) & (row + by < rows), rolled, 0.0)


def coarse_neighbours(v):
    row = iota(v.shape, 0)
    lane = iota(v.shape, 1)
    lo_x, hi_x = row_shift(v, -2), row_shift(v, 2)
    up = pltpu.roll(v, NZ - 8, 1)
    hi_y = jnp.where(lane < NZ - 8, up, jnp.where(row % 2 == 0, row_shift(up, 1), 0.0))
    down = pltpu.roll(v, 8, 1)
    lo_y = jnp.where(lane >= 8, down, jnp.where(row % 2 == 1, row_shift(down, -1), 0.0))
    hi_z = jnp.where(lane % 8 == 7, 0.0, pltpu.roll(v, NZ - 1, 1))
    lo_z = jnp.where(lane % 8 == 0, 0.0, pltpu.roll(v, 1, 1))
    return lo_x, hi_x, lo_y, hi_y, lo_z, hi_z


def coarse_step(state):
    near = [coarse_neighbours(v) for v in state]
    w, a, b, c = state

    def lap(f):
        lo_x, hi_x, lo_y, hi_y, lo_z, hi_z = near[f]
        return (0.25 * ((lo_x + hi_x) + (lo_y + hi_y)) + (1.0 / 256.0) * (lo_z + hi_z)) - (1.0 + 2.0 / 256.0) * state[f]

    def grad(f, k):
        return (near[f][2 * k + 1] - near[f][2 * k]) * (1.0 / 32.0 if k == 2 else 0.25)

    gx, gy, gz = grad(0, 0), grad(0, 1), grad(0, 2)
    diverge = grad(1, 0) + grad(2, 1) + grad(3, 2)
    new_w = w + coarse_dt * (lap(0) + 0.5 * diverge)
    new_a = a + coarse_dt * (gx + a * gz - a + lap(1))
    new_b = b + coarse_dt * (gy + b * gz - b + lap(2))
    new_c = c + coarse_dt * (2.0 * (gx * a + gy * b + gz * c) - (c - 1.0) + lap(3))
    return new_w, new_a, new_b, new_c


def guess_kernel(space_size, left, own, right, guess):
    place = lax.axis_index("space")
    parts = (left, own, right)
    rows = 16
    row = iota((rows, NZ), 0)
    plane = 2 * place - 2 + row // 2
    inside = (row < WINDOW) & (plane >= 0) & (plane < 2 * space_size)
    state = []
    for f in range(FIELDS):

        def pair_of(k, f=f):
            part = parts[k // 2]
            x = f * PLANES + k % 2 * 2
            return part[x] + part[x + 1]

        grid = halves(coarse_rows(pair_of, WINDOW), rows)
        state.append(grid * 2.0 if f == 0 else grid)
    for _ in range(COARSE_STEPS):
        state = [jnp.where(inside, v, 0.0) for v in coarse_step(state)]
    for f in range(FIELDS):
        guess[pl.ds(4 * f, 4), :] = state[f][4:8]


def second_kernel(space_size, left, own, right, left_kind, own_kind, right_kind, guess, fine_end, jump, even, odd, keep):
    kinds = (left_kind, own_kind, right_kind)

    def finish(f, x, t, value):
        fine_end[f * PLANES + x, t] = value * 2.0 if f == 0 else value

    fine_round(space_size, lax.axis_index("space"), (left, own, right), kinds, even, odd, keep, finish)
    ended = halves(coarse_rows(lambda k: fine_end[2 * k] + fine_end[2 * k + 1], PACKED), PACKED)
    jumped = ended - jnp.where(lax.axis_index("tm") == 0, 0.0, guess[...])
    for k in range(jump.shape[0]):
        jump[k] = jumped


def correct_kernel(jumps, guess, fine_end, out, grids, change):
    slices, spaces = jumps.shape[:2]
    mine = lax.axis_index("tm")
    place = lax.axis_index("space")
    for m in range(slices - 1):
        for s in range(spaces):
            for f in range(FIELDS):
                grids[m, f, pl.ds(4 * s, 4), :] = jumps[m, s, pl.ds(4 * f, 4), :]
    state = [grids[0, f] for f in range(FIELDS)]
    kept = state
    for m in range(1, slices):
        ended = state
        for _ in range(COARSE_STEPS):
            ended = coarse_step(ended)
        kept = [jnp.where(mine == m, ended[f], kept[f]) for f in range(FIELDS)]
        if m < slices - 1:
            state = [ended[f] + grids[m, f] for f in range(FIELDS)]
    for f in range(FIELDS):
        change[f] = kept[f]
    row = iota((8, NZ), 0)
    pieces = []
    for f in range(FIELDS):
        for x in range(PLANES // 2):
            k = 2 * x
            lines = [
                change[f, pl.ds(4 * place + k + half, 1), :] - guess[pl.ds(4 * f + k + half, 1), :] for half in range(2)
            ]
            tile = jnp.where(row < 4, lines[0], lines[1])
            tile = jnp.where(mine == 0, 0.0, tile)
            pieces += [tile] * (TILES // 2)
    stacked = jnp.concatenate(pieces, axis=0)
    stacked = stacked * pick_rows(stacked.shape)
    spread = (iota((NZ, NZ), 0) % 8 == iota((NZ, NZ), 1) // 16).astype(F32)
    wide = jnp.dot(stacked, spread, precision=HIGHEST, preferred_element_type=F32)
    for f in range(FIELDS):
        for x in range(PLANES):
            for t in range(TILES):
                k = ((f * 2 + x // 2) * (TILES // 2) + t // 2) * 8
                out[0, f, x, pl.ds(t, 8, stride=8), :] = fine_end[f * PLANES + x, t] + wide[k : k + 8]


def neighbours(block, size):
    upward = [(i, i + 1) for i in range(size - 1)]
    downward = [(target, source) for source, target in upward]
    return lax.ppermute(block, "space", upward), lax.ppermute(block, "space", downward)


def shaped(*shape):
    return jax.ShapeDtypeStruct(shape, F32)


def local(slices, space_size, starts, flags):
    fine_scratch = [
        pltpu.VMEM((FIELDS, WINDOW, TILES + 2, 8, NZ), F32),
        pltpu.VMEM((FIELDS, WINDOW, TILES + 2, 8, NZ), F32),
        pltpu.VMEM((2, WINDOW, TILES, 8, NZ), F32),
    ]
    opening = pl.pallas_call(
        prepare_kernel,
        out_shape=shaped(PACKED + PLANES, TILES, 8, NZ),
        in_specs=[VMEM] * 2,
        out_specs=VMEM,
        compiler_params=params(),
        name="prepare",
    )(starts, flags)
    left, right = neighbours(opening, space_size)
    middle = pl.pallas_call(
        functools.partial(first_kernel, space_size),
        out_shape=shaped(PACKED, TILES, 8, NZ),
        in_specs=[VMEM] * 3,
        out_specs=VMEM,
        scratch_shapes=fine_scratch,
        compiler_params=params(),
        name="first_round",
    )(left, opening, right)
    middle_left, middle_right = neighbours(middle, space_size)
    guess = pl.pallas_call(
        functools.partial(guess_kernel, space_size),
        out_shape=shaped(PACKED, NZ),
        in_specs=[VMEM] * 3,
        out_specs=VMEM,
        compiler_params=params(),
        name="guess_old",
    )(left, opening, right)
    fine_end, jump = pl.pallas_call(
        functools.partial(second_kernel, space_size),
        out_shape=(shaped(PACKED, TILES, 8, NZ), shaped(slices * space_size, PACKED, NZ)),
        in_specs=[VMEM] * 7,
        out_specs=(VMEM, VMEM),
        scratch_shapes=fine_scratch,
        compiler_params=params(),
        name="second_round",
    )(middle_left, middle, middle_right, left, opening, right, guess)
    jumps = lax.all_to_all(jump, ("tm", "space"), 0, 0)
    jumps = jumps.reshape(slices, space_size, PACKED, NZ)
    return pl.pallas_call(
        correct_kernel,
        out_shape=shaped(1, FIELDS, PLANES, NY, NZ),
        in_specs=[VMEM] * 3,
        out_specs=VMEM,
        scratch_shapes=[
            pltpu.VMEM((slices, FIELDS, space_size * 4, NZ), F32),
            pltpu.VMEM((FIELDS, space_size * 4, NZ), F32),
        ],
        compiler_params=params(),
        name="correct",
    )(jumps, guess, fine_end)


def solution(mesh):
    return jax.shard_map(
        functools.partial(local, mesh.shape["tm"], mesh.shape["space"]),
        mesh=mesh,
        in_specs=(P("tm", None, "space", None, None), P("space", None, None)),
        out_specs=P("tm", None, "space", None, None),
        check_vma=False,
    )
```

time: 197 us -> 65.6 us (0.33)
  the two profiles are of different devices: /device:TPU:11 before, /device:TPU:0 now
where the time goes in v2:
time: 65.6 us; the launch traced here: 65.4 us
  blocking collectives  30.9 us (47%)
  starting transfers between devices  19.6 us (30%)
  Pallas kernels  11.2 us (17%)
  local copies, waits for them, and re-layouts  1.94 us (3%)
  waiting for transfers between devices  1.7 us (3%)
    all_to_all x1, blocking collectives, local(): jumps = lax.all_to_all(jump, ('tm', 'space'), 0, 0)  30.9 us
    ppermute x2, starting transfers between devices, neighbours(): lax.ppermute(block, 'space', upward)  17 us
    pallas_call x1, Pallas kernels, local(): pl.pallas_call(functools.partial(second_kernel, space_size), out_shape=(s...  4.05 us
    pallas_call x1, Pallas kernels, local(): pl.pallas_call(functools.partial(first_kernel, space_size), out_shape=sha...  3.6 us
    ppermute x2, starting transfers between devices, neighbours(): lax.ppermute(block, 'space', downward)  2.58 us
    pallas_call x1, Pallas kernels, local(): pl.pallas_call(correct_kernel, out_shape=shaped(1, FIELDS, PLANES, NY, NZ...  1.98 us
    unnamed x4, local copies, waits for them, and re-layouts  1.94 us
    ppermute x2, waiting for transfers between devices, neighbours(): lax.ppermute(block, 'space', upward)  1.69 us
  transfers between devices with their start and end apart: 4, of which 1 were waited for; matrix products, arithmetic and copies ran while one was open for 0% of the time, Pallas kernels for 2%

profile of v2, /device:TPU:0, one launch (start us, length us, event | category | flops | bytes accessed | tf_op | source)
XLA Modules:
  0.0 65.4 jit_solution(1295156139363260693)
XLA Ops:
  0.0 0.0 copy-start
  0.0 1.0 %copy-done = f32[1,4,4,64,128]{4,3,2,1,0:T(8,128)S(1)} copy-done((f32[1,4,4,64,128]{4,3,2,1,0:T(8,128)S(1)}, f32[1,4,4,64,128]{4,3,2,1,0:T(8,128)}, u32[]{:S(2)}) %copy-start) | copy-done | bytes 524312
  1.0 0.0 copy-start.1
  1.0 0.9 %copy-done.1 = s32[4,64,128]{2,1,0:T(8,128)S(1)} copy-done((s32[4,64,128]{2,1,0:T(8,128)S(1)}, s32[4,64,128]{2,1,0:T(8,128)}, u32[]{:S(2)}) %copy-start.1) | copy-done | bytes 131096
  1.9 0.1 prepare.1.own.own_kind
  2.1 1.3 %collective-permute-start.1 = (f32[20,8,8,128]{3,2,1,0:T(8,128)S(1)}, f32[20,8,8,128]{3,2,1,0:T(8,128)S(1)}, u32[]{:S(2)}, u32[]{:S(2)}) collective-permute-start(f32[20,8,8,128]{3,2,1,0:T(8,128)S(1)} %prepare.1.own.own_kind), channel_id=1, source_target_pairs={{1,0},{2,1},{3,2},{4,3},{5,4},{6,5},{7,6},{9,8},{10,9},{11,10},{12... | collective-permute-start | bytes 1966088 | tf_op jit(solution)/shard_map/ppermute | solution.py:292
  3.4 3.1 %collective-permute-start = (f32[20,8,8,128]{3,2,1,0:T(8,128)S(1)}, f32[20,8,8,128]{3,2,1,0:T(8,128)S(1)}, u32[]{:S(2)}, u32[]{:S(2)}) collective-permute-start(f32[20,8,8,128]{3,2,1,0:T(8,128)S(1)} %prepare.1.own.own_kind), channel_id=1, source_target_pairs={{0,1},{1,2},{2,3},{3,4},{4,5},{5,6},{6,7},{8,9},{9,10},{10,11},{11... | collective-permute-start | bytes 1966088 | tf_op jit(solution)/shard_map/ppermute | solution.py:292
  6.5 0.0 collective-permute-done.1.right.right_kind
  6.5 1.7 %collective-permute-done.left.left_kind = f32[20,8,8,128]{3,2,1,0:T(8,128)S(1)} collective-permute-done((f32[20,8,8,128]{3,2,1,0:T(8,128)S(1)}, f32[20,8,8,128]{3,2,1,0:T(8,128)S(1)}, u32[]{:S(2)}, u32[]{:S(2)}) %collective-permute-start) | collective-permute-done | bytes 655392 | tf_op jit(solution)/shard_map/ppermute | solution.py:292
  8.1 3.6 %first_round.1.own = f32[16,8,8,128]{3,2,1,0:T(8,128)S(1)} custom-call(f32[20,8,8,128]{3,2,1,0:T(8,128)S(1)} %collective-permute-done.left.left_kind, f32[20,8,8,128]{3,2,1,0:T(8,128)S(1)} %prepare.1.own.own_kind, f32[20,8,8,128]{3,2,1,0:T(8,128)S(1)} %collective-permute-done.1.right.right_kind), custom_call_target="tpu_custom_call" | custom-call | tf_op jit(solution)/shard_map/first_round/pallas_call | solution.py:314
  11.7 1.3 %collective-permute-start.3 = (f32[16,8,8,128]{3,2,1,0:T(8,128)S(1)}, f32[16,8,8,128]{3,2,1,0:T(8,128)S(1)}, u32[]{:S(2)}, u32[]{:S(2)}) collective-permute-start(f32[16,8,8,128]{3,2,1,0:T(8,128)S(1)} %first_round.1.own), channel_id=1, source_target_pairs={{1,0},{2,1},{3,2},{4,3},{5,4},{6,5},{7,6},{9,8},{10,9},{11,10},{12... | collective-permute-start | bytes 1572872 | tf_op jit(solution)/shard_map/ppermute | solution.py:292
  13.0 13.9 %collective-permute-start.2 = (f32[16,8,8,128]{3,2,1,0:T(8,128)S(1)}, f32[16,8,8,128]{3,2,1,0:T(8,128)S(1)}, u32[]{:S(2)}, u32[]{:S(2)}) collective-permute-start(f32[16,8,8,128]{3,2,1,0:T(8,128)S(1)} %first_round.1.own), channel_id=1, source_target_pairs={{0,1},{1,2},{2,3},{3,4},{4,5},{5,6},{6,7},{8,9},{9,10},{10,11},{11... | collective-permute-start | bytes 1572872 | tf_op jit(solution)/shard_map/ppermute | solution.py:292
  27.0 1.4 %guess_old.1.guess = f32[16,128]{1,0:T(8,128)S(1)} custom-call(f32[20,8,8,128]{3,2,1,0:T(8,128)S(1)} %collective-permute-done.left.left_kind, f32[20,8,8,128]{3,2,1,0:T(8,128)S(1)} %prepare.1.own.own_kind, f32[20,8,8,128]{3,2,1,0:T(8,128)S(1)} %collective-permute-done.1.right.right_kind), custom_call_target="tpu_custom_call" | custom-call | tf_op jit(solution)/shard_map/guess_old/pallas_call | solution.py:324
  28.4 0.0 collective-permute-done.3.right
  28.4 0.0 collective-permute-done.2.left
  28.4 4.1 %second_round.1 = (f32[16,8,8,128]{3,2,1,0:T(8,128)S(1)}, f32[32,16,128]{2,1,0:T(8,128)S(1)}) custom-call(f32[16,8,8,128]{3,2,1,0:T(8,128)S(1)} %collective-permute-done.2.left, f32[16,8,8,128]{3,2,1,0:T(8,128)S(1)} %first_round.1.own, f32[16,8,8,128]{3,2,1,0:T(8,128)S(1)} %collective-permute-done.3.right, ...), custom_call_target="tpu_custom_call" | custom-call | tf_op jit(solution)/shard_map/second_round/pallas_call | solution.py:332
  32.5 30.9 %all_to_all.5 = f32[32,16,128]{2,1,0:T(8,128)S(1)} all-to-all(f32[32,16,128]{2,1,0:T(8,128)S(1)} %get-tuple-element.7), channel_id=1, replica_groups=mesh['tm'=4,'space'=8] {'tm','space'}, dimensions={0} | all-to-all | bytes 524288 | tf_op jit(solution)/shard_map/all_to_all | solution.py:341
  63.4 2.0 %correct.1 = f32[1,4,4,64,128]{4,3,2,1,0:T(8,128)} custom-call(f32[4,8,16,128]{3,2,1,0:T(8,128)S(1)} %bitcast.1, f32[16,128]{1,0:T(8,128)S(1)} %guess_old.1.guess, f32[16,8,8,128]{3,2,1,0:T(8,128)S(1)} %get-tuple-element.8.fine_end), custom_call_target="tpu_custom_call" | custom-call | tf_op jit(solution)/shard_map/correct/pallas_call | solution.py:343
Async XLA Ops:
  0.0 1.0 %copy-start = (f32[1,4,4,64,128]{4,3,2,1,0:T(8,128)S(1)}, f32[1,4,4,64,128]{4,3,2,1,0:T(8,128)}, u32[]{:S(2)}) copy-start(f32[1,4,4,64,128]{4,3,2,1,0:T(8,128)} %starts.1) | copy-start | bytes 1572868
  1.0 0.9 %copy-start.1 = (s32[4,64,128]{2,1,0:T(8,128)S(1)}, s32[4,64,128]{2,1,0:T(8,128)}, u32[]{:S(2)}) copy-start(s32[4,64,128]{2,1,0:T(8,128)} %flags.1) | copy-start | bytes 393220
  2.1 4.4 %collective-permute-start.1 = (f32[20,8,8,128]{3,2,1,0:T(8,128)S(1)}, f32[20,8,8,128]{3,2,1,0:T(8,128)S(1)}, u32[]{:S(2)}, u32[]{:S(2)}) collective-permute-start(f32[20,8,8,128]{3,2,1,0:T(8,128)S(1)} %prepare.1.own.own_kind), channel_id=1, source_target_pairs={{1,0},{2,1},{3,2},{4,3},{5,4},{6,5},{7,6},{9,8},{10,9},{11,10},{12... | collective-permute-start | bytes 1966088 | tf_op jit(solution)/shard_map/ppermute | solution.py:292
  3.4 4.7 %collective-permute-start = (f32[20,8,8,128]{3,2,1,0:T(8,128)S(1)}, f32[20,8,8,128]{3,2,1,0:T(8,128)S(1)}, u32[]{:S(2)}, u32[]{:S(2)}) collective-permute-start(f32[20,8,8,128]{3,2,1,0:T(8,128)S(1)} %prepare.1.own.own_kind), channel_id=1, source_target_pairs={{0,1},{1,2},{2,3},{3,4},{4,5},{5,6},{6,7},{8,9},{9,10},{10,11},{11... | collective-permute-start | bytes 1966088 | tf_op jit(solution)/shard_map/ppermute | solution.py:292
  11.7 16.7 %collective-permute-start.3 = (f32[16,8,8,128]{3,2,1,0:T(8,128)S(1)}, f32[16,8,8,128]{3,2,1,0:T(8,128)S(1)}, u32[]{:S(2)}, u32[]{:S(2)}) collective-permute-start(f32[16,8,8,128]{3,2,1,0:T(8,128)S(1)} %first_round.1.own), channel_id=1, source_target_pairs={{1,0},{2,1},{3,2},{4,3},{5,4},{6,5},{7,6},{9,8},{10,9},{11,10},{12... | collective-permute-start | bytes 1572872 | tf_op jit(solution)/shard_map/ppermute | solution.py:292
  13.0 15.4 %collective-permute-start.2 = (f32[16,8,8,128]{3,2,1,0:T(8,128)S(1)}, f32[16,8,8,128]{3,2,1,0:T(8,128)S(1)}, u32[]{:S(2)}, u32[]{:S(2)}) collective-permute-start(f32[16,8,8,128]{3,2,1,0:T(8,128)S(1)} %first_round.1.own), channel_id=1, source_target_pairs={{0,1},{1,2},{2,3},{3,4},{4,5},{5,6},{6,7},{8,9},{9,10},{10,11},{11... | collective-permute-start | bytes 1572872 | tf_op jit(solution)/shard_map/ppermute | solution.py:292

commit v3 on v2

--- a/solution.py
+++ b/solution.py
@@ -20,6 +20,7 @@
 ROUND = 4
 WINDOW = 3 * PLANES
 TILES = NY // 8
+GROUP = 4
 PACKED = FIELDS * PLANES
 F32 = jnp.float32
 HIGHEST = lax.Precision.HIGHEST
@@ -46,36 +47,42 @@
             sent[PACKED + x, t] = flags[x, pl.ds(t, 8, stride=8), :].astype(F32)
 
 
-def fine_plane(src, keep, p, store):
+def fine_tile(mid, lo_x, hi_x, lo_y, hi_y, kv, ks, low_lane, high_lane):
     beta = 1.0 / fine_dt - 7.0
     alpha = 1.0 / fine_dt - 6.0
+    lo_z = [jnp.where(low_lane, 0.0, pltpu.roll(v, 1, 1)) for v in mid]
+    hi_z = [jnp.where(high_lane, 0.0, pltpu.roll(v, NZ - 1, 1)) for v in mid]
+    total = [((lo_x[f] + hi_x[f]) + (lo_y[f] + hi_y[f])) + (lo_z[f] + hi_z[f]) for f in range(FIELDS)]
+    w, a, b, c = mid
+    gx = hi_x[0] - lo_x[0]
+    gy = hi_y[0] - lo_y[0]
+    gz = hi_z[0] - lo_z[0]
+    diverge = (hi_x[1] - lo_x[1]) + (hi_y[2] - lo_y[2]) + (hi_z[3] - lo_z[3])
+    stretch = gz + beta
+    new_w = kv * ((total[0] + 0.125 * diverge) + alpha * w)
+    new_a = ks * ((total[1] + gx) + a * stretch)
+    new_b = ks * ((total[2] + gy) + b * stretch)
+    new_c = fine_dt * ((total[3] + 2.0 * (gx * a + gy * b)) + ((stretch + gz) * c + 1.0))
+    return new_w, new_a, new_b, new_c
+
+
+def fine_plane(src, keep, p, store):
     lane = iota((8, NZ), 1)
     low_lane, high_lane = lane == 0, lane == NZ - 1
     fields = range(FIELDS)
-    lo_y = [src[f, p, 0] for f in fields]
-    mid = [src[f, p, 1] for f in fields]
-    for t in range(TILES):
-        hi_y = [src[f, p, t + 2] for f in fields]
-        lo_x = [src[f, p - 1, t + 1] for f in fields]
-        hi_x = [src[f, p + 1, t + 1] for f in fields]
-        lo_z = [jnp.where(low_lane, 0.0, pltpu.roll(v, 1, 1)) for v in mid]
-        hi_z = [jnp.where(high_lane, 0.0, pltpu.roll(v, NZ - 1, 1)) for v in mid]
-        total = [((lo_x[f] + hi_x[f]) + (lo_y[f] + hi_y[f])) + (lo_z[f] + hi_z[f]) for f in fields]
-        w, a, b, c = mid
-        gx = hi_x[0] - lo_x[0]
-        gy = hi_y[0] - lo_y[0]
-        gz = hi_z[0] - lo_z[0]
-        diverge = (hi_x[1] - lo_x[1]) + (hi_y[2] - lo_y[2]) + (hi_z[3] - lo_z[3])
-        kv = keep[0, p, t]
-        ks = keep[1, p, t]
-        stretch = gz + beta
-        new_w = kv * ((total[0] + 0.125 * diverge) + alpha * w)
-        new_a = ks * ((total[1] + gx) + a * stretch)
-        new_b = ks * ((total[2] + gy) + b * stretch)
-        new_c = fine_dt * ((total[3] + 2.0 * (gx * a + gy * b)) + ((stretch + gz) * c + 1.0))
-        for f, value in enumerate((new_w, new_a, new_b, new_c)):
-            store(f, t, value)
-        lo_y, mid = mid, hi_y
+    for begin in range(0, TILES, GROUP):
+        tiles = range(begin, begin + GROUP)
+        column = [[src[f, p, t] for f in fields] for t in range(begin, begin + GROUP + 2)]
+        lo_x = [[src[f, p - 1, t + 1] for f in fields] for t in tiles]
+        hi_x = [[src[f, p + 1, t + 1] for f in fields] for t in tiles]
+        kept = [(keep[0, p, t], keep[1, p, t]) for t in tiles]
+        fresh = [
+            fine_tile(column[i + 1], lo_x[i], hi_x[i], column[i], column[i + 2], *kept[i], low_lane, high_lane)
+            for i in range(GROUP)
+        ]
+        for i, t in enumerate(tiles):
+            for f in fields:
+                store(f, t, fresh[i][f])
 
 
 def put_tile(buffer, f, p, t, value):
@@ -245,14 +252,19 @@
         jump[k] = jumped
 
 
+def repeat_kernel(jumps, repeated):
+    for k in range(repeated.shape[0]):
+        repeated[k] = jumps[pl.ds(0, repeated.shape[1])]
+
+
 def correct_kernel(jumps, guess, fine_end, out, grids, change):
-    slices, spaces = jumps.shape[:2]
+    spaces, slices = jumps.shape[0], jumps.shape[1] + 1
     mine = lax.axis_index("tm")
     place = lax.axis_index("space")
     for m in range(slices - 1):
         for s in range(spaces):
             for f in range(FIELDS):
-                grids[m, f, pl.ds(4 * s, 4), :] = jumps[m, s, pl.ds(4 * f, 4), :]
+                grids[m, f, pl.ds(4 * s, 4), :] = jumps[s, m, pl.ds(4 * f, 4), :]
     state = [grids[0, f] for f in range(FIELDS)]
     kept = state
     for m in range(1, slices):
@@ -331,15 +343,23 @@
     )(left, opening, right)
     fine_end, jump = pl.pallas_call(
         functools.partial(second_kernel, space_size),
-        out_shape=(shaped(PACKED, TILES, 8, NZ), shaped(slices * space_size, PACKED, NZ)),
+        out_shape=(shaped(PACKED, TILES, 8, NZ), shaped(slices, PACKED, NZ)),
         in_specs=[VMEM] * 7,
         out_specs=(VMEM, VMEM),
         scratch_shapes=fine_scratch,
         compiler_params=params(),
         name="second_round",
     )(middle_left, middle, middle_right, left, opening, right, guess)
-    jumps = lax.all_to_all(jump, ("tm", "space"), 0, 0)
-    jumps = jumps.reshape(slices, space_size, PACKED, NZ)
+    earlier = lax.all_to_all(jump, "tm", 0, 0)
+    earlier = pl.pallas_call(
+        repeat_kernel,
+        out_shape=shaped(space_size, slices - 1, PACKED, NZ),
+        in_specs=[VMEM],
+        out_specs=VMEM,
+        compiler_params=params(),
+        name="repeat",
+    )(earlier)
+    jumps = lax.all_to_all(earlier, "space", 0, 0)
     return pl.pallas_call(
         correct_kernel,
         out_shape=shaped(1, FIELDS, PLANES, NY, NZ),

time: 65.6 us -> 69.4 us (1.058)
  blocking collectives: 30.9 us -> 34.7 us
    all_to_all x1 -> x2, blocking collectives: 30.9 us -> 34.7 us  [the longest x1 24.4 us: local(): jumps = lax.all_to_all(earlier, 'space', 0, 0)]
where the time goes in v3:
time: 69.4 us; the launch traced here: 69.1 us
  blocking collectives  34.7 us (50%)
  starting transfers between devices  19.6 us (28%)
  Pallas kernels  11.1 us (16%)
  local copies, waits for them, and re-layouts  1.94 us (3%)
  waiting for transfers between devices  1.7 us (2%)
    all_to_all x1, blocking collectives, local(): jumps = lax.all_to_all(earlier, 'space', 0, 0)  24.4 us
    ppermute x2, starting transfers between devices, neighbours(): lax.ppermute(block, 'space', upward)  17 us
    all_to_all x1, blocking collectives, local(): earlier = lax.all_to_all(jump, 'tm', 0, 0)  10.3 us
    pallas_call x1, Pallas kernels, local(): pl.pallas_call(functools.partial(second_kernel, space_size), out_shape=(s...  4.01 us
    pallas_call x1, Pallas kernels, local(): pl.pallas_call(functools.partial(first_kernel, space_size), out_shape=sha...  3.58 us
    ppermute x2, starting transfers between devices, neighbours(): lax.ppermute(block, 'space', downward)  2.58 us
    pallas_call x1, Pallas kernels, local(): pl.pallas_call(correct_kernel, out_shape=shaped(1, FIELDS, PLANES, NY, NZ...  1.98 us
    unnamed x4, local copies, waits for them, and re-layouts  1.94 us
  transfers between devices with their start and end apart: 4, of which 1 were waited for; matrix products, arithmetic and copies ran while one was open for 0% of the time, Pallas kernels for 2%

profile of v3, /device:TPU:0, one launch (start us, length us, event | category | flops | bytes accessed | tf_op | source)
XLA Modules:
  0.0 69.1 jit_solution(9731053253834873647)
XLA Ops:
  0.0 0.0 copy-start
  0.0 1.0 %copy-done = f32[1,4,4,64,128]{4,3,2,1,0:T(8,128)S(1)} copy-done((f32[1,4,4,64,128]{4,3,2,1,0:T(8,128)S(1)}, f32[1,4,4,64,128]{4,3,2,1,0:T(8,128)}, u32[]{:S(2)}) %copy-start) | copy-done | bytes 524312
  1.0 0.0 copy-start.1
  1.0 0.9 %copy-done.1 = s32[4,64,128]{2,1,0:T(8,128)S(1)} copy-done((s32[4,64,128]{2,1,0:T(8,128)S(1)}, s32[4,64,128]{2,1,0:T(8,128)}, u32[]{:S(2)}) %copy-start.1) | copy-done | bytes 131096
  1.9 0.1 prepare.1.own.own_kind
  2.1 1.3 %collective-permute-start.1 = (f32[20,8,8,128]{3,2,1,0:T(8,128)S(1)}, f32[20,8,8,128]{3,2,1,0:T(8,128)S(1)}, u32[]{:S(2)}, u32[]{:S(2)}) collective-permute-start(f32[20,8,8,128]{3,2,1,0:T(8,128)S(1)} %prepare.1.own.own_kind), channel_id=1, source_target_pairs={{1,0},{2,1},{3,2},{4,3},{5,4},{6,5},{7,6},{9,8},{10,9},{11,10},{12... | collective-permute-start | bytes 1966088 | tf_op jit(solution)/shard_map/ppermute | solution.py:304
  3.4 3.1 %collective-permute-start = (f32[20,8,8,128]{3,2,1,0:T(8,128)S(1)}, f32[20,8,8,128]{3,2,1,0:T(8,128)S(1)}, u32[]{:S(2)}, u32[]{:S(2)}) collective-permute-start(f32[20,8,8,128]{3,2,1,0:T(8,128)S(1)} %prepare.1.own.own_kind), channel_id=1, source_target_pairs={{0,1},{1,2},{2,3},{3,4},{4,5},{5,6},{6,7},{8,9},{9,10},{10,11},{11... | collective-permute-start | bytes 1966088 | tf_op jit(solution)/shard_map/ppermute | solution.py:304
  6.5 0.0 collective-permute-done.1.right.right_kind
  6.5 1.7 %collective-permute-done.left.left_kind = f32[20,8,8,128]{3,2,1,0:T(8,128)S(1)} collective-permute-done((f32[20,8,8,128]{3,2,1,0:T(8,128)S(1)}, f32[20,8,8,128]{3,2,1,0:T(8,128)S(1)}, u32[]{:S(2)}, u32[]{:S(2)}) %collective-permute-start) | collective-permute-done | bytes 655392 | tf_op jit(solution)/shard_map/ppermute | solution.py:304
  8.1 3.6 %first_round.1.own = f32[16,8,8,128]{3,2,1,0:T(8,128)S(1)} custom-call(f32[20,8,8,128]{3,2,1,0:T(8,128)S(1)} %collective-permute-done.left.left_kind, f32[20,8,8,128]{3,2,1,0:T(8,128)S(1)} %prepare.1.own.own_kind, f32[20,8,8,128]{3,2,1,0:T(8,128)S(1)} %collective-permute-done.1.right.right_kind), custom_call_target="tpu_custom_call" | custom-call | tf_op jit(solution)/shard_map/first_round/pallas_call | solution.py:326
  11.7 1.3 %collective-permute-start.3 = (f32[16,8,8,128]{3,2,1,0:T(8,128)S(1)}, f32[16,8,8,128]{3,2,1,0:T(8,128)S(1)}, u32[]{:S(2)}, u32[]{:S(2)}) collective-permute-start(f32[16,8,8,128]{3,2,1,0:T(8,128)S(1)} %first_round.1.own), channel_id=1, source_target_pairs={{1,0},{2,1},{3,2},{4,3},{5,4},{6,5},{7,6},{9,8},{10,9},{11,10},{12... | collective-permute-start | bytes 1572872 | tf_op jit(solution)/shard_map/ppermute | solution.py:304
  13.0 13.9 %collective-permute-start.2 = (f32[16,8,8,128]{3,2,1,0:T(8,128)S(1)}, f32[16,8,8,128]{3,2,1,0:T(8,128)S(1)}, u32[]{:S(2)}, u32[]{:S(2)}) collective-permute-start(f32[16,8,8,128]{3,2,1,0:T(8,128)S(1)} %first_round.1.own), channel_id=1, source_target_pairs={{0,1},{1,2},{2,3},{3,4},{4,5},{5,6},{6,7},{8,9},{9,10},{10,11},{11... | collective-permute-start | bytes 1572872 | tf_op jit(solution)/shard_map/ppermute | solution.py:304
  26.9 1.4 %guess_old.1.guess = f32[16,128]{1,0:T(8,128)S(1)} custom-call(f32[20,8,8,128]{3,2,1,0:T(8,128)S(1)} %collective-permute-done.left.left_kind, f32[20,8,8,128]{3,2,1,0:T(8,128)S(1)} %prepare.1.own.own_kind, f32[20,8,8,128]{3,2,1,0:T(8,128)S(1)} %collective-permute-done.1.right.right_kind), custom_call_target="tpu_custom_call" | custom-call | tf_op jit(solution)/shard_map/guess_old/pallas_call | solution.py:336
  28.4 0.0 collective-permute-done.3.right
  28.4 0.0 collective-permute-done.2.left
  28.4 4.0 %second_round.1 = (f32[16,8,8,128]{3,2,1,0:T(8,128)S(1)}, f32[4,16,128]{2,1,0:T(8,128)S(1)}) custom-call(f32[16,8,8,128]{3,2,1,0:T(8,128)S(1)} %collective-permute-done.2.left, f32[16,8,8,128]{3,2,1,0:T(8,128)S(1)} %first_round.1.own, f32[16,8,8,128]{3,2,1,0:T(8,128)S(1)} %collective-permute-done.3.right, ...), custom_call_target="tpu_custom_call" | custom-call | tf_op jit(solution)/shard_map/second_round/pallas_call | solution.py:344
  32.4 10.3 %all_to_all.10.jumps = f32[4,16,128]{2,1,0:T(8,128)S(1)} all-to-all(f32[4,16,128]{2,1,0:T(8,128)S(1)} %get-tuple-element.7), channel_id=1, replica_groups=mesh['tm'=4,'space'=8] {'tm'}, dimensions={0} | all-to-all | bytes 65536 | tf_op jit(solution)/shard_map/all_to_all | solution.py:353
  42.8 24.4 %all_to_all.11.jumps = f32[8,3,16,128]{3,2,1,0:T(8,128)S(1)} all-to-all(f32[8,3,16,128]{3,2,1,0:T(8,128)S(1)} %repeat.1), channel_id=1, replica_groups=mesh['tm'=4,'space'=8] {'space'}, dimensions={0} | all-to-all | bytes 393216 | tf_op jit(solution)/shard_map/all_to_all | solution.py:362
  67.2 2.0 %correct.1 = f32[1,4,4,64,128]{4,3,2,1,0:T(8,128)} custom-call(f32[8,3,16,128]{3,2,1,0:T(8,128)S(1)} %all_to_all.11.jumps, f32[16,128]{1,0:T(8,128)S(1)} %guess_old.1.guess, f32[16,8,8,128]{3,2,1,0:T(8,128)S(1)} %get-tuple-element.8.fine_end), custom_call_target="tpu_custom_call" | custom-call | tf_op jit(solution)/shard_map/correct/pallas_call | solution.py:363
  (1 shorter events, 0.0 us)
Async XLA Ops:
  0.0 1.0 %copy-start = (f32[1,4,4,64,128]{4,3,2,1,0:T(8,128)S(1)}, f32[1,4,4,64,128]{4,3,2,1,0:T(8,128)}, u32[]{:S(2)}) copy-start(f32[1,4,4,64,128]{4,3,2,1,0:T(8,128)} %starts.1) | copy-start | bytes 1572868
  1.0 0.9 %copy-start.1 = (s32[4,64,128]{2,1,0:T(8,128)S(1)}, s32[4,64,128]{2,1,0:T(8,128)}, u32[]{:S(2)}) copy-start(s32[4,64,128]{2,1,0:T(8,128)} %flags.1) | copy-start | bytes 393220
  2.1 4.4 %collective-permute-start.1 = (f32[20,8,8,128]{3,2,1,0:T(8,128)S(1)}, f32[20,8,8,128]{3,2,1,0:T(8,128)S(1)}, u32[]{:S(2)}, u32[]{:S(2)}) collective-permute-start(f32[20,8,8,128]{3,2,1,0:T(8,128)S(1)} %prepare.1.own.own_kind), channel_id=1, source_target_pairs={{1,0},{2,1},{3,2},{4,3},{5,4},{6,5},{7,6},{9,8},{10,9},{11,10},{12... | collective-permute-start | bytes 1966088 | tf_op jit(solution)/shard_map/ppermute | solution.py:304
  3.4 4.7 %collective-permute-start = (f32[20,8,8,128]{3,2,1,0:T(8,128)S(1)}, f32[20,8,8,128]{3,2,1,0:T(8,128)S(1)}, u32[]{:S(2)}, u32[]{:S(2)}) collective-permute-start(f32[20,8,8,128]{3,2,1,0:T(8,128)S(1)} %prepare.1.own.own_kind), channel_id=1, source_target_pairs={{0,1},{1,2},{2,3},{3,4},{4,5},{5,6},{6,7},{8,9},{9,10},{10,11},{11... | collective-permute-start | bytes 1966088 | tf_op jit(solution)/shard_map/ppermute | solution.py:304
  11.7 16.7 %collective-permute-start.3 = (f32[16,8,8,128]{3,2,1,0:T(8,128)S(1)}, f32[16,8,8,128]{3,2,1,0:T(8,128)S(1)}, u32[]{:S(2)}, u32[]{:S(2)}) collective-permute-start(f32[16,8,8,128]{3,2,1,0:T(8,128)S(1)} %first_round.1.own), channel_id=1, source_target_pairs={{1,0},{2,1},{3,2},{4,3},{5,4},{6,5},{7,6},{9,8},{10,9},{11,10},{12... | collective-permute-start | bytes 1572872 | tf_op jit(solution)/shard_map/ppermute | solution.py:304
  13.0 15.4 %collective-permute-start.2 = (f32[16,8,8,128]{3,2,1,0:T(8,128)S(1)}, f32[16,8,8,128]{3,2,1,0:T(8,128)S(1)}, u32[]{:S(2)}, u32[]{:S(2)}) collective-permute-start(f32[16,8,8,128]{3,2,1,0:T(8,128)S(1)} %first_round.1.own), channel_id=1, source_target_pairs={{0,1},{1,2},{2,3},{3,4},{4,5},{5,6},{6,7},{8,9},{9,10},{10,11},{11... | collective-permute-start | bytes 1572872 | tf_op jit(solution)/shard_map/ppermute | solution.py:304

commit v4 on v3

--- a/solution.py
+++ b/solution.py
@@ -36,18 +36,18 @@
     return pltpu.CompilerParams(vmem_limit_bytes=LIMIT)
 
 
-def prepare_kernel(starts, flags, sent):
+def prepare_kernel(starts, flags, tiles, kinds):
+    own = natural(starts)
     for f in range(FIELDS):
         for x in range(PLANES):
             for t in range(TILES):
-                v = starts[0, f, x, pl.ds(t, 8, stride=8), :]
-                sent[f * PLANES + x, t] = v * 0.5 if f == 0 else v
+                tiles[f * PLANES + x, t] = own(f, x, t)
     for x in range(PLANES):
         for t in range(TILES):
-            sent[PACKED + x, t] = flags[x, pl.ds(t, 8, stride=8), :].astype(F32)
-
-
-def fine_tile(mid, lo_x, hi_x, lo_y, hi_y, kv, ks, low_lane, high_lane):
+            kinds[x, pl.ds(8 * t, 8), :] = flags[x, pl.ds(t, 8, stride=8), :]
+
+
+def fine_tile(mid, lo_x, hi_x, lo_y, hi_y, kv, ks, kc, low_lane, high_lane):
     beta = 1.0 / fine_dt - 7.0
     alpha = 1.0 / fine_dt - 6.0
     lo_z = [jnp.where(low_lane, 0.0, pltpu.roll(v, 1, 1)) for v in mid]
@@ -62,14 +62,15 @@
     new_w = kv * ((total[0] + 0.125 * diverge) + alpha * w)
     new_a = ks * ((total[1] + gx) + a * stretch)
     new_b = ks * ((total[2] + gy) + b * stretch)
-    new_c = fine_dt * ((total[3] + 2.0 * (gx * a + gy * b)) + ((stretch + gz) * c + 1.0))
+    new_c = kc * ((total[3] + 2.0 * (gx * a + gy * b)) + ((stretch + gz) * c + 1.0))
     return new_w, new_a, new_b, new_c
 
 
-def fine_plane(src, keep, p, store):
+def fine_plane(src, keep, p, inside, store):
     lane = iota((8, NZ), 1)
     low_lane, high_lane = lane == 0, lane == NZ - 1
     fields = range(FIELDS)
+    kc = jnp.where(inside(p), fine_dt, 0.0).astype(F32)
     for begin in range(0, TILES, GROUP):
         tiles = range(begin, begin + GROUP)
         column = [[src[f, p, t] for f in fields] for t in range(begin, begin + GROUP + 2)]
@@ -77,7 +78,7 @@
         hi_x = [[src[f, p + 1, t + 1] for f in fields] for t in tiles]
         kept = [(keep[0, p, t], keep[1, p, t]) for t in tiles]
         fresh = [
-            fine_tile(column[i + 1], lo_x[i], hi_x[i], column[i], column[i + 2], *kept[i], low_lane, high_lane)
+            fine_tile(column[i + 1], lo_x[i], hi_x[i], column[i], column[i + 2], *kept[i], kc, low_lane, high_lane)
             for i in range(GROUP)
         ]
         for i, t in enumerate(tiles):
@@ -94,68 +95,73 @@
         buffer[f, p, 0] = jnp.where(row == 0, 0.0, pltpu.roll(value, 1, 0))
 
 
-def fine_round(space_size, place, parts, kinds, even, odd, keep, finish):
-    for j, part in enumerate(parts):
-
-        def load(x, carry, j=j, part=part):
+def fine_round(space_size, parts, kinds, even, odd, keep, planes_at_once, finish):
+    place = lax.axis_index("space")
+
+    def inside(p):
+        x = (place - 1) * PLANES + p
+        return (x >= 0) & (x < space_size * PLANES)
+
+    for j in range(3):
+
+        def load(x, carry, j=j):
+            p = j * PLANES + x
             for f in range(FIELDS):
                 for t in range(TILES):
-                    put_tile(even, f, j * PLANES + x, t, part[f * PLANES + x, t])
+                    put_tile(even, f, p, t, parts[j](f, x, t))
+            scale = jnp.where(inside(p), fine_dt, 0.0).astype(F32)
+            for t in range(TILES):
+                kind = kinds[j][x, pl.ds(8 * t, 8), :] if j == 1 else kinds[j][x, pl.ds(t, 8, stride=8), :]
+                keep[0, p, t] = jnp.where(kind != 1, scale, 0.0)
+                keep[1, p, t] = jnp.where(kind != 2, scale, 0.0)
             return carry
 
         lax.fori_loop(0, PLANES, load, 0)
 
-        def convert(x, carry, j=j, kind=kinds[j]):
-            v = kind[PACKED + x]
-            keep[0, j * PLANES + x] = jnp.where(v != 1.0, fine_dt, 0.0).astype(F32)
-            keep[1, j * PLANES + x] = jnp.where(v != 2.0, fine_dt, 0.0).astype(F32)
+    for step in range(ROUND):
+        src, dst = (even, odd) if step % 2 == 0 else (odd, even)
+        count = WINDOW - 2 * (step + 1)
+        many = planes_at_once(count)
+
+        def body(i, carry, src=src, dst=dst, first=step + 1, many=many):
+            for k in range(many):
+                p = first + i * many + k
+                if first == ROUND:
+                    store = lambda f, t, value: finish(f, p - PLANES, t, value)
+                else:
+                    store = lambda f, t, value: put_tile(dst, f, p, t, value)
+                fine_plane(src, keep, p, inside, store)
             return carry
 
-        lax.fori_loop(0, PLANES, convert, 0)
-
-    for edge, outside in ((PLANES - 1, place == 0), (2 * PLANES, place == space_size - 1)):
-
-        @pl.when(outside)
-        def _(edge=edge):
-            for f in range(FIELDS):
-                odd[f, edge] = jnp.zeros((TILES + 2, 8, NZ), F32)
-
-    first = jnp.where(place == 0, PLANES, 0)
-    last = jnp.where(place == space_size - 1, 2 * PLANES, WINDOW)
-    for step in range(ROUND - 1):
-        src, dst = (even, odd) if step % 2 == 0 else (odd, even)
-
-        def body(p, carry, src=src, dst=dst):
-            fine_plane(src, keep, p, lambda f, t, value: put_tile(dst, f, p, t, value))
-            return carry
-
-        lax.fori_loop(jnp.maximum(1 + step, first), jnp.minimum(WINDOW - 1 - step, last), body, 0)
-
-    src = even if ROUND % 2 == 1 else odd
-
-    def final(p, carry):
-        fine_plane(src, keep, p, lambda f, t, value: finish(f, p - PLANES, t, value))
-        return carry
-
-    lax.fori_loop(PLANES, 2 * PLANES, final, 0)
-
-
-def first_kernel(space_size, left, own, right, sent, even, odd, keep):
-    parts = (left, own, right)
-
+        lax.fori_loop(0, count // many, body, 0)
+
+
+def natural(part):
+    def tile(f, x, t):
+        v = part[0, f, x, pl.ds(t, 8, stride=8), :]
+        return v * 0.5 if f == 0 else v
+
+    return tile
+
+
+def tiled(part):
+    return lambda f, x, t: part[f * PLANES + x, t]
+
+
+def first_kernel(space_size, left, own, right, left_kind, own_kind, right_kind, ended, even, odd, keep):
     def finish(f, x, t, value):
-        sent[f * PLANES + x, t] = value
-
-    fine_round(space_size, lax.axis_index("space"), parts, parts, even, odd, keep, finish)
+        ended[f * PLANES + x, t] = value
+
+    parts = [natural(left), tiled(own), natural(right)]
+    fine_round(space_size, parts, (left_kind, own_kind, right_kind), even, odd, keep, lambda count: 2, finish)
 
 
 def coarse_rows(pair_of, count):
     pairs = count // 2
     pieces = []
     for k in range(pairs):
-        v = pair_of(k)
         for i in range(TILES // 2):
-            pieces.append(v[2 * i] + v[2 * i + 1])
+            pieces.append(pair_of(k, 2 * i) + pair_of(k, 2 * i + 1))
     stacked = jnp.concatenate(pieces, axis=0)
     gather = (iota((NZ, NZ), 0) // 16 == iota((NZ, NZ), 1) % 8).astype(F32)
     sums = jnp.dot(stacked, gather, precision=HIGHEST, preferred_element_type=F32)
@@ -218,7 +224,7 @@
 
 def guess_kernel(space_size, left, own, right, guess):
     place = lax.axis_index("space")
-    parts = (left, own, right)
+    parts = [natural(left), tiled(own), natural(right)]
     rows = 16
     row = iota((rows, NZ), 0)
     plane = 2 * place - 2 + row // 2
@@ -226,10 +232,8 @@
     state = []
     for f in range(FIELDS):
 
-        def pair_of(k, f=f):
-            part = parts[k // 2]
-            x = f * PLANES + k % 2 * 2
-            return part[x] + part[x + 1]
+        def pair_of(k, t, f=f):
+            return parts[k // 2](f, k % 2 * 2, t) + parts[k // 2](f, k % 2 * 2 + 1, t)
 
         grid = halves(coarse_rows(pair_of, WINDOW), rows)
         state.append(grid * 2.0 if f == 0 else grid)
@@ -241,30 +245,26 @@
 
 def second_kernel(space_size, left, own, right, left_kind, own_kind, right_kind, guess, fine_end, jump, even, odd, keep):
     kinds = (left_kind, own_kind, right_kind)
+    parts = [tiled(part) for part in (left, own, right)]
 
     def finish(f, x, t, value):
         fine_end[f * PLANES + x, t] = value * 2.0 if f == 0 else value
 
-    fine_round(space_size, lax.axis_index("space"), (left, own, right), kinds, even, odd, keep, finish)
-    ended = halves(coarse_rows(lambda k: fine_end[2 * k] + fine_end[2 * k + 1], PACKED), PACKED)
+    fine_round(space_size, parts, kinds, even, odd, keep, lambda count: count // 2, finish)
+    ended = halves(coarse_rows(lambda k, t: fine_end[2 * k, t] + fine_end[2 * k + 1, t], PACKED), PACKED)
     jumped = ended - jnp.where(lax.axis_index("tm") == 0, 0.0, guess[...])
     for k in range(jump.shape[0]):
         jump[k] = jumped
 
 
-def repeat_kernel(jumps, repeated):
-    for k in range(repeated.shape[0]):
-        repeated[k] = jumps[pl.ds(0, repeated.shape[1])]
-
-
 def correct_kernel(jumps, guess, fine_end, out, grids, change):
-    spaces, slices = jumps.shape[0], jumps.shape[1] + 1
+    slices, spaces = jumps.shape[:2]
     mine = lax.axis_index("tm")
     place = lax.axis_index("space")
     for m in range(slices - 1):
         for s in range(spaces):
             for f in range(FIELDS):
-                grids[m, f, pl.ds(4 * s, 4), :] = jumps[s, m, pl.ds(4 * f, 4), :]
+                grids[m, f, pl.ds(4 * s, 4), :] = jumps[m, s, pl.ds(4 * f, 4), :]
     state = [grids[0, f] for f in range(FIELDS)]
     kept = state
     for m in range(1, slices):
@@ -314,24 +314,25 @@
         pltpu.VMEM((FIELDS, WINDOW, TILES + 2, 8, NZ), F32),
         pltpu.VMEM((2, WINDOW, TILES, 8, NZ), F32),
     ]
-    opening = pl.pallas_call(
+    left, right = neighbours(starts, space_size)
+    left_kind, right_kind = neighbours(flags, space_size)
+    own, own_kind = pl.pallas_call(
         prepare_kernel,
-        out_shape=shaped(PACKED + PLANES, TILES, 8, NZ),
+        out_shape=(shaped(PACKED, TILES, 8, NZ), jax.ShapeDtypeStruct(flags.shape, flags.dtype)),
         in_specs=[VMEM] * 2,
-        out_specs=VMEM,
+        out_specs=(VMEM, VMEM),
         compiler_params=params(),
         name="prepare",
     )(starts, flags)
-    left, right = neighbours(opening, space_size)
     middle = pl.pallas_call(
         functools.partial(first_kernel, space_size),
         out_shape=shaped(PACKED, TILES, 8, NZ),
-        in_specs=[VMEM] * 3,
+        in_specs=[VMEM] * 6,
         out_specs=VMEM,
         scratch_shapes=fine_scratch,
         compiler_params=params(),
         name="first_round",
-    )(left, opening, right)
+    )(left, own, right, left_kind, own_kind, right_kind)
     middle_left, middle_right = neighbours(middle, space_size)
     guess = pl.pallas_call(
         functools.partial(guess_kernel, space_size),
@@ -340,26 +341,18 @@
         out_specs=VMEM,
         compiler_params=params(),
         name="guess_old",
-    )(left, opening, right)
+    )(left, own, right)
     fine_end, jump = pl.pallas_call(
         functools.partial(second_kernel, space_size),
-        out_shape=(shaped(PACKED, TILES, 8, NZ), shaped(slices, PACKED, NZ)),
+        out_shape=(shaped(PACKED, TILES, 8, NZ), shaped(slices * space_size, PACKED, NZ)),
         in_specs=[VMEM] * 7,
         out_specs=(VMEM, VMEM),
         scratch_shapes=fine_scratch,
         compiler_params=params(),
         name="second_round",
-    )(middle_left, middle, middle_right, left, opening, right, guess)
-    earlier = lax.all_to_all(jump, "tm", 0, 0)
-    earlier = pl.pallas_call(
-        repeat_kernel,
-        out_shape=shaped(space_size, slices - 1, PACKED, NZ),
-        in_specs=[VMEM],
-        out_specs=VMEM,
-        compiler_params=params(),
-        name="repeat",
-    )(earlier)
-    jumps = lax.all_to_all(earlier, "space", 0, 0)
+    )(middle_left, middle, middle_right, left_kind, own_kind, right_kind, guess)
+    jumps = lax.all_to_all(jump, ("tm", "space"), 0, 0)
+    jumps = jumps.reshape(slices, space_size, PACKED, NZ)
     return pl.pallas_call(
         correct_kernel,
         out_shape=shaped(1, FIELDS, PLANES, NY, NZ),

time: 69.4 us -> 61.7 us (0.89)
  blocking collectives: 34.7 us -> 26.2 us
  starting transfers between devices: 19.6 us -> 23.1 us
  waiting for transfers between devices: 1.7 us -> 0.03 us
  Pallas kernels: 11.1 us -> 10.1 us
    all_to_all x2 -> x1, blocking collectives: 34.7 us -> 26.2 us  [local(): jumps = lax.all_to_all(jump, ('tm', 'space'), 0, 0)]
    ppermute x2 -> x3, starting transfers between devices: 17 us -> 19.2 us  [neighbours(): lax.ppermute(block, 'space', upward)]
    ppermute x2 -> x3, waiting for transfers between devices: 1.69 us -> 0.02 us  [neighbours(): lax.ppermute(block, 'space', upward)]
    ppermute x2 -> x3, starting transfers between devices: 2.58 us -> 3.88 us  [neighbours(): lax.ppermute(block, 'space', downward)]
    pallas_call x1, Pallas kernels: 4.01 us -> 3.2 us  [local(): pl.pallas_call(functools.partial(second_kernel, space_size), out_shape=(s...]
  transfers between devices with their start and end apart: 4 -> 6, of which waited for: 1 -> 0; matrix products, arithmetic and copies ran while one was open for 0% -> 0% of each run, Pallas kernels for 2% -> 3%
where the time goes in v4:
time: 61.7 us; the launch traced here: 61.4 us
  blocking collectives  26.2 us (42%)
  starting transfers between devices  23.1 us (37%)
  Pallas kernels  10.1 us (16%)
  local copies, waits for them, and re-layouts  1.94 us (3%)
    all_to_all x1, blocking collectives, local(): jumps = lax.all_to_all(jump, ('tm', 'space'), 0, 0)  26.2 us
    ppermute x3, starting transfers between devices, neighbours(): lax.ppermute(block, 'space', upward)  19.2 us
    ppermute x3, starting transfers between devices, neighbours(): lax.ppermute(block, 'space', downward)  3.88 us
    pallas_call x1, Pallas kernels, local(): pl.pallas_call(functools.partial(first_kernel, space_size), out_shape=sha...  3.31 us
    pallas_call x1, Pallas kernels, local(): pl.pallas_call(functools.partial(second_kernel, space_size), out_shape=(s...  3.2 us
    pallas_call x1, Pallas kernels, local(): pl.pallas_call(correct_kernel, out_shape=shaped(1, FIELDS, PLANES, NY, NZ...  1.98 us
    unnamed x4, local copies, waits for them, and re-layouts  1.94 us
    pallas_call x1, Pallas kernels, local(): pl.pallas_call(functools.partial(guess_kernel, space_size), out_shape=sha...  1.45 us
  transfers between devices with their start and end apart: 6, of which 0 were waited for; matrix products, arithmetic and copies ran while one was open for 0% of the time, Pallas kernels for 3%

profile of v4, /device:TPU:0, one launch (start us, length us, event | category | flops | bytes accessed | tf_op | source)
XLA Modules:
  0.0 61.4 jit_solution(6271391361645128699)
XLA Ops:
  0.0 2.4 %collective-permute-start = (f32[1,4,4,64,128]{4,3,2,1,0:T(8,128)}, f32[1,4,4,64,128]{4,3,2,1,0:T(8,128)S(1)}, u32[]{:S(2)}, u32[]{:S(2)}) collective-permute-start(f32[1,4,4,64,128]{4,3,2,1,0:T(8,128)} %starts.1), channel_id=1, source_target_pairs={{0,1},{1,2},{2,3},{3,4},{4,5},{5,6},{6,7},{8,9},{9,10},{10,11},{11... | collective-permute-start | bytes 1572872 | tf_op jit(solution)/shard_map/ppermute | solution.py:304
  2.4 1.3 %collective-permute-start.1 = (f32[1,4,4,64,128]{4,3,2,1,0:T(8,128)}, f32[1,4,4,64,128]{4,3,2,1,0:T(8,128)S(1)}, u32[]{:S(2)}, u32[]{:S(2)}) collective-permute-start(f32[1,4,4,64,128]{4,3,2,1,0:T(8,128)} %starts.1), channel_id=1, source_target_pairs={{1,0},{2,1},{3,2},{4,3},{5,4},{6,5},{7,6},{9,8},{10,9},{11,10},{12... | collective-permute-start | bytes 1572872 | tf_op jit(solution)/shard_map/ppermute | solution.py:304
  3.7 1.3 %collective-permute-start.3 = (s32[4,64,128]{2,1,0:T(8,128)}, s32[4,64,128]{2,1,0:T(8,128)S(1)}, u32[]{:S(2)}, u32[]{:S(2)}) collective-permute-start(s32[4,64,128]{2,1,0:T(8,128)} %flags.1), channel_id=1, source_target_pairs={{1,0},{2,1},{3,2},{4,3},{5,4},{6,5},{7,6},{9,8},{10,9},{11,10},{12... | collective-permute-start | bytes 393224 | tf_op jit(solution)/shard_map/ppermute | solution.py:304
  5.0 5.7 %collective-permute-start.2 = (s32[4,64,128]{2,1,0:T(8,128)}, s32[4,64,128]{2,1,0:T(8,128)S(1)}, u32[]{:S(2)}, u32[]{:S(2)}) collective-permute-start(s32[4,64,128]{2,1,0:T(8,128)} %flags.1), channel_id=1, source_target_pairs={{0,1},{1,2},{2,3},{3,4},{4,5},{5,6},{6,7},{8,9},{9,10},{10,11},{11... | collective-permute-start | bytes 393224 | tf_op jit(solution)/shard_map/ppermute | solution.py:304
  10.7 0.0 copy-start
  10.7 1.0 %copy-done = f32[1,4,4,64,128]{4,3,2,1,0:T(8,128)S(1)} copy-done((f32[1,4,4,64,128]{4,3,2,1,0:T(8,128)S(1)}, f32[1,4,4,64,128]{4,3,2,1,0:T(8,128)}, u32[]{:S(2)}) %copy-start) | copy-done | bytes 524312
  11.8 0.0 copy-start.1
  11.8 0.9 %copy-done.1 = s32[4,64,128]{2,1,0:T(8,128)S(1)} copy-done((s32[4,64,128]{2,1,0:T(8,128)S(1)}, s32[4,64,128]{2,1,0:T(8,128)}, u32[]{:S(2)}) %copy-start.1) | copy-done | bytes 131096
  12.7 0.1 prepare.1
  12.8 0.0 collective-permute-done.3.right_kind
  12.8 0.0 collective-permute-done.2.left_kind
  12.8 0.0 collective-permute-done.left
  12.8 0.0 collective-permute-done.1.right
  12.9 3.3 %first_round.1.own = f32[16,8,8,128]{3,2,1,0:T(8,128)S(1)} custom-call(f32[1,4,4,64,128]{4,3,2,1,0:T(8,128)S(1)} %collective-permute-done.left, f32[16,8,8,128]{3,2,1,0:T(8,128)S(1)} %get-tuple-element.9.own, f32[1,4,4,64,128]{4,3,2,1,0:T(8,128)S(1)} %collective-permute-done.1.right, s32[4,64,128]{2,1,0:T(8,128)S(1)} %collective-permute-done.2.left_kind, ...), custom_call_target="tpu_custom_call" | custom-call | tf_op jit(solution)/shard_map/first_round/pallas_call | solution.py:327
  16.2 1.3 %collective-permute-start.5 = (f32[16,8,8,128]{3,2,1,0:T(8,128)S(1)}, f32[16,8,8,128]{3,2,1,0:T(8,128)S(1)}, u32[]{:S(2)}, u32[]{:S(2)}) collective-permute-start(f32[16,8,8,128]{3,2,1,0:T(8,128)S(1)} %first_round.1.own), channel_id=1, source_target_pairs={{1,0},{2,1},{3,2},{4,3},{5,4},{6,5},{7,6},{9,8},{10,9},{11,10},{12... | collective-permute-start | bytes 1572872 | tf_op jit(solution)/shard_map/ppermute | solution.py:304
  17.5 11.1 %collective-permute-start.4 = (f32[16,8,8,128]{3,2,1,0:T(8,128)S(1)}, f32[16,8,8,128]{3,2,1,0:T(8,128)S(1)}, u32[]{:S(2)}, u32[]{:S(2)}) collective-permute-start(f32[16,8,8,128]{3,2,1,0:T(8,128)S(1)} %first_round.1.own), channel_id=1, source_target_pairs={{0,1},{1,2},{2,3},{3,4},{4,5},{5,6},{6,7},{8,9},{9,10},{10,11},{11... | collective-permute-start | bytes 1572872 | tf_op jit(solution)/shard_map/ppermute | solution.py:304
  28.6 1.5 %guess_old.1.guess = f32[16,128]{1,0:T(8,128)S(1)} custom-call(f32[1,4,4,64,128]{4,3,2,1,0:T(8,128)S(1)} %collective-permute-done.left, f32[16,8,8,128]{3,2,1,0:T(8,128)S(1)} %get-tuple-element.9.own, f32[1,4,4,64,128]{4,3,2,1,0:T(8,128)S(1)} %collective-permute-done.1.right), custom_call_target="tpu_custom_call" | custom-call | tf_op jit(solution)/shard_map/guess_old/pallas_call | solution.py:337
  30.0 0.0 collective-permute-done.5.right
  30.0 0.0 collective-permute-done.4.left
  30.0 3.2 %second_round.1 = (f32[16,8,8,128]{3,2,1,0:T(8,128)S(1)}, f32[32,16,128]{2,1,0:T(8,128)S(1)}) custom-call(f32[16,8,8,128]{3,2,1,0:T(8,128)S(1)} %collective-permute-done.4.left, f32[16,8,8,128]{3,2,1,0:T(8,128)S(1)} %first_round.1.own, f32[16,8,8,128]{3,2,1,0:T(8,128)S(1)} %collective-permute-done.5.right, ...), custom_call_target="tpu_custom_call" | custom-call | tf_op jit(solution)/shard_map/second_round/pallas_call | solution.py:345
  33.2 26.2 %all_to_all.5 = f32[32,16,128]{2,1,0:T(8,128)S(1)} all-to-all(f32[32,16,128]{2,1,0:T(8,128)S(1)} %get-tuple-element.11), channel_id=1, replica_groups=mesh['tm'=4,'space'=8] {'tm','space'}, dimensions={0} | all-to-all | bytes 524288 | tf_op jit(solution)/shard_map/all_to_all | solution.py:354
  59.4 2.0 %correct.1 = f32[1,4,4,64,128]{4,3,2,1,0:T(8,128)} custom-call(f32[4,8,16,128]{3,2,1,0:T(8,128)S(1)} %bitcast.1, f32[16,128]{1,0:T(8,128)S(1)} %guess_old.1.guess, f32[16,8,8,128]{3,2,1,0:T(8,128)S(1)} %get-tuple-element.12.fine_end), custom_call_target="tpu_custom_call" | custom-call | tf_op jit(solution)/shard_map/correct/pallas_call | solution.py:356
Async XLA Ops:
  0.0 12.8 %collective-permute-start = (f32[1,4,4,64,128]{4,3,2,1,0:T(8,128)}, f32[1,4,4,64,128]{4,3,2,1,0:T(8,128)S(1)}, u32[]{:S(2)}, u32[]{:S(2)}) collective-permute-start(f32[1,4,4,64,128]{4,3,2,1,0:T(8,128)} %starts.1), channel_id=1, source_target_pairs={{0,1},{1,2},{2,3},{3,4},{4,5},{5,6},{6,7},{8,9},{9,10},{10,11},{11... | collective-permute-start | bytes 1572872 | tf_op jit(solution)/shard_map/ppermute | solution.py:304
  2.4 10.5 %collective-permute-start.1 = (f32[1,4,4,64,128]{4,3,2,1,0:T(8,128)}, f32[1,4,4,64,128]{4,3,2,1,0:T(8,128)S(1)}, u32[]{:S(2)}, u32[]{:S(2)}) collective-permute-start(f32[1,4,4,64,128]{4,3,2,1,0:T(8,128)} %starts.1), channel_id=1, source_target_pairs={{1,0},{2,1},{3,2},{4,3},{5,4},{6,5},{7,6},{9,8},{10,9},{11,10},{12... | collective-permute-start | bytes 1572872 | tf_op jit(solution)/shard_map/ppermute | solution.py:304
  3.7 9.1 %collective-permute-start.3 = (s32[4,64,128]{2,1,0:T(8,128)}, s32[4,64,128]{2,1,0:T(8,128)S(1)}, u32[]{:S(2)}, u32[]{:S(2)}) collective-permute-start(s32[4,64,128]{2,1,0:T(8,128)} %flags.1), channel_id=1, source_target_pairs={{1,0},{2,1},{3,2},{4,3},{5,4},{6,5},{7,6},{9,8},{10,9},{11,10},{12... | collective-permute-start | bytes 393224 | tf_op jit(solution)/shard_map/ppermute | solution.py:304
  5.0 7.8 %collective-permute-start.2 = (s32[4,64,128]{2,1,0:T(8,128)}, s32[4,64,128]{2,1,0:T(8,128)S(1)}, u32[]{:S(2)}, u32[]{:S(2)}) collective-permute-start(s32[4,64,128]{2,1,0:T(8,128)} %flags.1), channel_id=1, source_target_pairs={{0,1},{1,2},{2,3},{3,4},{4,5},{5,6},{6,7},{8,9},{9,10},{10,11},{11... | collective-permute-start | bytes 393224 | tf_op jit(solution)/shard_map/ppermute | solution.py:304
  10.7 1.0 %copy-start = (f32[1,4,4,64,128]{4,3,2,1,0:T(8,128)S(1)}, f32[1,4,4,64,128]{4,3,2,1,0:T(8,128)}, u32[]{:S(2)}) copy-start(f32[1,4,4,64,128]{4,3,2,1,0:T(8,128)} %starts.1) | copy-start | bytes 1572868
  11.8 0.9 %copy-start.1 = (s32[4,64,128]{2,1,0:T(8,128)S(1)}, s32[4,64,128]{2,1,0:T(8,128)}, u32[]{:S(2)}) copy-start(s32[4,64,128]{2,1,0:T(8,128)} %flags.1) | copy-start | bytes 393220
  16.2 13.8 %collective-permute-start.5 = (f32[16,8,8,128]{3,2,1,0:T(8,128)S(1)}, f32[16,8,8,128]{3,2,1,0:T(8,128)S(1)}, u32[]{:S(2)}, u32[]{:S(2)}) collective-permute-start(f32[16,8,8,128]{3,2,1,0:T(8,128)S(1)} %first_round.1.own), channel_id=1, source_target_pairs={{1,0},{2,1},{3,2},{4,3},{5,4},{6,5},{7,6},{9,8},{10,9},{11,10},{12... | collective-permute-start | bytes 1572872 | tf_op jit(solution)/shard_map/ppermute | solution.py:304
  17.5 12.6 %collective-permute-start.4 = (f32[16,8,8,128]{3,2,1,0:T(8,128)S(1)}, f32[16,8,8,128]{3,2,1,0:T(8,128)S(1)}, u32[]{:S(2)}, u32[]{:S(2)}) collective-permute-start(f32[16,8,8,128]{3,2,1,0:T(8,128)S(1)} %first_round.1.own), channel_id=1, source_target_pairs={{0,1},{1,2},{2,3},{3,4},{4,5},{5,6},{6,7},{8,9},{9,10},{10,11},{11... | collective-permute-start | bytes 1572872 | tf_op jit(solution)/shard_map/ppermute | solution.py:304

commit v5 on v4

--- a/solution.py
+++ b/solution.py
@@ -36,15 +36,22 @@
     return pltpu.CompilerParams(vmem_limit_bytes=LIMIT)
 
 
-def prepare_kernel(starts, flags, tiles, kinds):
-    own = natural(starts)
-    for f in range(FIELDS):
+def prepare_kernel(starts, flags, message_one, message_two, fields, kinds, sems):
+    copies = [pltpu.make_async_copy(starts, fields, sems.at[0]), pltpu.make_async_copy(flags, kinds, sems.at[1])]
+    for copy in copies:
+        copy.start()
+    for copy in copies:
+        copy.wait()
+    for f in range(FIELDS):
+        message = message_one if f < 2 else message_two
         for x in range(PLANES):
             for t in range(TILES):
-                tiles[f * PLANES + x, t] = own(f, x, t)
+                v = fields[0, f, x, pl.ds(t, 8, stride=8), :]
+                message[f % 2 * PLANES + x, t] = v * 0.5 if f == 0 else v
     for x in range(PLANES):
+        message = message_one if x < 2 else message_two
         for t in range(TILES):
-            kinds[x, pl.ds(8 * t, 8), :] = flags[x, pl.ds(t, 8, stride=8), :]
+            message[2 * PLANES + x % 2, t] = kinds[x, pl.ds(t, 8, stride=8), :].astype(F32)
 
 
 def fine_tile(mid, lo_x, hi_x, lo_y, hi_y, kv, ks, kc, low_lane, high_lane):
@@ -66,11 +73,11 @@
     return new_w, new_a, new_b, new_c
 
 
-def fine_plane(src, keep, p, inside, store):
+def fine_plane(src, keep, p, valid, store):
     lane = iota((8, NZ), 1)
     low_lane, high_lane = lane == 0, lane == NZ - 1
     fields = range(FIELDS)
-    kc = jnp.where(inside(p), fine_dt, 0.0).astype(F32)
+    kc = jnp.where(valid, fine_dt, 0.0).astype(F32)
     for begin in range(0, TILES, GROUP):
         tiles = range(begin, begin + GROUP)
         column = [[src[f, p, t] for f in fields] for t in range(begin, begin + GROUP + 2)]
@@ -95,65 +102,77 @@
         buffer[f, p, 0] = jnp.where(row == 0, 0.0, pltpu.roll(value, 1, 0))
 
 
-def fine_round(space_size, parts, kinds, even, odd, keep, planes_at_once, finish):
-    place = lax.axis_index("space")
-
-    def inside(p):
-        x = (place - 1) * PLANES + p
-        return (x >= 0) & (x < space_size * PLANES)
-
+class Slabs:
+
+    def __init__(self, space_size, own, first, second):
+        place = lax.axis_index("space")
+        self.own = own
+        self.first = {0: first[0], 2: first[1]}
+        self.second = second
+        self.low = place < turn(space_size)
+        self.there = {0: place > 0, 2: place < space_size - 1}
+
+    def row(self, j, half, k, t):
+        if j == 1:
+            return self.own[half][k, t]
+        if half == 0:
+            return self.first[j][k, t]
+        x, y = self.second[0][k, t], self.second[1][k, t]
+        v = jnp.where(self.low, x, y) if j == 0 else jnp.where(self.low, y, x)
+        return jnp.where(self.there[j], v, 0.0)
+
+    def field(self, j, f, x, t):
+        return self.row(j, f // 2, f % 2 * PLANES + x, t)
+
+    def kind(self, j, x, t):
+        return self.row(j, x // 2, 2 * PLANES + x % 2, t)
+
+
+def inside(space_size, p):
+    x = (lax.axis_index("space") - 1) * PLANES + p
+    return (x >= 0) & (x < space_size * PLANES)
+
+
+def fine_round(space_size, slabs, even, odd, keep, finish):
     for j in range(3):
-
-        def load(x, carry, j=j):
-            p = j * PLANES + x
+        for x in range(PLANES):
             for f in range(FIELDS):
                 for t in range(TILES):
-                    put_tile(even, f, p, t, parts[j](f, x, t))
-            scale = jnp.where(inside(p), fine_dt, 0.0).astype(F32)
-            for t in range(TILES):
-                kind = kinds[j][x, pl.ds(8 * t, 8), :] if j == 1 else kinds[j][x, pl.ds(t, 8, stride=8), :]
-                keep[0, p, t] = jnp.where(kind != 1, scale, 0.0)
-                keep[1, p, t] = jnp.where(kind != 2, scale, 0.0)
-            return carry
-
-        lax.fori_loop(0, PLANES, load, 0)
+                    put_tile(even, f, j * PLANES + x, t, slabs.field(j, f, x, t))
 
     for step in range(ROUND):
         src, dst = (even, odd) if step % 2 == 0 else (odd, even)
-        count = WINDOW - 2 * (step + 1)
-        many = planes_at_once(count)
-
-        def body(i, carry, src=src, dst=dst, first=step + 1, many=many):
+        many = PLANES + ROUND // 2 - 1 - step
+
+        def body(i, carry, src=src, dst=dst, step=step, many=many):
             for k in range(many):
-                p = first + i * many + k
-                if first == ROUND:
+                p = step + 1 + i * many + k
+                if step == ROUND - 1:
                     store = lambda f, t, value: finish(f, p - PLANES, t, value)
                 else:
                     store = lambda f, t, value: put_tile(dst, f, p, t, value)
-                fine_plane(src, keep, p, inside, store)
+                fine_plane(src, keep, p, inside(space_size, p), store)
             return carry
 
-        lax.fori_loop(0, count // many, body, 0)
-
-
-def natural(part):
-    def tile(f, x, t):
-        v = part[0, f, x, pl.ds(t, 8, stride=8), :]
-        return v * 0.5 if f == 0 else v
-
-    return tile
-
-
-def tiled(part):
-    return lambda f, x, t: part[f * PLANES + x, t]
-
-
-def first_kernel(space_size, left, own, right, left_kind, own_kind, right_kind, ended, even, odd, keep):
+        lax.fori_loop(0, 2, body, 0)
+
+
+def first_kernel(space_size, own_one, own_two, up, down, x, y, ended_one, ended_two, keep, even, odd):
+    slabs = Slabs(space_size, (own_one, own_two), (up, down), (x, y))
+    for j in range(3):
+        for k in range(PLANES):
+            p = j * PLANES + k
+            scale = jnp.where(inside(space_size, p), fine_dt, 0.0).astype(F32)
+            for t in range(TILES):
+                kind = slabs.kind(j, k, t)
+                keep[0, p, t] = jnp.where(kind != 1.0, scale, 0.0)
+                keep[1, p, t] = jnp.where(kind != 2.0, scale, 0.0)
+
     def finish(f, x, t, value):
-        ended[f * PLANES + x, t] = value
-
-    parts = [natural(left), tiled(own), natural(right)]
-    fine_round(space_size, parts, (left_kind, own_kind, right_kind), even, odd, keep, lambda count: 2, finish)
+        ended = ended_one if f < 2 else ended_two
+        ended[f % 2 * PLANES + x, t] = value
+
+    fine_round(space_size, slabs, even, odd, keep, finish)
 
 
 def coarse_rows(pair_of, count):
@@ -222,35 +241,34 @@
     return new_w, new_a, new_b, new_c
 
 
-def guess_kernel(space_size, left, own, right, guess):
+def guess_kernel(space_size, own_one, own_two, up, down, x, y, guess):
     place = lax.axis_index("space")
-    parts = [natural(left), tiled(own), natural(right)]
+    slabs = Slabs(space_size, (own_one, own_two), (up, down), (x, y))
     rows = 16
     row = iota((rows, NZ), 0)
     plane = 2 * place - 2 + row // 2
-    inside = (row < WINDOW) & (plane >= 0) & (plane < 2 * space_size)
+    valid = (row < WINDOW) & (plane >= 0) & (plane < 2 * space_size)
     state = []
     for f in range(FIELDS):
 
         def pair_of(k, t, f=f):
-            return parts[k // 2](f, k % 2 * 2, t) + parts[k // 2](f, k % 2 * 2 + 1, t)
+            return slabs.field(k // 2, f, k % 2 * 2, t) + slabs.field(k // 2, f, k % 2 * 2 + 1, t)
 
         grid = halves(coarse_rows(pair_of, WINDOW), rows)
         state.append(grid * 2.0 if f == 0 else grid)
     for _ in range(COARSE_STEPS):
-        state = [jnp.where(inside, v, 0.0) for v in coarse_step(state)]
+        state = [jnp.where(valid, v, 0.0) for v in coarse_step(state)]
     for f in range(FIELDS):
         guess[pl.ds(4 * f, 4), :] = state[f][4:8]
 
 
-def second_kernel(space_size, left, own, right, left_kind, own_kind, right_kind, guess, fine_end, jump, even, odd, keep):
-    kinds = (left_kind, own_kind, right_kind)
-    parts = [tiled(part) for part in (left, own, right)]
+def second_kernel(space_size, own_one, own_two, up, down, x, y, keep, guess, fine_end, jump, even, odd):
+    slabs = Slabs(space_size, (own_one, own_two), (up, down), (x, y))
 
     def finish(f, x, t, value):
         fine_end[f * PLANES + x, t] = value * 2.0 if f == 0 else value
 
-    fine_round(space_size, parts, kinds, even, odd, keep, lambda count: count // 2, finish)
+    fine_round(space_size, slabs, even, odd, keep, finish)
     ended = halves(coarse_rows(lambda k, t: fine_end[2 * k, t] + fine_end[2 * k + 1, t], PACKED), PACKED)
     jumped = ended - jnp.where(lax.axis_index("tm") == 0, 0.0, guess[...])
     for k in range(jump.shape[0]):
@@ -298,10 +316,30 @@
                 out[0, f, x, pl.ds(t, 8, stride=8), :] = fine_end[f * PLANES + x, t] + wide[k : k + 8]
 
 
-def neighbours(block, size):
+def relayed(size):
+    return size == 8
+
+
+def turn(size):
+    return size // 2 if relayed(size) else size
+
+
+def exchange(one, two, size):
     upward = [(i, i + 1) for i in range(size - 1)]
     downward = [(target, source) for source, target in upward]
-    return lax.ppermute(block, "space", upward), lax.ppermute(block, "space", downward)
+    if relayed(size):
+        half = size // 2
+        low_up, high_up = upward[: half - 1], upward[half:]
+        low_down, high_down = downward[: half - 1], downward[half:]
+        x = lax.ppermute(two, "space", low_up + high_down + [(half - 1, size - 1), (half, 0)])
+        up, down = lax.ppermute(one, "space", upward), lax.ppermute(one, "space", downward)
+        place = lax.axis_index("space")
+        passed = jnp.where((place == 0) | (place == size - 1), x, two)
+        y = lax.ppermute(passed, "space", low_down + high_up + [(0, half - 1), (size - 1, half)])
+    else:
+        x, y = lax.ppermute(two, "space", upward), lax.ppermute(two, "space", downward)
+        up, down = lax.ppermute(one, "space", upward), lax.ppermute(one, "space", downward)
+    return up, down, x, y
 
 
 def shaped(*shape):
@@ -309,48 +347,51 @@
 
 
 def local(slices, space_size, starts, flags):
-    fine_scratch = [
-        pltpu.VMEM((FIELDS, WINDOW, TILES + 2, 8, NZ), F32),
-        pltpu.VMEM((FIELDS, WINDOW, TILES + 2, 8, NZ), F32),
-        pltpu.VMEM((2, WINDOW, TILES, 8, NZ), F32),
-    ]
-    left, right = neighbours(starts, space_size)
-    left_kind, right_kind = neighbours(flags, space_size)
-    own, own_kind = pl.pallas_call(
+    half = shaped(2 * PLANES, TILES, 8, NZ)
+    message = shaped(2 * PLANES + 2, TILES, 8, NZ)
+    keep_shape = shaped(2, WINDOW, TILES, 8, NZ)
+    buffers = [pltpu.VMEM((FIELDS, WINDOW, TILES + 2, 8, NZ), F32)] * 2
+    opening = pl.pallas_call(
         prepare_kernel,
-        out_shape=(shaped(PACKED, TILES, 8, NZ), jax.ShapeDtypeStruct(flags.shape, flags.dtype)),
-        in_specs=[VMEM] * 2,
+        out_shape=(message, message),
+        in_specs=[pl.BlockSpec(memory_space=pltpu.HBM)] * 2,
         out_specs=(VMEM, VMEM),
+        scratch_shapes=[
+            pltpu.VMEM(starts.shape, F32),
+            pltpu.VMEM(flags.shape, flags.dtype),
+            pltpu.SemaphoreType.DMA((2,)),
+        ],
         compiler_params=params(),
         name="prepare",
     )(starts, flags)
-    middle = pl.pallas_call(
+    opening_near = exchange(*opening, space_size)
+    *middle, keep = pl.pallas_call(
         functools.partial(first_kernel, space_size),
-        out_shape=shaped(PACKED, TILES, 8, NZ),
+        out_shape=(half, half, keep_shape),
         in_specs=[VMEM] * 6,
-        out_specs=VMEM,
-        scratch_shapes=fine_scratch,
+        out_specs=(VMEM,) * 3,
+        scratch_shapes=buffers,
         compiler_params=params(),
         name="first_round",
-    )(left, own, right, left_kind, own_kind, right_kind)
-    middle_left, middle_right = neighbours(middle, space_size)
+    )(*opening, *opening_near)
+    middle_near = exchange(*middle, space_size)
     guess = pl.pallas_call(
         functools.partial(guess_kernel, space_size),
         out_shape=shaped(PACKED, NZ),
-        in_specs=[VMEM] * 3,
+        in_specs=[VMEM] * 6,
         out_specs=VMEM,
         compiler_params=params(),
         name="guess_old",
-    )(left, own, right)
+    )(*opening, *opening_near)
     fine_end, jump = pl.pallas_call(
         functools.partial(second_kernel, space_size),
         out_shape=(shaped(PACKED, TILES, 8, NZ), shaped(slices * space_size, PACKED, NZ)),
-        in_specs=[VMEM] * 7,
+        in_specs=[VMEM] * 8,
         out_specs=(VMEM, VMEM),
-        scratch_shapes=fine_scratch,
+        scratch_shapes=buffers,
         compiler_params=params(),
         name="second_round",
-    )(middle_left, middle, middle_right, left_kind, own_kind, right_kind, guess)
+    )(*middle, *middle_near, keep, guess)
     jumps = lax.all_to_all(jump, ("tm", "space"), 0, 0)
     jumps = jumps.reshape(slices, space_size, PACKED, NZ)
     return pl.pallas_call(

time: 61.7 us -> 58.1 us (0.942)
  waiting for transfers between devices: 0.03 us -> 11.9 us
  blocking collectives: 26.2 us -> 17.6 us
  starting transfers between devices: 23.1 us -> 16.7 us
    ppermute x6 -> x8, waiting for transfers between devices: 0.03 us -> 11.9 us  [the longest x2 9.44 us: exchange(): lax.ppermute(passed, 'space', low_down + high_up + [(0, half - 1), (size...]
    all_to_all x1, blocking collectives: 26.2 us -> 17.6 us  [local(): jumps = lax.all_to_all(jump, ('tm', 'space'), 0, 0)]
    ppermute x6 -> x8, starting transfers between devices: 23.1 us -> 16.7 us  [the longest x2 8.2 us: exchange(): lax.ppermute(one, 'space', upward)]
  transfers between devices with their start and end apart: 6 -> 8, of which waited for: 0 -> 4; matrix products, arithmetic and copies ran while one was open for 0% -> 0% of each run, Pallas kernels for 3% -> 2%
where the time goes in v5:
time: 58.1 us; the launch traced here: 57.8 us
  blocking collectives  17.6 us (30%)
  starting transfers between devices  16.7 us (29%)
  waiting for transfers between devices  11.9 us (20%)
  Pallas kernels  9.55 us (16%)
  local copies, waits for them, and re-layouts  1.94 us (3%)
    all_to_all x1, blocking collectives, local(): jumps = lax.all_to_all(jump, ('tm', 'space'), 0, 0)  17.6 us
    ppermute x2, waiting for transfers between devices, exchange(): lax.ppermute(passed, 'space', low_down + high_up + [(0, half - 1), (size...  9.44 us
    ppermute x2, starting transfers between devices, exchange(): lax.ppermute(one, 'space', upward)  8.2 us
    pallas_call x1, Pallas kernels, local(): pl.pallas_call(functools.partial(second_kernel, space_size), out_shape=(s...  3.09 us
    ppermute x2, starting transfers between devices, exchange(): lax.ppermute(two, 'space', low_up + high_down + [(half - 1, size - 1), (h...  3.02 us
    ppermute x2, starting transfers between devices, exchange(): lax.ppermute(passed, 'space', low_down + high_up + [(0, half - 1), (size...  2.9 us
    pallas_call x1, Pallas kernels, local(): pl.pallas_call(functools.partial(first_kernel, space_size), out_shape=(ha...  2.7 us
    ppermute x2, starting transfers between devices, exchange(): lax.ppermute(one, 'space', downward)  2.56 us
  transfers between devices with their start and end apart: 8, of which 4 were waited for; matrix products, arithmetic and copies ran while one was open for 0% of the time, Pallas kernels for 2%

profile of v5, /device:TPU:0, one launch (start us, length us, event | category | flops | bytes accessed | tf_op | source)
XLA Modules:
  0.0 57.8 jit_solution(2617636931477616756)
XLA Ops:
  0.0 1.0 %copy-done = f32[1,4,4,64,128]{4,3,2,1,0:T(8,128)S(1)} copy-done((f32[1,4,4,64,128]{4,3,2,1,0:T(8,128)S(1)}, f32[1,4,4,64,128]{4,3,2,1,0:T(8,128)}, u32[]{:S(2)}) %copy-start) | copy-done | bytes 524312
  1.0 0.9 %copy-done.1 = s32[4,64,128]{2,1,0:T(8,128)S(1)} copy-done((s32[4,64,128]{2,1,0:T(8,128)S(1)}, s32[4,64,128]{2,1,0:T(8,128)}, u32[]{:S(2)}) %copy-start.1) | copy-done | bytes 131096
  1.9 0.3 prepare.1
  2.3 0.5 collective-permute-start.2
  2.8 1.3 %collective-permute-start.1 = (f32[10,8,8,128]{3,2,1,0:T(8,128)S(1)}, f32[10,8,8,128]{3,2,1,0:T(8,128)S(1)}, u32[]{:S(2)}, u32[]{:S(2)}) collective-permute-start(f32[10,8,8,128]{3,2,1,0:T(8,128)S(1)} %get-tuple-element.12.own_one), channel_id=1, source_target_pairs={{1,0},{2,1},{3,2},{4,3},{5,4},{6,5},{7,6},{9,8},{10,9},{11,10},{12... | collective-permute-start | bytes 983048 | tf_op jit(solution)/shard_map/ppermute | solution.py:335
  4.1 5.2 %collective-permute-start = (f32[10,8,8,128]{3,2,1,0:T(8,128)S(1)}, f32[10,8,8,128]{3,2,1,0:T(8,128)S(1)}, u32[]{:S(2)}, u32[]{:S(2)}) collective-permute-start(f32[10,8,8,128]{3,2,1,0:T(8,128)S(1)} %get-tuple-element.12.own_one), channel_id=1, source_target_pairs={{0,1},{1,2},{2,3},{3,4},{4,5},{5,6},{6,7},{8,9},{9,10},{10,11},{11... | collective-permute-start | bytes 983048 | tf_op jit(solution)/shard_map/ppermute | solution.py:335
  9.3 1.1 %collective-permute-done.2.x = f32[10,8,8,128]{3,2,1,0:T(8,128)S(1)} collective-permute-done((f32[10,8,8,128]{3,2,1,0:T(8,128)S(1)}, f32[10,8,8,128]{3,2,1,0:T(8,128)S(1)}, u32[]{:S(2)}, u32[]{:S(2)}) %collective-permute-start.2) | collective-permute-done | bytes 327712 | tf_op jit(solution)/shard_map/ppermute | solution.py:334
  10.4 2.1 %collective-permute-start.3 = (f32[10,8,8,128]{3,2,1,0:T(8,128)S(1)}, f32[10,8,8,128]{3,2,1,0:T(8,128)S(1)}, u32[]{:S(2)}, u32[]{:S(2)}) collective-permute-start(f32[10,8,8,128]{3,2,1,0:T(8,128)S(1)} %broadcast_select_fusion), channel_id=1, source_target_pairs={{1,0},{2,1},{3,2},{4,5},{5,6},{6,7},{0,3},{7,4},{9,8},{10,9},{11,1... | collective-permute-start | bytes 983048 | tf_op jit(solution)/shard_map/ppermute | solution.py:338
  12.6 0.0 collective-permute-done.1.down
  12.6 0.0 collective-permute-done.up
  12.6 5.8 %collective-permute-done.3.y = f32[10,8,8,128]{3,2,1,0:T(8,128)S(1)} collective-permute-done((f32[10,8,8,128]{3,2,1,0:T(8,128)S(1)}, f32[10,8,8,128]{3,2,1,0:T(8,128)S(1)}, u32[]{:S(2)}, u32[]{:S(2)}) %collective-permute-start.3) | collective-permute-done | bytes 327712 | tf_op jit(solution)/shard_map/ppermute | solution.py:338
  18.4 2.7 %first_round.1 = (f32[8,8,8,128]{3,2,1,0:T(8,128)S(1)}, f32[8,8,8,128]{3,2,1,0:T(8,128)S(1)}, f32[2,12,8,8,128]{4,3,2,1,0:T(8,128)S(1)}) custom-call(f32[10,8,8,128]{3,2,1,0:T(8,128)S(1)} %get-tuple-element.12.own_one, f32[10,8,8,128]{3,2,1,0:T(8,128)S(1)} %get-tuple-element.13.own_two, f32[10,8,8,128]{3,2,1,0:T(8,128)S(1)} %collective-permute-done.up, ...), custom_call_target="tpu_custom_call" | custom-call | tf_op jit(solution)/shard_map/first_round/pallas_call | solution.py:368
  21.1 2.5 %collective-permute-start.6 = (f32[8,8,8,128]{3,2,1,0:T(8,128)S(1)}, f32[8,8,8,128]{3,2,1,0:T(8,128)S(1)}, u32[]{:S(2)}, u32[]{:S(2)}) collective-permute-start(f32[8,8,8,128]{3,2,1,0:T(8,128)S(1)} %get-tuple-element.15.own_two), channel_id=1, source_target_pairs={{0,1},{1,2},{2,3},{5,4},{6,5},{7,6},{3,7},{4,0},{8,9},{9,10},{10,1... | collective-permute-start | bytes 786440 | tf_op jit(solution)/shard_map/ppermute | solution.py:334
  23.6 1.3 %collective-permute-start.5 = (f32[8,8,8,128]{3,2,1,0:T(8,128)S(1)}, f32[8,8,8,128]{3,2,1,0:T(8,128)S(1)}, u32[]{:S(2)}, u32[]{:S(2)}) collective-permute-start(f32[8,8,8,128]{3,2,1,0:T(8,128)S(1)} %get-tuple-element.14.own_one), channel_id=1, source_target_pairs={{1,0},{2,1},{3,2},{4,3},{5,4},{6,5},{7,6},{9,8},{10,9},{11,10},{12... | collective-permute-start | bytes 786440 | tf_op jit(solution)/shard_map/ppermute | solution.py:335
  24.9 3.0 %collective-permute-start.4 = (f32[8,8,8,128]{3,2,1,0:T(8,128)S(1)}, f32[8,8,8,128]{3,2,1,0:T(8,128)S(1)}, u32[]{:S(2)}, u32[]{:S(2)}) collective-permute-start(f32[8,8,8,128]{3,2,1,0:T(8,128)S(1)} %get-tuple-element.14.own_one), channel_id=1, source_target_pairs={{0,1},{1,2},{2,3},{3,4},{4,5},{5,6},{6,7},{8,9},{9,10},{10,11},{11... | collective-permute-start | bytes 786440 | tf_op jit(solution)/shard_map/ppermute | solution.py:335
  27.9 1.4 %collective-permute-done.6.x = f32[8,8,8,128]{3,2,1,0:T(8,128)S(1)} collective-permute-done((f32[8,8,8,128]{3,2,1,0:T(8,128)S(1)}, f32[8,8,8,128]{3,2,1,0:T(8,128)S(1)}, u32[]{:S(2)}, u32[]{:S(2)}) %collective-permute-start.6) | collective-permute-done | bytes 262176 | tf_op jit(solution)/shard_map/ppermute | solution.py:334
  29.3 0.8 %collective-permute-start.7 = (f32[8,8,8,128]{3,2,1,0:T(8,128)S(1)}, f32[8,8,8,128]{3,2,1,0:T(8,128)S(1)}, u32[]{:S(2)}, u32[]{:S(2)}) collective-permute-start(f32[8,8,8,128]{3,2,1,0:T(8,128)S(1)} %broadcast_select_fusion.1), channel_id=1, source_target_pairs={{1,0},{2,1},{3,2},{4,5},{5,6},{6,7},{0,3},{7,4},{9,8},{10,9},{11,1... | collective-permute-start | bytes 786440 | tf_op jit(solution)/shard_map/ppermute | solution.py:338
  30.1 1.4 %guess_old.1.guess = f32[16,128]{1,0:T(8,128)S(1)} custom-call(f32[10,8,8,128]{3,2,1,0:T(8,128)S(1)} %get-tuple-element.12.own_one, f32[10,8,8,128]{3,2,1,0:T(8,128)S(1)} %get-tuple-element.13.own_two, f32[10,8,8,128]{3,2,1,0:T(8,128)S(1)} %collective-permute-done.up, f32[10,8,8,128]{3,2,1,0:T(8,128)S(1)} %collective-permute-done.1.down, ...), custom_call_target="tpu_custom_call" | custom-call | tf_op jit(solution)/shard_map/guess_old/pallas_call | solution.py:378
  31.5 0.0 collective-permute-done.5.down
  31.5 0.0 collective-permute-done.4.up
  31.5 3.6 %collective-permute-done.7.y = f32[8,8,8,128]{3,2,1,0:T(8,128)S(1)} collective-permute-done((f32[8,8,8,128]{3,2,1,0:T(8,128)S(1)}, f32[8,8,8,128]{3,2,1,0:T(8,128)S(1)}, u32[]{:S(2)}, u32[]{:S(2)}) %collective-permute-start.7) | collective-permute-done | bytes 262176 | tf_op jit(solution)/shard_map/ppermute | solution.py:338
  35.2 3.1 %second_round.1 = (f32[16,8,8,128]{3,2,1,0:T(8,128)S(1)}, f32[32,16,128]{2,1,0:T(8,128)S(1)}) custom-call(f32[8,8,8,128]{3,2,1,0:T(8,128)S(1)} %get-tuple-element.14.own_one, f32[8,8,8,128]{3,2,1,0:T(8,128)S(1)} %get-tuple-element.15.own_two, f32[8,8,8,128]{3,2,1,0:T(8,128)S(1)} %collective-permute-done.4.up, ...), custom_call_target="tpu_custom_call" | custom-call | tf_op jit(solution)/shard_map/second_round/pallas_call | solution.py:386
  38.3 17.6 %all_to_all.5 = f32[32,16,128]{2,1,0:T(8,128)S(1)} all-to-all(f32[32,16,128]{2,1,0:T(8,128)S(1)} %get-tuple-element.17), channel_id=1, replica_groups=mesh['tm'=4,'space'=8] {'tm','space'}, dimensions={0} | all-to-all | bytes 524288 | tf_op jit(solution)/shard_map/all_to_all | solution.py:395
  55.8 2.0 %correct.1 = f32[1,4,4,64,128]{4,3,2,1,0:T(8,128)} custom-call(f32[4,8,16,128]{3,2,1,0:T(8,128)S(1)} %bitcast.1, f32[16,128]{1,0:T(8,128)S(1)} %guess_old.1.guess, f32[16,8,8,128]{3,2,1,0:T(8,128)S(1)} %get-tuple-element.18.fine_end), custom_call_target="tpu_custom_call" | custom-call | tf_op jit(solution)/shard_map/correct/pallas_call | solution.py:397
  (4 shorter events, 0.1 us)
Async XLA Ops:
  0.0 1.0 %copy-start = (f32[1,4,4,64,128]{4,3,2,1,0:T(8,128)S(1)}, f32[1,4,4,64,128]{4,3,2,1,0:T(8,128)}, u32[]{:S(2)}) copy-start(f32[1,4,4,64,128]{4,3,2,1,0:T(8,128)} %starts.1) | copy-start | bytes 1572868
  1.0 0.9 %copy-start.1 = (s32[4,64,128]{2,1,0:T(8,128)S(1)}, s32[4,64,128]{2,1,0:T(8,128)}, u32[]{:S(2)}) copy-start(s32[4,64,128]{2,1,0:T(8,128)} %flags.1) | copy-start | bytes 393220
  2.3 8.1 %collective-permute-start.2 = (f32[10,8,8,128]{3,2,1,0:T(8,128)S(1)}, f32[10,8,8,128]{3,2,1,0:T(8,128)S(1)}, u32[]{:S(2)}, u32[]{:S(2)}) collective-permute-start(f32[10,8,8,128]{3,2,1,0:T(8,128)S(1)} %get-tuple-element.13.own_two), channel_id=1, source_target_pairs={{0,1},{1,2},{2,3},{5,4},{6,5},{7,6},{3,7},{4,0},{8,9},{9,10},{10,1... | collective-permute-start | bytes 983048 | tf_op jit(solution)/shard_map/ppermute | solution.py:334
  2.8 9.8 %collective-permute-start.1 = (f32[10,8,8,128]{3,2,1,0:T(8,128)S(1)}, f32[10,8,8,128]{3,2,1,0:T(8,128)S(1)}, u32[]{:S(2)}, u32[]{:S(2)}) collective-permute-start(f32[10,8,8,128]{3,2,1,0:T(8,128)S(1)} %get-tuple-element.12.own_one), channel_id=1, source_target_pairs={{1,0},{2,1},{3,2},{4,3},{5,4},{6,5},{7,6},{9,8},{10,9},{11,10},{12... | collective-permute-start | bytes 983048 | tf_op jit(solution)/shard_map/ppermute | solution.py:335
  4.1 8.5 %collective-permute-start = (f32[10,8,8,128]{3,2,1,0:T(8,128)S(1)}, f32[10,8,8,128]{3,2,1,0:T(8,128)S(1)}, u32[]{:S(2)}, u32[]{:S(2)}) collective-permute-start(f32[10,8,8,128]{3,2,1,0:T(8,128)S(1)} %get-tuple-element.12.own_one), channel_id=1, source_target_pairs={{0,1},{1,2},{2,3},{3,4},{4,5},{5,6},{6,7},{8,9},{9,10},{10,11},{11... | collective-permute-start | bytes 983048 | tf_op jit(solution)/shard_map/ppermute | solution.py:335
  10.4 7.9 %collective-permute-start.3 = (f32[10,8,8,128]{3,2,1,0:T(8,128)S(1)}, f32[10,8,8,128]{3,2,1,0:T(8,128)S(1)}, u32[]{:S(2)}, u32[]{:S(2)}) collective-permute-start(f32[10,8,8,128]{3,2,1,0:T(8,128)S(1)} %broadcast_select_fusion), channel_id=1, source_target_pairs={{1,0},{2,1},{3,2},{4,5},{5,6},{6,7},{0,3},{7,4},{9,8},{10,9},{11,1... | collective-permute-start | bytes 983048 | tf_op jit(solution)/shard_map/ppermute | solution.py:338
  21.1 8.2 %collective-permute-start.6 = (f32[8,8,8,128]{3,2,1,0:T(8,128)S(1)}, f32[8,8,8,128]{3,2,1,0:T(8,128)S(1)}, u32[]{:S(2)}, u32[]{:S(2)}) collective-permute-start(f32[8,8,8,128]{3,2,1,0:T(8,128)S(1)} %get-tuple-element.15.own_two), channel_id=1, source_target_pairs={{0,1},{1,2},{2,3},{5,4},{6,5},{7,6},{3,7},{4,0},{8,9},{9,10},{10,1... | collective-permute-start | bytes 786440 | tf_op jit(solution)/shard_map/ppermute | solution.py:334
  23.6 7.9 %collective-permute-start.5 = (f32[8,8,8,128]{3,2,1,0:T(8,128)S(1)}, f32[8,8,8,128]{3,2,1,0:T(8,128)S(1)}, u32[]{:S(2)}, u32[]{:S(2)}) collective-permute-start(f32[8,8,8,128]{3,2,1,0:T(8,128)S(1)} %get-tuple-element.14.own_one), channel_id=1, source_target_pairs={{1,0},{2,1},{3,2},{4,3},{5,4},{6,5},{7,6},{9,8},{10,9},{11,10},{12... | collective-permute-start | bytes 786440 | tf_op jit(solution)/shard_map/ppermute | solution.py:335
  24.9 6.6 %collective-permute-start.4 = (f32[8,8,8,128]{3,2,1,0:T(8,128)S(1)}, f32[8,8,8,128]{3,2,1,0:T(8,128)S(1)}, u32[]{:S(2)}, u32[]{:S(2)}) collective-permute-start(f32[8,8,8,128]{3,2,1,0:T(8,128)S(1)} %get-tuple-element.14.own_one), channel_id=1, source_target_pairs={{0,1},{1,2},{2,3},{3,4},{4,5},{5,6},{6,7},{8,9},{9,10},{10,11},{11... | collective-permute-start | bytes 786440 | tf_op jit(solution)/shard_map/ppermute | solution.py:335
  29.3 5.8 %collective-permute-start.7 = (f32[8,8,8,128]{3,2,1,0:T(8,128)S(1)}, f32[8,8,8,128]{3,2,1,0:T(8,128)S(1)}, u32[]{:S(2)}, u32[]{:S(2)}) collective-permute-start(f32[8,8,8,128]{3,2,1,0:T(8,128)S(1)} %broadcast_select_fusion.1), channel_id=1, source_target_pairs={{1,0},{2,1},{3,2},{4,5},{5,6},{6,7},{0,3},{7,4},{9,8},{10,9},{11,1... | collective-permute-start | bytes 786440 | tf_op jit(solution)/shard_map/ppermute | solution.py:338

commit v6 on v5

--- a/solution.py
+++ b/solution.py
@@ -104,21 +104,19 @@
 
 class Slabs:
 
-    def __init__(self, space_size, own, first, second):
+    def __init__(self, space_size, own, near):
         place = lax.axis_index("space")
         self.own = own
-        self.first = {0: first[0], 2: first[1]}
-        self.second = second
-        self.low = place < turn(space_size)
+        self.near = (near[:2], near[2:])
+        self.from_first = (place % 2 == 1, place < turn(space_size))
         self.there = {0: place > 0, 2: place < space_size - 1}
 
     def row(self, j, half, k, t):
         if j == 1:
             return self.own[half][k, t]
-        if half == 0:
-            return self.first[j][k, t]
-        x, y = self.second[0][k, t], self.second[1][k, t]
-        v = jnp.where(self.low, x, y) if j == 0 else jnp.where(self.low, y, x)
+        v, other = (ref[k, t] for ref in self.near[half])
+        first = self.from_first[half]
+        v = jnp.where(first, v, other) if j == 0 else jnp.where(first, other, v)
         return jnp.where(self.there[j], v, 0.0)
 
     def field(self, j, f, x, t):
@@ -157,8 +155,8 @@
         lax.fori_loop(0, 2, body, 0)
 
 
-def first_kernel(space_size, own_one, own_two, up, down, x, y, ended_one, ended_two, keep, even, odd):
-    slabs = Slabs(space_size, (own_one, own_two), (up, down), (x, y))
+def first_kernel(space_size, own_one, own_two, inner, outer, x, y, ended_one, ended_two, keep, even, odd):
+    slabs = Slabs(space_size, (own_one, own_two), (inner, outer, x, y))
     for j in range(3):
         for k in range(PLANES):
             p = j * PLANES + k
@@ -241,9 +239,9 @@
     return new_w, new_a, new_b, new_c
 
 
-def guess_kernel(space_size, own_one, own_two, up, down, x, y, guess):
+def guess_kernel(space_size, own_one, own_two, inner, outer, x, y, guess):
     place = lax.axis_index("space")
-    slabs = Slabs(space_size, (own_one, own_two), (up, down), (x, y))
+    slabs = Slabs(space_size, (own_one, own_two), (inner, outer, x, y))
     rows = 16
     row = iota((rows, NZ), 0)
     plane = 2 * place - 2 + row // 2
@@ -262,8 +260,8 @@
         guess[pl.ds(4 * f, 4), :] = state[f][4:8]
 
 
-def second_kernel(space_size, own_one, own_two, up, down, x, y, keep, guess, fine_end, jump, even, odd):
-    slabs = Slabs(space_size, (own_one, own_two), (up, down), (x, y))
+def second_kernel(space_size, own_one, own_two, inner, outer, x, y, keep, guess, fine_end, jump, even, odd):
+    slabs = Slabs(space_size, (own_one, own_two), (inner, outer, x, y))
 
     def finish(f, x, t, value):
         fine_end[f * PLANES + x, t] = value * 2.0 if f == 0 else value
@@ -271,36 +269,42 @@
     fine_round(space_size, slabs, even, odd, keep, finish)
     ended = halves(coarse_rows(lambda k, t: fine_end[2 * k, t] + fine_end[2 * k + 1, t], PACKED), PACKED)
     jumped = ended - jnp.where(lax.axis_index("tm") == 0, 0.0, guess[...])
-    for k in range(jump.shape[0]):
-        jump[k] = jumped
-
-
-def correct_kernel(jumps, guess, fine_end, out, grids, change):
-    slices, spaces = jumps.shape[:2]
+    jump[...] = jumped
+
+
+def correct_kernel(slices, space_size, *refs):
+    jumps, (guess, fine_end, out, grids) = refs[:-4], refs[-4:]
     mine = lax.axis_index("tm")
     place = lax.axis_index("space")
-    for m in range(slices - 1):
-        for s in range(spaces):
+    rows = grids.shape[2]
+    centre = 4 * slices
+    plane = 2 * (place - slices) + iota((rows, NZ), 0) // 2
+    valid = (plane >= 0) & (plane < 2 * space_size)
+    grids[...] = jnp.zeros_like(grids)
+    at = 0
+    for k in range(1, slices):
+        for j in range(-k, k + 1):
             for f in range(FIELDS):
-                grids[m, f, pl.ds(4 * s, 4), :] = jumps[m, s, pl.ds(4 * f, 4), :]
-    state = [grids[0, f] for f in range(FIELDS)]
-    kept = state
-    for m in range(1, slices):
+                grids[k - 1, f, pl.ds(centre + 4 * j, 4), :] = jumps[at][pl.ds(4 * f, 4), :]
+            at += 1
+    state = None
+    for k in range(slices - 1, -1, -1):
         ended = state
-        for _ in range(COARSE_STEPS):
-            ended = coarse_step(ended)
-        kept = [jnp.where(mine == m, ended[f], kept[f]) for f in range(FIELDS)]
-        if m < slices - 1:
-            state = [ended[f] + grids[m, f] for f in range(FIELDS)]
-    for f in range(FIELDS):
-        change[f] = kept[f]
+        if state is not None:
+            for _ in range(COARSE_STEPS):
+                ended = [jnp.where(valid, v, 0.0) for v in coarse_step(ended)]
+        if k > 0:
+            state = [jnp.where(valid, grids[k - 1, f], 0.0) for f in range(FIELDS)]
+            if ended is not None:
+                state = [state[f] + jnp.where(mine > k, ended[f], 0.0) for f in range(FIELDS)]
     row = iota((8, NZ), 0)
     pieces = []
     for f in range(FIELDS):
         for x in range(PLANES // 2):
             k = 2 * x
             lines = [
-                change[f, pl.ds(4 * place + k + half, 1), :] - guess[pl.ds(4 * f + k + half, 1), :] for half in range(2)
+                ended[f][centre + k + half : centre + k + half + 1] - guess[pl.ds(4 * f + k + half, 1), :]
+                for half in range(2)
             ]
             tile = jnp.where(row < 4, lines[0], lines[1])
             tile = jnp.where(mine == 0, 0.0, tile)
@@ -325,21 +329,38 @@
 
 
 def exchange(one, two, size):
-    upward = [(i, i + 1) for i in range(size - 1)]
-    downward = [(target, source) for source, target in upward]
+    inner = [(i, i ^ 1) for i in range(size)]
+    outer = [(0, 0)] + [(i, (i - 1 ^ 1) + 1) for i in range(1, size - 1)] + [(size - 1, size - 1)]
     if relayed(size):
         half = size // 2
-        low_up, high_up = upward[: half - 1], upward[half:]
-        low_down, high_down = downward[: half - 1], downward[half:]
-        x = lax.ppermute(two, "space", low_up + high_down + [(half - 1, size - 1), (half, 0)])
-        up, down = lax.ppermute(one, "space", upward), lax.ppermute(one, "space", downward)
+        first = [(i, i + 1) for i in range(half - 1)] + [(half - 1, size - 1)]
+        first += [(i, i - 1) for i in range(size - 1, half, -1)] + [(half, 0)]
+        second = [(i, i - 1) for i in range(half - 1, 0, -1)] + [(0, half - 1)]
+        second += [(i, i + 1) for i in range(half, size - 1)] + [(size - 1, half)]
+    else:
+        first = [(i, (i + 1) % size) for i in range(size)]
+        second = [(i, (i - 1) % size) for i in range(size)]
+    x = lax.ppermute(two, "space", first)
+    across = lax.ppermute(one, "space", outer)
+    within = lax.ppermute(one, "space", inner)
+    if relayed(size):
         place = lax.axis_index("space")
-        passed = jnp.where((place == 0) | (place == size - 1), x, two)
-        y = lax.ppermute(passed, "space", low_down + high_up + [(0, half - 1), (size - 1, half)])
-    else:
-        x, y = lax.ppermute(two, "space", upward), lax.ppermute(two, "space", downward)
-        up, down = lax.ppermute(one, "space", upward), lax.ppermute(one, "space", downward)
-    return up, down, x, y
+        two = jnp.where((place == 0) | (place == size - 1), x, two)
+    y = lax.ppermute(two, "space", second)
+    return within, across, x, y
+
+
+def earlier_jumps(jump, slices, space_size):
+    found = []
+    for k in range(1, slices):
+        for j in range(-k, k + 1):
+            route = []
+            for m in range(slices):
+                for s in range(space_size):
+                    target = (m + k) % slices * space_size + (s - j) % space_size
+                    route.append((m * space_size + s, target))
+            found.append(lax.ppermute(jump, ("tm", "space"), route))
+    return found
 
 
 def shaped(*shape):
@@ -385,27 +406,23 @@
     )(*opening, *opening_near)
     fine_end, jump = pl.pallas_call(
         functools.partial(second_kernel, space_size),
-        out_shape=(shaped(PACKED, TILES, 8, NZ), shaped(slices * space_size, PACKED, NZ)),
+        out_shape=(shaped(PACKED, TILES, 8, NZ), shaped(PACKED, NZ)),
         in_specs=[VMEM] * 8,
         out_specs=(VMEM, VMEM),
         scratch_shapes=buffers,
         compiler_params=params(),
         name="second_round",
     )(*middle, *middle_near, keep, guess)
-    jumps = lax.all_to_all(jump, ("tm", "space"), 0, 0)
-    jumps = jumps.reshape(slices, space_size, PACKED, NZ)
+    jumps = earlier_jumps(jump, slices, space_size)
     return pl.pallas_call(
-        correct_kernel,
+        functools.partial(correct_kernel, slices, space_size),
         out_shape=shaped(1, FIELDS, PLANES, NY, NZ),
-        in_specs=[VMEM] * 3,
+        in_specs=[VMEM] * (len(jumps) + 2),
         out_specs=VMEM,
-        scratch_shapes=[
-            pltpu.VMEM((slices, FIELDS, space_size * 4, NZ), F32),
-            pltpu.VMEM((FIELDS, space_size * 4, NZ), F32),
-        ],
+        scratch_shapes=[pltpu.VMEM((slices - 1, FIELDS, 8 * slices, NZ), F32)],
         compiler_params=params(),
         name="correct",
-    )(jumps, guess, fine_end)
+    )(*jumps, guess, fine_end)
 
 
 def solution(mesh):

time: 58.1 us -> 70.7 us (1.22)
  starting transfers between devices: 16.7 us -> 38.7 us
  blocking collectives: 17.6 us -> 0 us
  waiting for transfers between devices: 11.9 us -> 20.3 us
    ppermute x8 -> x23, starting transfers between devices: 16.7 us -> 38.7 us  [the longest x15 27.2 us: earlier_jumps(): found.append(lax.ppermute(jump, ('tm', 'space'), route))]
    all_to_all x1 -> x0, blocking collectives: 17.6 us -> none  [local(): jumps = lax.all_to_all(jump, ('tm', 'space'), 0, 0)]
    ppermute x8 -> x23, waiting for transfers between devices: 11.9 us -> 20.3 us  [the longest x2 9.35 us: exchange(): y = lax.ppermute(two, 'space', second)]
  transfers between devices with their start and end apart: 8 -> 23, of which waited for: 4 -> 7; matrix products, arithmetic and copies ran while one was open for 0% -> 0% of each run, Pallas kernels for 2% -> 2%
where the time goes in v6:
time: 70.7 us; the launch traced here: 70.5 us
  starting transfers between devices  38.7 us (55%)
  waiting for transfers between devices  20.3 us (29%)
  Pallas kernels  9.48 us (13%)
  local copies, waits for them, and re-layouts  1.94 us (3%)
    ppermute x15, starting transfers between devices, earlier_jumps(): found.append(lax.ppermute(jump, ('tm', 'space'), route))  27.2 us
    ppermute x2, waiting for transfers between devices, exchange(): y = lax.ppermute(two, 'space', second)  9.35 us
    ppermute x15, waiting for transfers between devices, earlier_jumps(): found.append(lax.ppermute(jump, ('tm', 'space'), route))  6.69 us
    ppermute x2, starting transfers between devices, exchange(): within = lax.ppermute(one, 'space', inner)  5.25 us
    ppermute x2, starting transfers between devices, exchange(): x = lax.ppermute(two, 'space', first)  4.25 us
    ppermute x2, waiting for transfers between devices, exchange(): x = lax.ppermute(two, 'space', first)  4.2 us
    pallas_call x1, Pallas kernels, local(): pl.pallas_call(functools.partial(second_kernel, space_size), out_shape=(s...  3.11 us
    pallas_call x1, Pallas kernels, local(): pl.pallas_call(functools.partial(first_kernel, space_size), out_shape=(ha...  2.73 us
  transfers between devices with their start and end apart: 23, of which 7 were waited for; matrix products, arithmetic and copies ran while one was open for 0% of the time, Pallas kernels for 2%

profile of v6, /device:TPU:0, one launch (start us, length us, event | category | flops | bytes accessed | tf_op | source)
XLA Modules:
  0.0 70.5 jit_solution(11928931310761924043)
XLA Ops:
  0.0 1.0 %copy-done = f32[1,4,4,64,128]{4,3,2,1,0:T(8,128)S(1)} copy-done((f32[1,4,4,64,128]{4,3,2,1,0:T(8,128)S(1)}, f32[1,4,4,64,128]{4,3,2,1,0:T(8,128)}, u32[]{:S(2)}) %copy-start) | copy-done | bytes 524312
  3.5 3.9 %collective-permute-start = (f32[10,8,8,128]{3,2,1,0:T(8,128)S(1)}, f32[10,8,8,128]{3,2,1,0:T(8,128)S(1)}, u32[]{:S(2)}, u32[]{:S(2)}) collective-permute-start(f32[10,8,8,128]{3,2,1,0:T(8,128)S(1)} %get-tuple-element.12.own_one), channel_id=1, source_target_pairs={{0,1},{1,0},{2,3},{3,2},{4,5},{5,4},{6,7},{7,6},{8,9},{9,8},{10,11... | collective-permute-start | bytes 983048 | tf_op jit(solution)/shard_map/ppermute | solution.py:345
  7.4 3.0 %collective-permute-done.2.x = f32[10,8,8,128]{3,2,1,0:T(8,128)S(1)} collective-permute-done((f32[10,8,8,128]{3,2,1,0:T(8,128)S(1)}, f32[10,8,8,128]{3,2,1,0:T(8,128)S(1)}, u32[]{:S(2)}, u32[]{:S(2)}) %collective-permute-start.2) | collective-permute-done | bytes 327712 | tf_op jit(solution)/shard_map/ppermute | solution.py:343
  10.5 5.8 %collective-permute-done.3.y = f32[10,8,8,128]{3,2,1,0:T(8,128)S(1)} collective-permute-done((f32[10,8,8,128]{3,2,1,0:T(8,128)S(1)}, f32[10,8,8,128]{3,2,1,0:T(8,128)S(1)}, u32[]{:S(2)}, u32[]{:S(2)}) %collective-permute-start.3) | collective-permute-done | bytes 327712 | tf_op jit(solution)/shard_map/ppermute | solution.py:349
  16.3 2.7 %first_round.1 = (f32[8,8,8,128]{3,2,1,0:T(8,128)S(1)}, f32[8,8,8,128]{3,2,1,0:T(8,128)S(1)}, f32[2,12,8,8,128]{4,3,2,1,0:T(8,128)S(1)}) custom-call(f32[10,8,8,128]{3,2,1,0:T(8,128)S(1)} %get-tuple-element.12.own_one, f32[10,8,8,128]{3,2,1,0:T(8,128)S(1)} %get-tuple-element.13.own_two, f32[10,8,8,128]{3,2,1,0:T(8,128)S(1)} %collective-permute-done.inner, ...), custom_call_target="tpu_custom_call" | custom-call | tf_op jit(solution)/shard_map/first_round/pallas_call | solution.py:389
  19.1 3.7 %collective-permute-start.6 = (f32[8,8,8,128]{3,2,1,0:T(8,128)S(1)}, f32[8,8,8,128]{3,2,1,0:T(8,128)S(1)}, u32[]{:S(2)}, u32[]{:S(2)}) collective-permute-start(f32[8,8,8,128]{3,2,1,0:T(8,128)S(1)} %get-tuple-element.15.own_two), channel_id=1, source_target_pairs={{0,1},{1,2},{2,3},{3,7},{7,6},{6,5},{5,4},{4,0},{8,9},{9,10},{10,1... | collective-permute-start | bytes 786440 | tf_op jit(solution)/shard_map/ppermute | solution.py:343
  23.5 1.3 %collective-permute-start.4 = (f32[8,8,8,128]{3,2,1,0:T(8,128)S(1)}, f32[8,8,8,128]{3,2,1,0:T(8,128)S(1)}, u32[]{:S(2)}, u32[]{:S(2)}) collective-permute-start(f32[8,8,8,128]{3,2,1,0:T(8,128)S(1)} %get-tuple-element.14.own_one), channel_id=1, source_target_pairs={{0,1},{1,0},{2,3},{3,2},{4,5},{5,4},{6,7},{7,6},{8,9},{9,8},{10,11... | collective-permute-start | bytes 786440 | tf_op jit(solution)/shard_map/ppermute | solution.py:345
  24.8 1.2 %collective-permute-done.6.x = f32[8,8,8,128]{3,2,1,0:T(8,128)S(1)} collective-permute-done((f32[8,8,8,128]{3,2,1,0:T(8,128)S(1)}, f32[8,8,8,128]{3,2,1,0:T(8,128)S(1)}, u32[]{:S(2)}, u32[]{:S(2)}) %collective-permute-start.6) | collective-permute-done | bytes 262176 | tf_op jit(solution)/shard_map/ppermute | solution.py:343
  26.6 1.4 %guess_old.1.guess.refs_15_ = f32[16,128]{1,0:T(8,128)S(1)} custom-call(f32[10,8,8,128]{3,2,1,0:T(8,128)S(1)} %get-tuple-element.12.own_one, f32[10,8,8,128]{3,2,1,0:T(8,128)S(1)} %get-tuple-element.13.own_two, f32[10,8,8,128]{3,2,1,0:T(8,128)S(1)} %collective-permute-done.inner, f32[10,8,8,128]{3,2,1,0:T(8,128)S(1)} %collective-permute-done.1.outer, ...), custom_call_target="tpu_custom_call" | custom-call | tf_op jit(solution)/shard_map/guess_old/pallas_call | solution.py:399
  28.1 3.5 %collective-permute-done.7.y = f32[8,8,8,128]{3,2,1,0:T(8,128)S(1)} collective-permute-done((f32[8,8,8,128]{3,2,1,0:T(8,128)S(1)}, f32[8,8,8,128]{3,2,1,0:T(8,128)S(1)}, u32[]{:S(2)}, u32[]{:S(2)}) %collective-permute-start.7) | collective-permute-done | bytes 262176 | tf_op jit(solution)/shard_map/ppermute | solution.py:349
  31.6 3.1 %second_round.1 = (f32[16,8,8,128]{3,2,1,0:T(8,128)S(1)}, f32[16,128]{1,0:T(8,128)S(1)}) custom-call(f32[8,8,8,128]{3,2,1,0:T(8,128)S(1)} %get-tuple-element.14.own_one, f32[8,8,8,128]{3,2,1,0:T(8,128)S(1)} %get-tuple-element.15.own_two, f32[8,8,8,128]{3,2,1,0:T(8,128)S(1)} %collective-permute-done.4.inner, ...), custom_call_target="tpu_custom_call" | custom-call | tf_op jit(solution)/shard_map/second_round/pallas_call | solution.py:407
  34.8 5.6 %collective-permute-start.22 = (f32[16,128]{1,0:T(8,128)S(1)}, f32[16,128]{1,0:T(8,128)S(1)}, u32[]{:S(2)}, u32[]{:S(2)}) collective-permute-start(f32[16,128]{1,0:T(8,128)S(1)} %get-tuple-element.17), channel_id=1, source_target_pairs={{0,29},{1,30},{2,31},{3,24},{4,25},{5,26},{6,27},{7,28},{8,5},{9,6... | collective-permute-start | bytes 24584 | tf_op jit(solution)/shard_map/ppermute | solution.py:362
  40.4 2.2 %collective-permute-start.21 = (f32[16,128]{1,0:T(8,128)S(1)}, f32[16,128]{1,0:T(8,128)S(1)}, u32[]{:S(2)}, u32[]{:S(2)}) collective-permute-start(f32[16,128]{1,0:T(8,128)S(1)} %get-tuple-element.17), channel_id=1, source_target_pairs={{0,30},{1,31},{2,24},{3,25},{4,26},{5,27},{6,28},{7,29},{8,6},{9,7... | collective-permute-start | bytes 24584 | tf_op jit(solution)/shard_map/ppermute | solution.py:362
  43.1 2.4 %collective-permute-start.18 = (f32[16,128]{1,0:T(8,128)S(1)}, f32[16,128]{1,0:T(8,128)S(1)}, u32[]{:S(2)}, u32[]{:S(2)}) collective-permute-start(f32[16,128]{1,0:T(8,128)S(1)} %get-tuple-element.17), channel_id=1, source_target_pairs={{0,25},{1,26},{2,27},{3,28},{4,29},{5,30},{6,31},{7,24},{8,1},{9,2... | collective-permute-start | bytes 24584 | tf_op jit(solution)/shard_map/ppermute | solution.py:362
  45.5 2.1 %collective-permute-start.17 = (f32[16,128]{1,0:T(8,128)S(1)}, f32[16,128]{1,0:T(8,128)S(1)}, u32[]{:S(2)}, u32[]{:S(2)}) collective-permute-start(f32[16,128]{1,0:T(8,128)S(1)} %get-tuple-element.17), channel_id=1, source_target_pairs={{0,26},{1,27},{2,28},{3,29},{4,30},{5,31},{6,24},{7,25},{8,2},{9,3... | collective-permute-start | bytes 24584 | tf_op jit(solution)/shard_map/ppermute | solution.py:362
  47.6 2.3 %collective-permute-start.16 = (f32[16,128]{1,0:T(8,128)S(1)}, f32[16,128]{1,0:T(8,128)S(1)}, u32[]{:S(2)}, u32[]{:S(2)}) collective-permute-start(f32[16,128]{1,0:T(8,128)S(1)} %get-tuple-element.17), channel_id=1, source_target_pairs={{0,27},{1,28},{2,29},{3,30},{4,31},{5,24},{6,25},{7,26},{8,3},{9,4... | collective-permute-start | bytes 24584 | tf_op jit(solution)/shard_map/ppermute | solution.py:362
  49.9 4.5 %collective-permute-start.15 = (f32[16,128]{1,0:T(8,128)S(1)}, f32[16,128]{1,0:T(8,128)S(1)}, u32[]{:S(2)}, u32[]{:S(2)}) collective-permute-start(f32[16,128]{1,0:T(8,128)S(1)} %get-tuple-element.17), channel_id=1, source_target_pairs={{0,22},{1,23},{2,16},{3,17},{4,18},{5,19},{6,20},{7,21},{8,30},{9,... | collective-permute-start | bytes 24584 | tf_op jit(solution)/shard_map/ppermute | solution.py:362
  54.8 2.3 %collective-permute-start.12 = (f32[16,128]{1,0:T(8,128)S(1)}, f32[16,128]{1,0:T(8,128)S(1)}, u32[]{:S(2)}, u32[]{:S(2)}) collective-permute-start(f32[16,128]{1,0:T(8,128)S(1)} %get-tuple-element.17), channel_id=1, source_target_pairs={{0,17},{1,18},{2,19},{3,20},{4,21},{5,22},{6,23},{7,16},{8,25},{9,... | collective-permute-start | bytes 24584 | tf_op jit(solution)/shard_map/ppermute | solution.py:362
  57.3 3.0 %collective-permute-start.10 = (f32[16,128]{1,0:T(8,128)S(1)}, f32[16,128]{1,0:T(8,128)S(1)}, u32[]{:S(2)}, u32[]{:S(2)}) collective-permute-start(f32[16,128]{1,0:T(8,128)S(1)} %get-tuple-element.17), channel_id=1, source_target_pairs={{0,15},{1,8},{2,9},{3,10},{4,11},{5,12},{6,13},{7,14},{8,23},{9,16... | collective-permute-start | bytes 24584 | tf_op jit(solution)/shard_map/ppermute | solution.py:362
  60.3 1.7 %collective-permute-start.9 = (f32[16,128]{1,0:T(8,128)S(1)}, f32[16,128]{1,0:T(8,128)S(1)}, u32[]{:S(2)}, u32[]{:S(2)}) collective-permute-start(f32[16,128]{1,0:T(8,128)S(1)} %get-tuple-element.17), channel_id=1, source_target_pairs={{0,8},{1,9},{2,10},{3,11},{4,12},{5,13},{6,14},{7,15},{8,16},{9,17... | collective-permute-start | bytes 24584 | tf_op jit(solution)/shard_map/ppermute | solution.py:362
  62.0 1.5 %collective-permute-done.11.refs_3_ = f32[16,128]{1,0:T(8,128)S(1)} collective-permute-done((f32[16,128]{1,0:T(8,128)S(1)}, f32[16,128]{1,0:T(8,128)S(1)}, u32[]{:S(2)}, u32[]{:S(2)}) %collective-permute-start.11) | collective-permute-done | bytes 8224 | tf_op jit(solution)/shard_map/ppermute | solution.py:362
  63.5 2.3 %collective-permute-done.9.refs_1_ = f32[16,128]{1,0:T(8,128)S(1)} collective-permute-done((f32[16,128]{1,0:T(8,128)S(1)}, f32[16,128]{1,0:T(8,128)S(1)}, u32[]{:S(2)}, u32[]{:S(2)}) %collective-permute-start.9) | collective-permute-done | bytes 8224 | tf_op jit(solution)/shard_map/ppermute | solution.py:362
  65.7 2.9 %collective-permute-done.8.refs_0_ = f32[16,128]{1,0:T(8,128)S(1)} collective-permute-done((f32[16,128]{1,0:T(8,128)S(1)}, f32[16,128]{1,0:T(8,128)S(1)}, u32[]{:S(2)}, u32[]{:S(2)}) %collective-permute-start.8) | collective-permute-done | bytes 8224 | tf_op jit(solution)/shard_map/ppermute | solution.py:362
  68.7 1.8 %correct.1 = f32[1,4,4,64,128]{4,3,2,1,0:T(8,128)} custom-call(f32[16,128]{1,0:T(8,128)S(1)} %collective-permute-done.8.refs_0_, f32[16,128]{1,0:T(8,128)S(1)} %collective-permute-done.9.refs_1_, f32[16,128]{1,0:T(8,128)S(1)} %collective-permute-done.10.refs_2_, f32[16,128]{1,0:T(8,128)S(1)} %collective-permute-done.11.refs_3_, ...), custom_call_target="tpu_custom_call" | custom-call | tf_op jit(solution)/shard_map/correct/pallas_call | solution.py:417
  (33 shorter events, 4.9 us)
Async XLA Ops:
  0.0 1.0 %copy-start = (f32[1,4,4,64,128]{4,3,2,1,0:T(8,128)S(1)}, f32[1,4,4,64,128]{4,3,2,1,0:T(8,128)}, u32[]{:S(2)}) copy-start(f32[1,4,4,64,128]{4,3,2,1,0:T(8,128)} %starts.1) | copy-start | bytes 1572868
  2.3 8.1 %collective-permute-start.2 = (f32[10,8,8,128]{3,2,1,0:T(8,128)S(1)}, f32[10,8,8,128]{3,2,1,0:T(8,128)S(1)}, u32[]{:S(2)}, u32[]{:S(2)}) collective-permute-start(f32[10,8,8,128]{3,2,1,0:T(8,128)S(1)} %get-tuple-element.13.own_two), channel_id=1, source_target_pairs={{0,1},{1,2},{2,3},{3,7},{7,6},{6,5},{5,4},{4,0},{8,9},{9,10},{10,1... | collective-permute-start | bytes 983048 | tf_op jit(solution)/shard_map/ppermute | solution.py:343
  2.8 7.7 %collective-permute-start.1 = (f32[10,8,8,128]{3,2,1,0:T(8,128)S(1)}, f32[10,8,8,128]{3,2,1,0:T(8,128)S(1)}, u32[]{:S(2)}, u32[]{:S(2)}) collective-permute-start(f32[10,8,8,128]{3,2,1,0:T(8,128)S(1)} %get-tuple-element.12.own_one), channel_id=1, source_target_pairs={{0,0},{1,2},{2,1},{3,4},{4,3},{5,6},{6,5},{7,7},{8,8},{9,10},{10,9... | collective-permute-start | bytes 983048 | tf_op jit(solution)/shard_map/ppermute | solution.py:344
  3.5 7.0 %collective-permute-start = (f32[10,8,8,128]{3,2,1,0:T(8,128)S(1)}, f32[10,8,8,128]{3,2,1,0:T(8,128)S(1)}, u32[]{:S(2)}, u32[]{:S(2)}) collective-permute-start(f32[10,8,8,128]{3,2,1,0:T(8,128)S(1)} %get-tuple-element.12.own_one), channel_id=1, source_target_pairs={{0,1},{1,0},{2,3},{3,2},{4,5},{5,4},{6,7},{7,6},{8,9},{9,8},{10,11... | collective-permute-start | bytes 983048 | tf_op jit(solution)/shard_map/ppermute | solution.py:345
  10.4 5.9 %collective-permute-start.3 = (f32[10,8,8,128]{3,2,1,0:T(8,128)S(1)}, f32[10,8,8,128]{3,2,1,0:T(8,128)S(1)}, u32[]{:S(2)}, u32[]{:S(2)}) collective-permute-start(f32[10,8,8,128]{3,2,1,0:T(8,128)S(1)} %broadcast_select_fusion), channel_id=1, source_target_pairs={{3,2},{2,1},{1,0},{0,3},{4,5},{5,6},{6,7},{7,4},{11,10},{10,9},{9,... | collective-permute-start | bytes 983048 | tf_op jit(solution)/shard_map/ppermute | solution.py:349
  19.1 7.0 %collective-permute-start.6 = (f32[8,8,8,128]{3,2,1,0:T(8,128)S(1)}, f32[8,8,8,128]{3,2,1,0:T(8,128)S(1)}, u32[]{:S(2)}, u32[]{:S(2)}) collective-permute-start(f32[8,8,8,128]{3,2,1,0:T(8,128)S(1)} %get-tuple-element.15.own_two), channel_id=1, source_target_pairs={{0,1},{1,2},{2,3},{3,7},{7,6},{6,5},{5,4},{4,0},{8,9},{9,10},{10,1... | collective-permute-start | bytes 786440 | tf_op jit(solution)/shard_map/ppermute | solution.py:343
  22.8 5.3 %collective-permute-start.5 = (f32[8,8,8,128]{3,2,1,0:T(8,128)S(1)}, f32[8,8,8,128]{3,2,1,0:T(8,128)S(1)}, u32[]{:S(2)}, u32[]{:S(2)}) collective-permute-start(f32[8,8,8,128]{3,2,1,0:T(8,128)S(1)} %get-tuple-element.14.own_one), channel_id=1, source_target_pairs={{0,0},{1,2},{2,1},{3,4},{4,3},{5,6},{6,5},{7,7},{8,8},{9,10},{10,9... | collective-permute-start | bytes 786440 | tf_op jit(solution)/shard_map/ppermute | solution.py:344
  23.5 4.6 %collective-permute-start.4 = (f32[8,8,8,128]{3,2,1,0:T(8,128)S(1)}, f32[8,8,8,128]{3,2,1,0:T(8,128)S(1)}, u32[]{:S(2)}, u32[]{:S(2)}) collective-permute-start(f32[8,8,8,128]{3,2,1,0:T(8,128)S(1)} %get-tuple-element.14.own_one), channel_id=1, source_target_pairs={{0,1},{1,0},{2,3},{3,2},{4,5},{5,4},{6,7},{7,6},{8,9},{9,8},{10,11... | collective-permute-start | bytes 786440 | tf_op jit(solution)/shard_map/ppermute | solution.py:345
  26.1 5.6 %collective-permute-start.7 = (f32[8,8,8,128]{3,2,1,0:T(8,128)S(1)}, f32[8,8,8,128]{3,2,1,0:T(8,128)S(1)}, u32[]{:S(2)}, u32[]{:S(2)}) collective-permute-start(f32[8,8,8,128]{3,2,1,0:T(8,128)S(1)} %broadcast_select_fusion.1), channel_id=1, source_target_pairs={{3,2},{2,1},{1,0},{0,3},{4,5},{5,6},{6,7},{7,4},{11,10},{10,9},{9,... | collective-permute-start | bytes 786440 | tf_op jit(solution)/shard_map/ppermute | solution.py:349
  34.8 10.7 %collective-permute-start.22 = (f32[16,128]{1,0:T(8,128)S(1)}, f32[16,128]{1,0:T(8,128)S(1)}, u32[]{:S(2)}, u32[]{:S(2)}) collective-permute-start(f32[16,128]{1,0:T(8,128)S(1)} %get-tuple-element.17), channel_id=1, source_target_pairs={{0,29},{1,30},{2,31},{3,24},{4,25},{5,26},{6,27},{7,28},{8,5},{9,6... | collective-permute-start | bytes 24584 | tf_op jit(solution)/shard_map/ppermute | solution.py:362
  40.4 7.2 %collective-permute-start.21 = (f32[16,128]{1,0:T(8,128)S(1)}, f32[16,128]{1,0:T(8,128)S(1)}, u32[]{:S(2)}, u32[]{:S(2)}) collective-permute-start(f32[16,128]{1,0:T(8,128)S(1)} %get-tuple-element.17), channel_id=1, source_target_pairs={{0,30},{1,31},{2,24},{3,25},{4,26},{5,27},{6,28},{7,29},{8,6},{9,7... | collective-permute-start | bytes 24584 | tf_op jit(solution)/shard_map/ppermute | solution.py:362
  42.6 7.3 %collective-permute-start.20 = (f32[16,128]{1,0:T(8,128)S(1)}, f32[16,128]{1,0:T(8,128)S(1)}, u32[]{:S(2)}, u32[]{:S(2)}) collective-permute-start(f32[16,128]{1,0:T(8,128)S(1)} %get-tuple-element.17), channel_id=1, source_target_pairs={{0,31},{1,24},{2,25},{3,26},{4,27},{5,28},{6,29},{7,30},{8,7},{9,0... | collective-permute-start | bytes 24584 | tf_op jit(solution)/shard_map/ppermute | solution.py:362
  42.6 11.8 %collective-permute-start.19 = (f32[16,128]{1,0:T(8,128)S(1)}, f32[16,128]{1,0:T(8,128)S(1)}, u32[]{:S(2)}, u32[]{:S(2)}) collective-permute-start(f32[16,128]{1,0:T(8,128)S(1)} %get-tuple-element.17), channel_id=1, source_target_pairs={{0,24},{1,25},{2,26},{3,27},{4,28},{5,29},{6,30},{7,31},{8,0},{9,1... | collective-permute-start | bytes 24584 | tf_op jit(solution)/shard_map/ppermute | solution.py:362
  43.1 11.3 %collective-permute-start.18 = (f32[16,128]{1,0:T(8,128)S(1)}, f32[16,128]{1,0:T(8,128)S(1)}, u32[]{:S(2)}, u32[]{:S(2)}) collective-permute-start(f32[16,128]{1,0:T(8,128)S(1)} %get-tuple-element.17), channel_id=1, source_target_pairs={{0,25},{1,26},{2,27},{3,28},{4,29},{5,30},{6,31},{7,24},{8,1},{9,2... | collective-permute-start | bytes 24584 | tf_op jit(solution)/shard_map/ppermute | solution.py:362
  45.5 9.3 %collective-permute-start.17 = (f32[16,128]{1,0:T(8,128)S(1)}, f32[16,128]{1,0:T(8,128)S(1)}, u32[]{:S(2)}, u32[]{:S(2)}) collective-permute-start(f32[16,128]{1,0:T(8,128)S(1)} %get-tuple-element.17), channel_id=1, source_target_pairs={{0,26},{1,27},{2,28},{3,29},{4,30},{5,31},{6,24},{7,25},{8,2},{9,3... | collective-permute-start | bytes 24584 | tf_op jit(solution)/shard_map/ppermute | solution.py:362
  47.6 9.5 %collective-permute-start.16 = (f32[16,128]{1,0:T(8,128)S(1)}, f32[16,128]{1,0:T(8,128)S(1)}, u32[]{:S(2)}, u32[]{:S(2)}) collective-permute-start(f32[16,128]{1,0:T(8,128)S(1)} %get-tuple-element.17), channel_id=1, source_target_pairs={{0,27},{1,28},{2,29},{3,30},{4,31},{5,24},{6,25},{7,26},{8,3},{9,4... | collective-permute-start | bytes 24584 | tf_op jit(solution)/shard_map/ppermute | solution.py:362
  49.9 7.4 %collective-permute-start.15 = (f32[16,128]{1,0:T(8,128)S(1)}, f32[16,128]{1,0:T(8,128)S(1)}, u32[]{:S(2)}, u32[]{:S(2)}) collective-permute-start(f32[16,128]{1,0:T(8,128)S(1)} %get-tuple-element.17), channel_id=1, source_target_pairs={{0,22},{1,23},{2,16},{3,17},{4,18},{5,19},{6,20},{7,21},{8,30},{9,... | collective-permute-start | bytes 24584 | tf_op jit(solution)/shard_map/ppermute | solution.py:362
  54.4 5.9 %collective-permute-start.14 = (f32[16,128]{1,0:T(8,128)S(1)}, f32[16,128]{1,0:T(8,128)S(1)}, u32[]{:S(2)}, u32[]{:S(2)}) collective-permute-start(f32[16,128]{1,0:T(8,128)S(1)} %get-tuple-element.17), channel_id=1, source_target_pairs={{0,23},{1,16},{2,17},{3,18},{4,19},{5,20},{6,21},{7,22},{8,31},{9,... | collective-permute-start | bytes 24584 | tf_op jit(solution)/shard_map/ppermute | solution.py:362
  54.4 7.6 %collective-permute-start.13 = (f32[16,128]{1,0:T(8,128)S(1)}, f32[16,128]{1,0:T(8,128)S(1)}, u32[]{:S(2)}, u32[]{:S(2)}) collective-permute-start(f32[16,128]{1,0:T(8,128)S(1)} %get-tuple-element.17), channel_id=1, source_target_pairs={{0,16},{1,17},{2,18},{3,19},{4,20},{5,21},{6,22},{7,23},{8,24},{9,... | collective-permute-start | bytes 24584 | tf_op jit(solution)/shard_map/ppermute | solution.py:362
  54.8 7.2 %collective-permute-start.12 = (f32[16,128]{1,0:T(8,128)S(1)}, f32[16,128]{1,0:T(8,128)S(1)}, u32[]{:S(2)}, u32[]{:S(2)}) collective-permute-start(f32[16,128]{1,0:T(8,128)S(1)} %get-tuple-element.17), channel_id=1, source_target_pairs={{0,17},{1,18},{2,19},{3,20},{4,21},{5,22},{6,23},{7,16},{8,25},{9,... | collective-permute-start | bytes 24584 | tf_op jit(solution)/shard_map/ppermute | solution.py:362
  57.1 6.3 %collective-permute-start.11 = (f32[16,128]{1,0:T(8,128)S(1)}, f32[16,128]{1,0:T(8,128)S(1)}, u32[]{:S(2)}, u32[]{:S(2)}) collective-permute-start(f32[16,128]{1,0:T(8,128)S(1)} %get-tuple-element.17), channel_id=1, source_target_pairs={{0,18},{1,19},{2,20},{3,21},{4,22},{5,23},{6,16},{7,17},{8,26},{9,... | collective-permute-start | bytes 24584 | tf_op jit(solution)/shard_map/ppermute | solution.py:362
  57.3 6.2 %collective-permute-start.10 = (f32[16,128]{1,0:T(8,128)S(1)}, f32[16,128]{1,0:T(8,128)S(1)}, u32[]{:S(2)}, u32[]{:S(2)}) collective-permute-start(f32[16,128]{1,0:T(8,128)S(1)} %get-tuple-element.17), channel_id=1, source_target_pairs={{0,15},{1,8},{2,9},{3,10},{4,11},{5,12},{6,13},{7,14},{8,23},{9,16... | collective-permute-start | bytes 24584 | tf_op jit(solution)/shard_map/ppermute | solution.py:362
  60.3 5.4 %collective-permute-start.9 = (f32[16,128]{1,0:T(8,128)S(1)}, f32[16,128]{1,0:T(8,128)S(1)}, u32[]{:S(2)}, u32[]{:S(2)}) collective-permute-start(f32[16,128]{1,0:T(8,128)S(1)} %get-tuple-element.17), channel_id=1, source_target_pairs={{0,8},{1,9},{2,10},{3,11},{4,12},{5,13},{6,14},{7,15},{8,16},{9,17... | collective-permute-start | bytes 24584 | tf_op jit(solution)/shard_map/ppermute | solution.py:362
  62.0 6.7 %collective-permute-start.8 = (f32[16,128]{1,0:T(8,128)S(1)}, f32[16,128]{1,0:T(8,128)S(1)}, u32[]{:S(2)}, u32[]{:S(2)}) collective-permute-start(f32[16,128]{1,0:T(8,128)S(1)} %get-tuple-element.17), channel_id=1, source_target_pairs={{0,9},{1,10},{2,11},{3,12},{4,13},{5,14},{6,15},{7,8},{8,17},{9,18... | collective-permute-start | bytes 24584 | tf_op jit(solution)/shard_map/ppermute | solution.py:362
  (1 other events, 0.9 us)

commit v7 on v6

--- a/solution.py
+++ b/solution.py
@@ -36,22 +36,27 @@
     return pltpu.CompilerParams(vmem_limit_bytes=LIMIT)
 
 
-def prepare_kernel(starts, flags, message_one, message_two, fields, kinds, sems):
+def prepare_kernel(starts, flags, whole, message_one, message_two, fields, kinds, sems):
     copies = [pltpu.make_async_copy(starts, fields, sems.at[0]), pltpu.make_async_copy(flags, kinds, sems.at[1])]
     for copy in copies:
         copy.start()
     for copy in copies:
         copy.wait()
+    messages = (message_one, message_two)
     for f in range(FIELDS):
-        message = message_one if f < 2 else message_two
         for x in range(PLANES):
             for t in range(TILES):
                 v = fields[0, f, x, pl.ds(t, 8, stride=8), :]
-                message[f % 2 * PLANES + x, t] = v * 0.5 if f == 0 else v
+                put_row(whole, messages, f // 2, f % 2 * PLANES + x, t, v * 0.5 if f == 0 else v)
     for x in range(PLANES):
-        message = message_one if x < 2 else message_two
         for t in range(TILES):
-            message[2 * PLANES + x % 2, t] = kinds[x, pl.ds(t, 8, stride=8), :].astype(F32)
+            v = kinds[x, pl.ds(t, 8, stride=8), :].astype(F32)
+            put_row(whole, messages, x // 2, 2 * PLANES + x % 2, t, v)
+
+
+def put_row(whole, messages, half, k, t, value):
+    whole[half * messages[0].shape[0] + k, t] = value
+    messages[half][k, t] = value
 
 
 def fine_tile(mid, lo_x, hi_x, lo_y, hi_y, kv, ks, kc, low_lane, high_lane):
@@ -104,19 +109,23 @@
 
 class Slabs:
 
-    def __init__(self, space_size, own, near):
+    def __init__(self, space_size, whole, inner, outer_one, outer_two, outer_relayed):
         place = lax.axis_index("space")
-        self.own = own
-        self.near = (near[:2], near[2:])
-        self.from_first = (place % 2 == 1, place < turn(space_size))
+        self.whole, self.inner, self.outer = whole, inner, (outer_one, outer_two)
+        self.rows = whole.shape[0] // 2
+        self.relayed = outer_relayed
+        self.odd = place % 2 == 1
+        self.by_relay = (place == space_size // 2 - 1) | (place == space_size // 2)
         self.there = {0: place > 0, 2: place < space_size - 1}
 
     def row(self, j, half, k, t):
         if j == 1:
-            return self.own[half][k, t]
-        v, other = (ref[k, t] for ref in self.near[half])
-        first = self.from_first[half]
-        v = jnp.where(first, v, other) if j == 0 else jnp.where(first, other, v)
+            return self.whole[half * self.rows + k, t]
+        inner = self.inner[half * self.rows + k, t]
+        outer = self.outer[half][k, t]
+        if half == 1:
+            outer = jnp.where(self.by_relay, self.relayed[k, t], outer)
+        v = jnp.where(self.odd, inner, outer) if j == 0 else jnp.where(self.odd, outer, inner)
         return jnp.where(self.there[j], v, 0.0)
 
     def field(self, j, f, x, t):
@@ -155,8 +164,8 @@
         lax.fori_loop(0, 2, body, 0)
 
 
-def first_kernel(space_size, own_one, own_two, inner, outer, x, y, ended_one, ended_two, keep, even, odd):
-    slabs = Slabs(space_size, (own_one, own_two), (inner, outer, x, y))
+def first_kernel(space_size, own, inner, outer_one, outer_two, relayed, ended, ended_one, ended_two, keep, even, odd):
+    slabs = Slabs(space_size, own, inner, outer_one, outer_two, relayed)
     for j in range(3):
         for k in range(PLANES):
             p = j * PLANES + k
@@ -167,8 +176,7 @@
                 keep[1, p, t] = jnp.where(kind != 2.0, scale, 0.0)
 
     def finish(f, x, t, value):
-        ended = ended_one if f < 2 else ended_two
-        ended[f % 2 * PLANES + x, t] = value
+        put_row(ended, (ended_one, ended_two), f // 2, f % 2 * PLANES + x, t, value)
 
     fine_round(space_size, slabs, even, odd, keep, finish)
 
@@ -239,9 +247,9 @@
     return new_w, new_a, new_b, new_c
 
 
-def guess_kernel(space_size, own_one, own_two, inner, outer, x, y, guess):
+def guess_kernel(space_size, own, inner, outer_one, outer_two, relayed, guess):
     place = lax.axis_index("space")
-    slabs = Slabs(space_size, (own_one, own_two), (inner, outer, x, y))
+    slabs = Slabs(space_size, own, inner, outer_one, outer_two, relayed)
     rows = 16
     row = iota((rows, NZ), 0)
     plane = 2 * place - 2 + row // 2
@@ -260,8 +268,8 @@
         guess[pl.ds(4 * f, 4), :] = state[f][4:8]
 
 
-def second_kernel(space_size, own_one, own_two, inner, outer, x, y, keep, guess, fine_end, jump, even, odd):
-    slabs = Slabs(space_size, (own_one, own_two), (inner, outer, x, y))
+def second_kernel(space_size, own, inner, outer_one, outer_two, relayed, keep, guess, fine_end, jump, even, odd):
+    slabs = Slabs(space_size, own, inner, outer_one, outer_two, relayed)
 
     def finish(f, x, t, value):
         fine_end[f * PLANES + x, t] = value * 2.0 if f == 0 else value
@@ -269,11 +277,12 @@
     fine_round(space_size, slabs, even, odd, keep, finish)
     ended = halves(coarse_rows(lambda k, t: fine_end[2 * k, t] + fine_end[2 * k + 1, t], PACKED), PACKED)
     jumped = ended - jnp.where(lax.axis_index("tm") == 0, 0.0, guess[...])
-    jump[...] = jumped
-
-
-def correct_kernel(slices, space_size, *refs):
-    jumps, (guess, fine_end, out, grids) = refs[:-4], refs[-4:]
+    for k in range(jump.shape[0]):
+        jump[k] = jumped
+
+
+def correct_kernel(jumps, guess, fine_end, out, grids):
+    slices, space_size = jumps.shape[:2]
     mine = lax.axis_index("tm")
     place = lax.axis_index("space")
     rows = grids.shape[2]
@@ -281,12 +290,12 @@
     plane = 2 * (place - slices) + iota((rows, NZ), 0) // 2
     valid = (plane >= 0) & (plane < 2 * space_size)
     grids[...] = jnp.zeros_like(grids)
-    at = 0
     for k in range(1, slices):
+        m = jnp.maximum(mine - k, 0)
         for j in range(-k, k + 1):
+            s = jnp.clip(place + j, 0, space_size - 1)
             for f in range(FIELDS):
-                grids[k - 1, f, pl.ds(centre + 4 * j, 4), :] = jumps[at][pl.ds(4 * f, 4), :]
-            at += 1
+                grids[k - 1, f, pl.ds(centre + 4 * j, 4), :] = jumps[m, s, pl.ds(4 * f, 4), :]
     state = None
     for k in range(slices - 1, -1, -1):
         ended = state
@@ -320,47 +329,22 @@
                 out[0, f, x, pl.ds(t, 8, stride=8), :] = fine_end[f * PLANES + x, t] + wide[k : k + 8]
 
 
-def relayed(size):
-    return size == 8
-
-
-def turn(size):
-    return size // 2 if relayed(size) else size
-
-
-def exchange(one, two, size):
-    inner = [(i, i ^ 1) for i in range(size)]
-    outer = [(0, 0)] + [(i, (i - 1 ^ 1) + 1) for i in range(1, size - 1)] + [(size - 1, size - 1)]
-    if relayed(size):
-        half = size // 2
-        first = [(i, i + 1) for i in range(half - 1)] + [(half - 1, size - 1)]
-        first += [(i, i - 1) for i in range(size - 1, half, -1)] + [(half, 0)]
-        second = [(i, i - 1) for i in range(half - 1, 0, -1)] + [(0, half - 1)]
-        second += [(i, i + 1) for i in range(half, size - 1)] + [(size - 1, half)]
-    else:
-        first = [(i, (i + 1) % size) for i in range(size)]
-        second = [(i, (i - 1) % size) for i in range(size)]
-    x = lax.ppermute(two, "space", first)
-    across = lax.ppermute(one, "space", outer)
-    within = lax.ppermute(one, "space", inner)
-    if relayed(size):
-        place = lax.axis_index("space")
-        two = jnp.where((place == 0) | (place == size - 1), x, two)
-    y = lax.ppermute(two, "space", second)
-    return within, across, x, y
-
-
-def earlier_jumps(jump, slices, space_size):
-    found = []
-    for k in range(1, slices):
-        for j in range(-k, k + 1):
-            route = []
-            for m in range(slices):
-                for s in range(space_size):
-                    target = (m + k) % slices * space_size + (s - j) % space_size
-                    route.append((m * space_size + s, target))
-            found.append(lax.ppermute(jump, ("tm", "space"), route))
-    return found
+def exchange(whole, one, two, size):
+    ends = [(0, 0), (size - 1, size - 1)]
+    across = [(i, (i - 1 ^ 1) + 1) for i in range(1, size - 1)]
+    within = [(i, i ^ 1) for i in range(size)]
+    if size != 8:
+        outer_two = lax.ppermute(two, "space", across + ends)
+        outer_one = lax.ppermute(one, "space", across + ends)
+        inner = lax.ppermute(whole, "space", within)
+        return inner, outer_one, outer_two, outer_two
+    straight = [pair for pair in across if pair[0] not in (3, 4)]
+    outer_two = lax.ppermute(two, "space", straight + [(3, 7), (7, 3), (4, 0), (0, 4)])
+    outer_one = lax.ppermute(one, "space", across + ends)
+    inner = lax.ppermute(whole, "space", within)
+    stay = [(source, source) for source, target in straight]
+    relayed = lax.ppermute(outer_two, "space", stay + [(7, 4), (0, 3), (3, 7), (4, 0)])
+    return inner, outer_one, outer_two, relayed
 
 
 def shaped(*shape):
@@ -374,9 +358,9 @@
     buffers = [pltpu.VMEM((FIELDS, WINDOW, TILES + 2, 8, NZ), F32)] * 2
     opening = pl.pallas_call(
         prepare_kernel,
-        out_shape=(message, message),
+        out_shape=(shaped(PACKED + PLANES, TILES, 8, NZ), message, message),
         in_specs=[pl.BlockSpec(memory_space=pltpu.HBM)] * 2,
-        out_specs=(VMEM, VMEM),
+        out_specs=(VMEM,) * 3,
         scratch_shapes=[
             pltpu.VMEM(starts.shape, F32),
             pltpu.VMEM(flags.shape, flags.dtype),
@@ -388,41 +372,42 @@
     opening_near = exchange(*opening, space_size)
     *middle, keep = pl.pallas_call(
         functools.partial(first_kernel, space_size),
-        out_shape=(half, half, keep_shape),
-        in_specs=[VMEM] * 6,
-        out_specs=(VMEM,) * 3,
+        out_shape=(shaped(PACKED, TILES, 8, NZ), half, half, keep_shape),
+        in_specs=[VMEM] * 5,
+        out_specs=(VMEM,) * 4,
         scratch_shapes=buffers,
         compiler_params=params(),
         name="first_round",
-    )(*opening, *opening_near)
+    )(opening[0], *opening_near)
     middle_near = exchange(*middle, space_size)
     guess = pl.pallas_call(
         functools.partial(guess_kernel, space_size),
         out_shape=shaped(PACKED, NZ),
-        in_specs=[VMEM] * 6,
+        in_specs=[VMEM] * 5,
         out_specs=VMEM,
         compiler_params=params(),
         name="guess_old",
-    )(*opening, *opening_near)
+    )(opening[0], *opening_near)
     fine_end, jump = pl.pallas_call(
         functools.partial(second_kernel, space_size),
-        out_shape=(shaped(PACKED, TILES, 8, NZ), shaped(PACKED, NZ)),
-        in_specs=[VMEM] * 8,
+        out_shape=(shaped(PACKED, TILES, 8, NZ), shaped(slices * space_size, PACKED, NZ)),
+        in_specs=[VMEM] * 7,
         out_specs=(VMEM, VMEM),
         scratch_shapes=buffers,
         compiler_params=params(),
         name="second_round",
-    )(*middle, *middle_near, keep, guess)
-    jumps = earlier_jumps(jump, slices, space_size)
+    )(middle[0], *middle_near, keep, guess)
+    jumps = lax.all_to_all(jump, ("tm", "space"), 0, 0)
+    jumps = jumps.reshape(slices, space_size, PACKED, NZ)
     return pl.pallas_call(
-        functools.partial(correct_kernel, slices, space_size),
+        correct_kernel,
         out_shape=shaped(1, FIELDS, PLANES, NY, NZ),
-        in_specs=[VMEM] * (len(jumps) + 2),
+        in_specs=[VMEM] * 3,
         out_specs=VMEM,
         scratch_shapes=[pltpu.VMEM((slices - 1, FIELDS, 8 * slices, NZ), F32)],
         compiler_params=params(),
         name="correct",
-    )(*jumps, guess, fine_end)
+    )(jumps, guess, fine_end)
 
 
 def solution(mesh):

time: 70.7 us -> 57 us (0.81)
  starting transfers between devices: 38.7 us -> 10.3 us
  blocking collectives: 0 us -> 14.9 us
    ppermute x23 -> x8, starting transfers between devices: 38.7 us -> 10.3 us  [the longest x2 4.54 us: exchange(): lax.ppermute(two, 'space', straight + [(3, 7), (7, 3), (4, 0), (0, 4)])]
    all_to_all x0 -> x1, blocking collectives: none -> 14.9 us  [local(): jumps = lax.all_to_all(jump, ('tm', 'space'), 0, 0)]
    ppermute x23 -> x8, waiting for transfers between devices: 20.3 us -> 19.9 us  [the longest x2 11.3 us: exchange(): lax.ppermute(outer_two, 'space', stay + [(7, 4), (0, 3), (3, 7), (4, 0)])]
  transfers between devices with their start and end apart: 23 -> 8, of which waited for: 7 -> 4; matrix products, arithmetic and copies ran while one was open for 0% -> 0% of each run, Pallas kernels for 2% -> 3%
where the time goes in v7:
time: 57 us; the launch traced here: 56.7 us
  waiting for transfers between devices  19.9 us (35%)
  blocking collectives  14.9 us (26%)
  starting transfers between devices  10.3 us (18%)
  Pallas kernels  9.59 us (17%)
  local copies, waits for them, and re-layouts  1.94 us (3%)
    all_to_all x1, blocking collectives, local(): jumps = lax.all_to_all(jump, ('tm', 'space'), 0, 0)  14.9 us
    ppermute x2, waiting for transfers between devices, exchange(): lax.ppermute(outer_two, 'space', stay + [(7, 4), (0, 3), (3, 7), (4, 0)])  11.3 us
    ppermute x2, waiting for transfers between devices, exchange(): lax.ppermute(two, 'space', straight + [(3, 7), (7, 3), (4, 0), (0, 4)])  8.55 us
    ppermute x2, starting transfers between devices, exchange(): lax.ppermute(two, 'space', straight + [(3, 7), (7, 3), (4, 0), (0, 4)])  4.54 us
    ppermute x2, starting transfers between devices, exchange(): lax.ppermute(outer_two, 'space', stay + [(7, 4), (0, 3), (3, 7), (4, 0)])  4.38 us
    pallas_call x1, Pallas kernels, local(): pl.pallas_call(functools.partial(second_kernel, space_size), out_shape=(s...  3.16 us
    pallas_call x1, Pallas kernels, local(): pl.pallas_call(functools.partial(first_kernel, space_size), out_shape=(sh...  2.76 us
    unnamed x4, local copies, waits for them, and re-layouts  1.94 us
  transfers between devices with their start and end apart: 8, of which 4 were waited for; matrix products, arithmetic and copies ran while one was open for 0% of the time, Pallas kernels for 3%

profile of v7, /device:TPU:0, one launch (start us, length us, event | category | flops | bytes accessed | tf_op | source)
XLA Modules:
  0.0 56.7 jit_solution(6389573783446697080)
XLA Ops:
  0.0 1.0 %copy-done = f32[1,4,4,64,128]{4,3,2,1,0:T(8,128)S(1)} copy-done((f32[1,4,4,64,128]{4,3,2,1,0:T(8,128)S(1)}, f32[1,4,4,64,128]{4,3,2,1,0:T(8,128)}, u32[]{:S(2)}) %copy-start) | copy-done | bytes 524312
  1.0 0.9 %copy-done.1 = s32[4,64,128]{2,1,0:T(8,128)S(1)} copy-done((s32[4,64,128]{2,1,0:T(8,128)S(1)}, s32[4,64,128]{2,1,0:T(8,128)}, u32[]{:S(2)}) %copy-start.1) | copy-done | bytes 131096
  1.9 0.4 prepare.1
  2.3 3.0 %collective-permute-start.2 = (f32[10,8,8,128]{3,2,1,0:T(8,128)S(1)}, f32[10,8,8,128]{3,2,1,0:T(8,128)S(1)}, u32[]{:S(2)}, u32[]{:S(2)}) collective-permute-start(f32[10,8,8,128]{3,2,1,0:T(8,128)S(1)} %get-tuple-element.16), channel_id=1, source_target_pairs={{1,2},{2,1},{5,6},{6,5},{3,7},{7,3},{4,0},{0,4},{9,10},{10,9},{13,... | collective-permute-start | bytes 983048 | tf_op jit(solution)/shard_map/ppermute | solution.py:342
  5.3 0.1 collective-permute-start
  5.4 0.7 %collective-permute-start.1 = (f32[10,8,8,128]{3,2,1,0:T(8,128)S(1)}, f32[10,8,8,128]{3,2,1,0:T(8,128)S(1)}, u32[]{:S(2)}, u32[]{:S(2)}) collective-permute-start(f32[10,8,8,128]{3,2,1,0:T(8,128)S(1)} %get-tuple-element.15), channel_id=1, source_target_pairs={{1,2},{2,1},{3,4},{4,3},{5,6},{6,5},{0,0},{7,7},{9,10},{10,9},{11,... | collective-permute-start | bytes 983048 | tf_op jit(solution)/shard_map/ppermute | solution.py:343
  6.1 4.3 %collective-permute-done.2.outer_two = f32[10,8,8,128]{3,2,1,0:T(8,128)S(1)} collective-permute-done((f32[10,8,8,128]{3,2,1,0:T(8,128)S(1)}, f32[10,8,8,128]{3,2,1,0:T(8,128)S(1)}, u32[]{:S(2)}, u32[]{:S(2)}) %collective-permute-start.2) | collective-permute-done | bytes 327712 | tf_op jit(solution)/shard_map/ppermute | solution.py:342
  10.4 2.5 %collective-permute-start.3 = (f32[10,8,8,128]{3,2,1,0:T(8,128)S(1)}, f32[10,8,8,128]{3,2,1,0:T(8,128)S(1)}, u32[]{:S(2)}, u32[]{:S(2)}) collective-permute-start(f32[10,8,8,128]{3,2,1,0:T(8,128)S(1)} %collective-permute-done.2.outer_two), channel_id=1, source_target_pairs={{1,1},{2,2},{5,5},{6,6},{7,4},{0,3},{3,7},{4,0},{9,9},{10,10},{13,... | collective-permute-start | bytes 983048 | tf_op jit(solution)/shard_map/ppermute | solution.py:346
  12.9 0.0 collective-permute-done.1.outer_one
  12.9 6.5 %collective-permute-done.3.relayed = f32[10,8,8,128]{3,2,1,0:T(8,128)S(1)} collective-permute-done((f32[10,8,8,128]{3,2,1,0:T(8,128)S(1)}, f32[10,8,8,128]{3,2,1,0:T(8,128)S(1)}, u32[]{:S(2)}, u32[]{:S(2)}) %collective-permute-start.3) | collective-permute-done | bytes 327712 | tf_op jit(solution)/shard_map/ppermute | solution.py:346
  19.4 0.0 collective-permute-done.inner
  19.4 2.8 %first_round.1 = (f32[16,8,8,128]{3,2,1,0:T(8,128)S(1)}, f32[8,8,8,128]{3,2,1,0:T(8,128)S(1)}, f32[8,8,8,128]{3,2,1,0:T(8,128)S(1)}, f32[2,12,8,8,128]{4,3,2,1,0:T(8,128)S(1)}) custom-call(f32[20,8,8,128]{3,2,1,0:T(8,128)S(1)} %get-tuple-element.14.own, f32[20,8,8,128]{3,2,1,0:T(8,128)S(1)} %collective-permute-done.inner, ...), custom_call_target="tpu_custom_call" | custom-call | tf_op jit(solution)/shard_map/first_round/pallas_call | solution.py:373
  22.1 1.5 %collective-permute-start.6 = (f32[8,8,8,128]{3,2,1,0:T(8,128)S(1)}, f32[8,8,8,128]{3,2,1,0:T(8,128)S(1)}, u32[]{:S(2)}, u32[]{:S(2)}) collective-permute-start(f32[8,8,8,128]{3,2,1,0:T(8,128)S(1)} %get-tuple-element.19), channel_id=1, source_target_pairs={{1,2},{2,1},{5,6},{6,5},{3,7},{7,3},{4,0},{0,4},{9,10},{10,9},{13,... | collective-permute-start | bytes 786440 | tf_op jit(solution)/shard_map/ppermute | solution.py:342
  23.6 0.0 collective-permute-start.4
  23.6 0.7 %collective-permute-start.5 = (f32[8,8,8,128]{3,2,1,0:T(8,128)S(1)}, f32[8,8,8,128]{3,2,1,0:T(8,128)S(1)}, u32[]{:S(2)}, u32[]{:S(2)}) collective-permute-start(f32[8,8,8,128]{3,2,1,0:T(8,128)S(1)} %get-tuple-element.18), channel_id=1, source_target_pairs={{1,2},{2,1},{3,4},{4,3},{5,6},{6,5},{0,0},{7,7},{9,10},{10,9},{11,... | collective-permute-start | bytes 786440 | tf_op jit(solution)/shard_map/ppermute | solution.py:343
  24.3 4.3 %collective-permute-done.6.outer_two = f32[8,8,8,128]{3,2,1,0:T(8,128)S(1)} collective-permute-done((f32[8,8,8,128]{3,2,1,0:T(8,128)S(1)}, f32[8,8,8,128]{3,2,1,0:T(8,128)S(1)}, u32[]{:S(2)}, u32[]{:S(2)}) %collective-permute-start.6) | collective-permute-done | bytes 262176 | tf_op jit(solution)/shard_map/ppermute | solution.py:342
  28.6 1.9 %collective-permute-start.7 = (f32[8,8,8,128]{3,2,1,0:T(8,128)S(1)}, f32[8,8,8,128]{3,2,1,0:T(8,128)S(1)}, u32[]{:S(2)}, u32[]{:S(2)}) collective-permute-start(f32[8,8,8,128]{3,2,1,0:T(8,128)S(1)} %collective-permute-done.6.outer_two), channel_id=1, source_target_pairs={{1,1},{2,2},{5,5},{6,6},{7,4},{0,3},{3,7},{4,0},{9,9},{10,10},{13,... | collective-permute-start | bytes 786440 | tf_op jit(solution)/shard_map/ppermute | solution.py:346
  30.5 1.5 %guess_old.1.guess = f32[16,128]{1,0:T(8,128)S(1)} custom-call(f32[20,8,8,128]{3,2,1,0:T(8,128)S(1)} %get-tuple-element.14.own, f32[20,8,8,128]{3,2,1,0:T(8,128)S(1)} %collective-permute-done.inner, f32[10,8,8,128]{3,2,1,0:T(8,128)S(1)} %collective-permute-done.1.outer_one, f32[10,8,8,128]{3,2,1,0:T(8,128)S(1)} %collective-permute-done.2.outer_two, ...), custom_call_target="tpu_custom_call" | custom-call | tf_op jit(solution)/shard_map/guess_old/pallas_call | solution.py:383
  31.9 0.0 collective-permute-done.5.outer_one
  31.9 0.0 collective-permute-done.4.inner
  32.0 4.9 %collective-permute-done.7.relayed = f32[8,8,8,128]{3,2,1,0:T(8,128)S(1)} collective-permute-done((f32[8,8,8,128]{3,2,1,0:T(8,128)S(1)}, f32[8,8,8,128]{3,2,1,0:T(8,128)S(1)}, u32[]{:S(2)}, u32[]{:S(2)}) %collective-permute-start.7) | collective-permute-done | bytes 262176 | tf_op jit(solution)/shard_map/ppermute | solution.py:346
  36.8 3.2 %second_round.1 = (f32[16,8,8,128]{3,2,1,0:T(8,128)S(1)}, f32[32,16,128]{2,1,0:T(8,128)S(1)}) custom-call(f32[16,8,8,128]{3,2,1,0:T(8,128)S(1)} %get-tuple-element.17.own, f32[16,8,8,128]{3,2,1,0:T(8,128)S(1)} %collective-permute-done.4.inner, f32[8,8,8,128]{3,2,1,0:T(8,128)S(1)} %collective-permute-done.5.outer_one, ...), custom_call_target="tpu_custom_call" | custom-call | tf_op jit(solution)/shard_map/second_round/pallas_call | solution.py:391
  40.0 14.9 %all_to_all.5 = f32[32,16,128]{2,1,0:T(8,128)S(1)} all-to-all(f32[32,16,128]{2,1,0:T(8,128)S(1)} %get-tuple-element.21), channel_id=1, replica_groups=mesh['tm'=4,'space'=8] {'tm','space'}, dimensions={0} | all-to-all | bytes 524288 | tf_op jit(solution)/shard_map/all_to_all | solution.py:400
  54.8 1.9 %correct.1 = f32[1,4,4,64,128]{4,3,2,1,0:T(8,128)} custom-call(f32[4,8,16,128]{3,2,1,0:T(8,128)S(1)} %bitcast.1, f32[16,128]{1,0:T(8,128)S(1)} %guess_old.1.guess, f32[16,8,8,128]{3,2,1,0:T(8,128)S(1)} %get-tuple-element.22.fine_end), custom_call_target="tpu_custom_call" | custom-call | tf_op jit(solution)/shard_map/correct/pallas_call | solution.py:402
  (2 shorter events, 0.0 us)
Async XLA Ops:
  0.0 1.0 %copy-start = (f32[1,4,4,64,128]{4,3,2,1,0:T(8,128)S(1)}, f32[1,4,4,64,128]{4,3,2,1,0:T(8,128)}, u32[]{:S(2)}) copy-start(f32[1,4,4,64,128]{4,3,2,1,0:T(8,128)} %starts.1) | copy-start | bytes 1572868
  1.0 0.9 %copy-start.1 = (s32[4,64,128]{2,1,0:T(8,128)S(1)}, s32[4,64,128]{2,1,0:T(8,128)}, u32[]{:S(2)}) copy-start(s32[4,64,128]{2,1,0:T(8,128)} %flags.1) | copy-start | bytes 393220
  2.3 8.1 %collective-permute-start.2 = (f32[10,8,8,128]{3,2,1,0:T(8,128)S(1)}, f32[10,8,8,128]{3,2,1,0:T(8,128)S(1)}, u32[]{:S(2)}, u32[]{:S(2)}) collective-permute-start(f32[10,8,8,128]{3,2,1,0:T(8,128)S(1)} %get-tuple-element.16), channel_id=1, source_target_pairs={{1,2},{2,1},{5,6},{6,5},{3,7},{7,3},{4,0},{0,4},{9,10},{10,9},{13,... | collective-permute-start | bytes 983048 | tf_op jit(solution)/shard_map/ppermute | solution.py:342
  5.3 14.0 %collective-permute-start = (f32[20,8,8,128]{3,2,1,0:T(8,128)S(1)}, f32[20,8,8,128]{3,2,1,0:T(8,128)S(1)}, u32[]{:S(2)}, u32[]{:S(2)}) collective-permute-start(f32[20,8,8,128]{3,2,1,0:T(8,128)S(1)} %get-tuple-element.14.own), channel_id=1, source_target_pairs={{0,1},{1,0},{2,3},{3,2},{4,5},{5,4},{6,7},{7,6},{8,9},{9,8},{10,11... | collective-permute-start | bytes 1966088 | tf_op jit(solution)/shard_map/ppermute | solution.py:344
  5.4 7.5 %collective-permute-start.1 = (f32[10,8,8,128]{3,2,1,0:T(8,128)S(1)}, f32[10,8,8,128]{3,2,1,0:T(8,128)S(1)}, u32[]{:S(2)}, u32[]{:S(2)}) collective-permute-start(f32[10,8,8,128]{3,2,1,0:T(8,128)S(1)} %get-tuple-element.15), channel_id=1, source_target_pairs={{1,2},{2,1},{3,4},{4,3},{5,6},{6,5},{0,0},{7,7},{9,10},{10,9},{11,... | collective-permute-start | bytes 983048 | tf_op jit(solution)/shard_map/ppermute | solution.py:343
  10.4 9.0 %collective-permute-start.3 = (f32[10,8,8,128]{3,2,1,0:T(8,128)S(1)}, f32[10,8,8,128]{3,2,1,0:T(8,128)S(1)}, u32[]{:S(2)}, u32[]{:S(2)}) collective-permute-start(f32[10,8,8,128]{3,2,1,0:T(8,128)S(1)} %collective-permute-done.2.outer_two), channel_id=1, source_target_pairs={{1,1},{2,2},{5,5},{6,6},{7,4},{0,3},{3,7},{4,0},{9,9},{10,10},{13,... | collective-permute-start | bytes 983048 | tf_op jit(solution)/shard_map/ppermute | solution.py:346
  22.1 6.4 %collective-permute-start.6 = (f32[8,8,8,128]{3,2,1,0:T(8,128)S(1)}, f32[8,8,8,128]{3,2,1,0:T(8,128)S(1)}, u32[]{:S(2)}, u32[]{:S(2)}) collective-permute-start(f32[8,8,8,128]{3,2,1,0:T(8,128)S(1)} %get-tuple-element.19), channel_id=1, source_target_pairs={{1,2},{2,1},{5,6},{6,5},{3,7},{7,3},{4,0},{0,4},{9,10},{10,9},{13,... | collective-permute-start | bytes 786440 | tf_op jit(solution)/shard_map/ppermute | solution.py:342
  23.6 8.3 %collective-permute-start.4 = (f32[16,8,8,128]{3,2,1,0:T(8,128)S(1)}, f32[16,8,8,128]{3,2,1,0:T(8,128)S(1)}, u32[]{:S(2)}, u32[]{:S(2)}) collective-permute-start(f32[16,8,8,128]{3,2,1,0:T(8,128)S(1)} %get-tuple-element.17.own), channel_id=1, source_target_pairs={{0,1},{1,0},{2,3},{3,2},{4,5},{5,4},{6,7},{7,6},{8,9},{9,8},{10,11... | collective-permute-start | bytes 1572872 | tf_op jit(solution)/shard_map/ppermute | solution.py:344
  23.6 8.3 %collective-permute-start.5 = (f32[8,8,8,128]{3,2,1,0:T(8,128)S(1)}, f32[8,8,8,128]{3,2,1,0:T(8,128)S(1)}, u32[]{:S(2)}, u32[]{:S(2)}) collective-permute-start(f32[8,8,8,128]{3,2,1,0:T(8,128)S(1)} %get-tuple-element.18), channel_id=1, source_target_pairs={{1,2},{2,1},{3,4},{4,3},{5,6},{6,5},{0,0},{7,7},{9,10},{10,9},{11,... | collective-permute-start | bytes 786440 | tf_op jit(solution)/shard_map/ppermute | solution.py:343
  28.6 8.3 %collective-permute-start.7 = (f32[8,8,8,128]{3,2,1,0:T(8,128)S(1)}, f32[8,8,8,128]{3,2,1,0:T(8,128)S(1)}, u32[]{:S(2)}, u32[]{:S(2)}) collective-permute-start(f32[8,8,8,128]{3,2,1,0:T(8,128)S(1)} %collective-permute-done.6.outer_two), channel_id=1, source_target_pairs={{1,1},{2,2},{5,5},{6,6},{7,4},{0,3},{3,7},{4,0},{9,9},{10,10},{13,... | collective-permute-start | bytes 786440 | tf_op jit(solution)/shard_map/ppermute | solution.py:346

commit v8 on v6

--- a/solution.py
+++ b/solution.py
@@ -269,11 +269,12 @@
     fine_round(space_size, slabs, even, odd, keep, finish)
     ended = halves(coarse_rows(lambda k, t: fine_end[2 * k, t] + fine_end[2 * k + 1, t], PACKED), PACKED)
     jumped = ended - jnp.where(lax.axis_index("tm") == 0, 0.0, guess[...])
-    jump[...] = jumped
-
-
-def correct_kernel(slices, space_size, *refs):
-    jumps, (guess, fine_end, out, grids) = refs[:-4], refs[-4:]
+    for k in range(jump.shape[0]):
+        jump[k] = jumped
+
+
+def correct_kernel(jumps, others, guess, fine_end, out, grids):
+    slices, space_size = jumps.shape[0] + 1, jumps.shape[1] * 2
     mine = lax.axis_index("tm")
     place = lax.axis_index("space")
     rows = grids.shape[2]
@@ -281,12 +282,13 @@
     plane = 2 * (place - slices) + iota((rows, NZ), 0) // 2
     valid = (plane >= 0) & (plane < 2 * space_size)
     grids[...] = jnp.zeros_like(grids)
-    at = 0
     for k in range(1, slices):
+        m = jnp.maximum(mine - k, 0)
         for j in range(-k, k + 1):
+            s = jnp.clip(place + j, 0, space_size - 1)
+            source = jumps if j % 2 == 0 else others
             for f in range(FIELDS):
-                grids[k - 1, f, pl.ds(centre + 4 * j, 4), :] = jumps[at][pl.ds(4 * f, 4), :]
-            at += 1
+                grids[k - 1, f, pl.ds(centre + 4 * j, 4), :] = source[m, s // 2, pl.ds(4 * f, 4), :]
     state = None
     for k in range(slices - 1, -1, -1):
         ended = state
@@ -350,19 +352,6 @@
     return within, across, x, y
 
 
-def earlier_jumps(jump, slices, space_size):
-    found = []
-    for k in range(1, slices):
-        for j in range(-k, k + 1):
-            route = []
-            for m in range(slices):
-                for s in range(space_size):
-                    target = (m + k) % slices * space_size + (s - j) % space_size
-                    route.append((m * space_size + s, target))
-            found.append(lax.ppermute(jump, ("tm", "space"), route))
-    return found
-
-
 def shaped(*shape):
     return jax.ShapeDtypeStruct(shape, F32)
 
@@ -376,7 +365,7 @@
         prepare_kernel,
         out_shape=(message, message),
         in_specs=[pl.BlockSpec(memory_space=pltpu.HBM)] * 2,
-        out_specs=(VMEM, VMEM),
+        out_specs=(VMEM,) * 2,
         scratch_shapes=[
             pltpu.VMEM(starts.shape, F32),
             pltpu.VMEM(flags.shape, flags.dtype),
@@ -406,23 +395,26 @@
     )(*opening, *opening_near)
     fine_end, jump = pl.pallas_call(
         functools.partial(second_kernel, space_size),
-        out_shape=(shaped(PACKED, TILES, 8, NZ), shaped(PACKED, NZ)),
+        out_shape=(shaped(PACKED, TILES, 8, NZ), shaped(slices * space_size // 2, PACKED, NZ)),
         in_specs=[VMEM] * 8,
         out_specs=(VMEM, VMEM),
         scratch_shapes=buffers,
         compiler_params=params(),
         name="second_round",
     )(*middle, *middle_near, keep, guess)
-    jumps = earlier_jumps(jump, slices, space_size)
+    members = [range(core, slices * space_size, 2) for core in range(2)]
+    jumps = lax.all_to_all(jump, ("tm", "space"), 0, 0, axis_index_groups=[list(group) for group in members])
+    jumps = jumps.reshape(slices, space_size // 2, PACKED, NZ)[: slices - 1]
+    others = lax.ppermute(jumps, "space", [(i, i ^ 1) for i in range(space_size)])
     return pl.pallas_call(
-        functools.partial(correct_kernel, slices, space_size),
+        correct_kernel,
         out_shape=shaped(1, FIELDS, PLANES, NY, NZ),
-        in_specs=[VMEM] * (len(jumps) + 2),
+        in_specs=[VMEM] * 4,
         out_specs=VMEM,
         scratch_shapes=[pltpu.VMEM((slices - 1, FIELDS, 8 * slices, NZ), F32)],
         compiler_params=params(),
         name="correct",
-    )(*jumps, guess, fine_end)
+    )(jumps, others, guess, fine_end)
 
 
 def solution(mesh):

time: 70.7 us -> 55 us (0.78)
  starting transfers between devices: 38.7 us -> 11.5 us
  blocking collectives: 0 us -> 16.8 us
  waiting for transfers between devices: 20.3 us -> 14.8 us
    ppermute x15 -> x1, starting transfers between devices: 27.2 us -> 0.07 us  [local(): lax.ppermute(jumps, 'space', [(i, i ^ 1) for i in range(space_size)])]
    all_to_all x0 -> x1, blocking collectives: none -> 16.8 us  [local(): lax.all_to_all(jump, ('tm', 'space'), 0, 0, axis_index_groups=[list(group...]
    ppermute x15 -> x1, waiting for transfers between devices: 6.69 us -> 1.29 us  [local(): lax.ppermute(jumps, 'space', [(i, i ^ 1) for i in range(space_size)])]
  transfers between devices with their start and end apart: 23 -> 9, of which waited for: 7 -> 5; matrix products, arithmetic and copies ran while one was open for 0% -> 0% of each run, Pallas kernels for 2% -> 3%
where the time goes in v8:
time: 55 us; the launch traced here: 54.8 us
  blocking collectives  16.8 us (31%)
  waiting for transfers between devices  14.8 us (27%)
  starting transfers between devices  11.5 us (21%)
  Pallas kernels  9.53 us (17%)
  local copies, waits for them, and re-layouts  1.95 us (4%)
    all_to_all x1, blocking collectives, local(): lax.all_to_all(jump, ('tm', 'space'), 0, 0, axis_index_groups=[list(group...  16.8 us
    ppermute x2, waiting for transfers between devices, exchange(): y = lax.ppermute(two, 'space', second)  9.35 us
    ppermute x2, starting transfers between devices, exchange(): within = lax.ppermute(one, 'space', inner)  5.25 us
    ppermute x2, starting transfers between devices, exchange(): x = lax.ppermute(two, 'space', first)  4.25 us
    ppermute x2, waiting for transfers between devices, exchange(): x = lax.ppermute(two, 'space', first)  4.2 us
    pallas_call x1, Pallas kernels, local(): pl.pallas_call(functools.partial(second_kernel, space_size), out_shape=(s...  3.12 us
    pallas_call x1, Pallas kernels, local(): pl.pallas_call(functools.partial(first_kernel, space_size), out_shape=(ha...  2.73 us
    unnamed x4, local copies, waits for them, and re-layouts  1.94 us
  transfers between devices with their start and end apart: 9, of which 5 were waited for; matrix products, arithmetic and copies ran while one was open for 0% of the time, Pallas kernels for 3%

profile of v8, /device:TPU:0, one launch (start us, length us, event | category | flops | bytes accessed | tf_op | source)
XLA Modules:
  0.0 54.8 jit_solution(9807428350308518024)
XLA Ops:
  0.0 1.0 %copy-done = f32[1,4,4,64,128]{4,3,2,1,0:T(8,128)S(1)} copy-done((f32[1,4,4,64,128]{4,3,2,1,0:T(8,128)S(1)}, f32[1,4,4,64,128]{4,3,2,1,0:T(8,128)}, u32[]{:S(2)}) %copy-start) | copy-done | bytes 524312
  1.0 0.9 %copy-done.1 = s32[4,64,128]{2,1,0:T(8,128)S(1)} copy-done((s32[4,64,128]{2,1,0:T(8,128)S(1)}, s32[4,64,128]{2,1,0:T(8,128)}, u32[]{:S(2)}) %copy-start.1) | copy-done | bytes 131096
  1.9 0.3 prepare.1
  2.3 0.5 collective-permute-start.2
  2.8 0.7 %collective-permute-start.1 = (f32[10,8,8,128]{3,2,1,0:T(8,128)S(1)}, f32[10,8,8,128]{3,2,1,0:T(8,128)S(1)}, u32[]{:S(2)}, u32[]{:S(2)}) collective-permute-start(f32[10,8,8,128]{3,2,1,0:T(8,128)S(1)} %get-tuple-element.12.own_one), channel_id=1, source_target_pairs={{0,0},{1,2},{2,1},{3,4},{4,3},{5,6},{6,5},{7,7},{8,8},{9,10},{10,9... | collective-permute-start | bytes 983048 | tf_op jit(solution)/shard_map/ppermute | solution.py:346
  3.5 3.9 %collective-permute-start = (f32[10,8,8,128]{3,2,1,0:T(8,128)S(1)}, f32[10,8,8,128]{3,2,1,0:T(8,128)S(1)}, u32[]{:S(2)}, u32[]{:S(2)}) collective-permute-start(f32[10,8,8,128]{3,2,1,0:T(8,128)S(1)} %get-tuple-element.12.own_one), channel_id=1, source_target_pairs={{0,1},{1,0},{2,3},{3,2},{4,5},{5,4},{6,7},{7,6},{8,9},{9,8},{10,11... | collective-permute-start | bytes 983048 | tf_op jit(solution)/shard_map/ppermute | solution.py:347
  7.4 3.0 %collective-permute-done.2.x = f32[10,8,8,128]{3,2,1,0:T(8,128)S(1)} collective-permute-done((f32[10,8,8,128]{3,2,1,0:T(8,128)S(1)}, f32[10,8,8,128]{3,2,1,0:T(8,128)S(1)}, u32[]{:S(2)}, u32[]{:S(2)}) %collective-permute-start.2) | collective-permute-done | bytes 327712 | tf_op jit(solution)/shard_map/ppermute | solution.py:345
  10.4 0.1 collective-permute-start.3
  10.5 0.0 collective-permute-done.1.outer
  10.5 5.8 %collective-permute-done.3.y = f32[10,8,8,128]{3,2,1,0:T(8,128)S(1)} collective-permute-done((f32[10,8,8,128]{3,2,1,0:T(8,128)S(1)}, f32[10,8,8,128]{3,2,1,0:T(8,128)S(1)}, u32[]{:S(2)}, u32[]{:S(2)}) %collective-permute-start.3) | collective-permute-done | bytes 327712 | tf_op jit(solution)/shard_map/ppermute | solution.py:351
  16.3 2.7 %first_round.1 = (f32[8,8,8,128]{3,2,1,0:T(8,128)S(1)}, f32[8,8,8,128]{3,2,1,0:T(8,128)S(1)}, f32[2,12,8,8,128]{4,3,2,1,0:T(8,128)S(1)}) custom-call(f32[10,8,8,128]{3,2,1,0:T(8,128)S(1)} %get-tuple-element.12.own_one, f32[10,8,8,128]{3,2,1,0:T(8,128)S(1)} %get-tuple-element.13.own_two, f32[10,8,8,128]{3,2,1,0:T(8,128)S(1)} %collective-permute-done.inner, ...), custom_call_target="tpu_custom_call" | custom-call | tf_op jit(solution)/shard_map/first_round/pallas_call | solution.py:378
  19.1 3.7 %collective-permute-start.6 = (f32[8,8,8,128]{3,2,1,0:T(8,128)S(1)}, f32[8,8,8,128]{3,2,1,0:T(8,128)S(1)}, u32[]{:S(2)}, u32[]{:S(2)}) collective-permute-start(f32[8,8,8,128]{3,2,1,0:T(8,128)S(1)} %get-tuple-element.15.own_two), channel_id=1, source_target_pairs={{0,1},{1,2},{2,3},{3,7},{7,6},{6,5},{5,4},{4,0},{8,9},{9,10},{10,1... | collective-permute-start | bytes 786440 | tf_op jit(solution)/shard_map/ppermute | solution.py:345
  22.8 0.7 %collective-permute-start.5 = (f32[8,8,8,128]{3,2,1,0:T(8,128)S(1)}, f32[8,8,8,128]{3,2,1,0:T(8,128)S(1)}, u32[]{:S(2)}, u32[]{:S(2)}) collective-permute-start(f32[8,8,8,128]{3,2,1,0:T(8,128)S(1)} %get-tuple-element.14.own_one), channel_id=1, source_target_pairs={{0,0},{1,2},{2,1},{3,4},{4,3},{5,6},{6,5},{7,7},{8,8},{9,10},{10,9... | collective-permute-start | bytes 786440 | tf_op jit(solution)/shard_map/ppermute | solution.py:346
  23.5 1.3 %collective-permute-start.4 = (f32[8,8,8,128]{3,2,1,0:T(8,128)S(1)}, f32[8,8,8,128]{3,2,1,0:T(8,128)S(1)}, u32[]{:S(2)}, u32[]{:S(2)}) collective-permute-start(f32[8,8,8,128]{3,2,1,0:T(8,128)S(1)} %get-tuple-element.14.own_one), channel_id=1, source_target_pairs={{0,1},{1,0},{2,3},{3,2},{4,5},{5,4},{6,7},{7,6},{8,9},{9,8},{10,11... | collective-permute-start | bytes 786440 | tf_op jit(solution)/shard_map/ppermute | solution.py:347
  24.8 1.2 %collective-permute-done.6.x = f32[8,8,8,128]{3,2,1,0:T(8,128)S(1)} collective-permute-done((f32[8,8,8,128]{3,2,1,0:T(8,128)S(1)}, f32[8,8,8,128]{3,2,1,0:T(8,128)S(1)}, u32[]{:S(2)}, u32[]{:S(2)}) %collective-permute-start.6) | collective-permute-done | bytes 262176 | tf_op jit(solution)/shard_map/ppermute | solution.py:345
  26.1 0.6 %collective-permute-start.7 = (f32[8,8,8,128]{3,2,1,0:T(8,128)S(1)}, f32[8,8,8,128]{3,2,1,0:T(8,128)S(1)}, u32[]{:S(2)}, u32[]{:S(2)}) collective-permute-start(f32[8,8,8,128]{3,2,1,0:T(8,128)S(1)} %broadcast_select_fusion.1), channel_id=1, source_target_pairs={{3,2},{2,1},{1,0},{0,3},{4,5},{5,6},{6,7},{7,4},{11,10},{10,9},{9,... | collective-permute-start | bytes 786440 | tf_op jit(solution)/shard_map/ppermute | solution.py:351
  26.6 1.4 %guess_old.1.guess = f32[16,128]{1,0:T(8,128)S(1)} custom-call(f32[10,8,8,128]{3,2,1,0:T(8,128)S(1)} %get-tuple-element.12.own_one, f32[10,8,8,128]{3,2,1,0:T(8,128)S(1)} %get-tuple-element.13.own_two, f32[10,8,8,128]{3,2,1,0:T(8,128)S(1)} %collective-permute-done.inner, f32[10,8,8,128]{3,2,1,0:T(8,128)S(1)} %collective-permute-done.1.outer, ...), custom_call_target="tpu_custom_call" | custom-call | tf_op jit(solution)/shard_map/guess_old/pallas_call | solution.py:388
  28.1 0.0 collective-permute-done.5.outer
  28.1 3.5 %collective-permute-done.7.y = f32[8,8,8,128]{3,2,1,0:T(8,128)S(1)} collective-permute-done((f32[8,8,8,128]{3,2,1,0:T(8,128)S(1)}, f32[8,8,8,128]{3,2,1,0:T(8,128)S(1)}, u32[]{:S(2)}, u32[]{:S(2)}) %collective-permute-start.7) | collective-permute-done | bytes 262176 | tf_op jit(solution)/shard_map/ppermute | solution.py:351
  31.6 3.1 %second_round.1 = (f32[16,8,8,128]{3,2,1,0:T(8,128)S(1)}, f32[16,16,128]{2,1,0:T(8,128)S(1)}) custom-call(f32[8,8,8,128]{3,2,1,0:T(8,128)S(1)} %get-tuple-element.14.own_one, f32[8,8,8,128]{3,2,1,0:T(8,128)S(1)} %get-tuple-element.15.own_two, f32[8,8,8,128]{3,2,1,0:T(8,128)S(1)} %collective-permute-done.4.inner, ...), custom_call_target="tpu_custom_call" | custom-call | tf_op jit(solution)/shard_map/second_round/pallas_call | solution.py:396
  34.8 16.8 %all_to_all.5 = f32[16,16,128]{2,1,0:T(8,128)S(1)} all-to-all(f32[16,16,128]{2,1,0:T(8,128)S(1)} %get-tuple-element.17), channel_id=1, replica_groups={{0,2,4,6,8,10,12,14,16,18,20,22,24,26,28,30},{1,3,5,7,9,11,13,15,17,19,..., dimensions={0} | all-to-all | bytes 262144 | tf_op jit(solution)/shard_map/all_to_all | solution.py:406
  51.6 0.1 collective-permute-start.8
  51.6 1.3 %collective-permute-done.8.others = f32[3,4,16,128]{3,2,1,0:T(8,128)S(1)} collective-permute-done((f32[3,4,16,128]{3,2,1,0:T(8,128)S(1)}, f32[3,4,16,128]{3,2,1,0:T(8,128)S(1)}, u32[]{:S(2)}, u32[]{:S(2)}) %collective-permute-start.8) | collective-permute-done | bytes 98336 | tf_op jit(solution)/shard_map/ppermute | solution.py:408
  52.9 1.9 %correct.1 = f32[1,4,4,64,128]{4,3,2,1,0:T(8,128)} custom-call(f32[3,4,16,128]{3,2,1,0:T(8,128)S(1)} %bitcast.2, f32[3,4,16,128]{3,2,1,0:T(8,128)S(1)} %collective-permute-done.8.others, f32[16,128]{1,0:T(8,128)S(1)} %guess_old.1.guess, f32[16,8,8,128]{3,2,1,0:T(8,128)S(1)} %get-tuple-element.18.fine_end), custom_call_target="tpu_custom_call" | custom-call | tf_op jit(solution)/shard_map/correct/pallas_call | solution.py:409
  (7 shorter events, 0.1 us)
Async XLA Ops:
  0.0 1.0 %copy-start = (f32[1,4,4,64,128]{4,3,2,1,0:T(8,128)S(1)}, f32[1,4,4,64,128]{4,3,2,1,0:T(8,128)}, u32[]{:S(2)}) copy-start(f32[1,4,4,64,128]{4,3,2,1,0:T(8,128)} %starts.1) | copy-start | bytes 1572868
  1.0 0.9 %copy-start.1 = (s32[4,64,128]{2,1,0:T(8,128)S(1)}, s32[4,64,128]{2,1,0:T(8,128)}, u32[]{:S(2)}) copy-start(s32[4,64,128]{2,1,0:T(8,128)} %flags.1) | copy-start | bytes 393220
  2.3 8.1 %collective-permute-start.2 = (f32[10,8,8,128]{3,2,1,0:T(8,128)S(1)}, f32[10,8,8,128]{3,2,1,0:T(8,128)S(1)}, u32[]{:S(2)}, u32[]{:S(2)}) collective-permute-start(f32[10,8,8,128]{3,2,1,0:T(8,128)S(1)} %get-tuple-element.13.own_two), channel_id=1, source_target_pairs={{0,1},{1,2},{2,3},{3,7},{7,6},{6,5},{5,4},{4,0},{8,9},{9,10},{10,1... | collective-permute-start | bytes 983048 | tf_op jit(solution)/shard_map/ppermute | solution.py:345
  2.8 7.7 %collective-permute-start.1 = (f32[10,8,8,128]{3,2,1,0:T(8,128)S(1)}, f32[10,8,8,128]{3,2,1,0:T(8,128)S(1)}, u32[]{:S(2)}, u32[]{:S(2)}) collective-permute-start(f32[10,8,8,128]{3,2,1,0:T(8,128)S(1)} %get-tuple-element.12.own_one), channel_id=1, source_target_pairs={{0,0},{1,2},{2,1},{3,4},{4,3},{5,6},{6,5},{7,7},{8,8},{9,10},{10,9... | collective-permute-start | bytes 983048 | tf_op jit(solution)/shard_map/ppermute | solution.py:346
  3.5 7.0 %collective-permute-start = (f32[10,8,8,128]{3,2,1,0:T(8,128)S(1)}, f32[10,8,8,128]{3,2,1,0:T(8,128)S(1)}, u32[]{:S(2)}, u32[]{:S(2)}) collective-permute-start(f32[10,8,8,128]{3,2,1,0:T(8,128)S(1)} %get-tuple-element.12.own_one), channel_id=1, source_target_pairs={{0,1},{1,0},{2,3},{3,2},{4,5},{5,4},{6,7},{7,6},{8,9},{9,8},{10,11... | collective-permute-start | bytes 983048 | tf_op jit(solution)/shard_map/ppermute | solution.py:347
  10.4 5.9 %collective-permute-start.3 = (f32[10,8,8,128]{3,2,1,0:T(8,128)S(1)}, f32[10,8,8,128]{3,2,1,0:T(8,128)S(1)}, u32[]{:S(2)}, u32[]{:S(2)}) collective-permute-start(f32[10,8,8,128]{3,2,1,0:T(8,128)S(1)} %broadcast_select_fusion), channel_id=1, source_target_pairs={{3,2},{2,1},{1,0},{0,3},{4,5},{5,6},{6,7},{7,4},{11,10},{10,9},{9,... | collective-permute-start | bytes 983048 | tf_op jit(solution)/shard_map/ppermute | solution.py:351
  19.1 7.0 %collective-permute-start.6 = (f32[8,8,8,128]{3,2,1,0:T(8,128)S(1)}, f32[8,8,8,128]{3,2,1,0:T(8,128)S(1)}, u32[]{:S(2)}, u32[]{:S(2)}) collective-permute-start(f32[8,8,8,128]{3,2,1,0:T(8,128)S(1)} %get-tuple-element.15.own_two), channel_id=1, source_target_pairs={{0,1},{1,2},{2,3},{3,7},{7,6},{6,5},{5,4},{4,0},{8,9},{9,10},{10,1... | collective-permute-start | bytes 786440 | tf_op jit(solution)/shard_map/ppermute | solution.py:345
  22.8 5.3 %collective-permute-start.5 = (f32[8,8,8,128]{3,2,1,0:T(8,128)S(1)}, f32[8,8,8,128]{3,2,1,0:T(8,128)S(1)}, u32[]{:S(2)}, u32[]{:S(2)}) collective-permute-start(f32[8,8,8,128]{3,2,1,0:T(8,128)S(1)} %get-tuple-element.14.own_one), channel_id=1, source_target_pairs={{0,0},{1,2},{2,1},{3,4},{4,3},{5,6},{6,5},{7,7},{8,8},{9,10},{10,9... | collective-permute-start | bytes 786440 | tf_op jit(solution)/shard_map/ppermute | solution.py:346
  23.5 4.6 %collective-permute-start.4 = (f32[8,8,8,128]{3,2,1,0:T(8,128)S(1)}, f32[8,8,8,128]{3,2,1,0:T(8,128)S(1)}, u32[]{:S(2)}, u32[]{:S(2)}) collective-permute-start(f32[8,8,8,128]{3,2,1,0:T(8,128)S(1)} %get-tuple-element.14.own_one), channel_id=1, source_target_pairs={{0,1},{1,0},{2,3},{3,2},{4,5},{5,4},{6,7},{7,6},{8,9},{9,8},{10,11... | collective-permute-start | bytes 786440 | tf_op jit(solution)/shard_map/ppermute | solution.py:347
  26.1 5.6 %collective-permute-start.7 = (f32[8,8,8,128]{3,2,1,0:T(8,128)S(1)}, f32[8,8,8,128]{3,2,1,0:T(8,128)S(1)}, u32[]{:S(2)}, u32[]{:S(2)}) collective-permute-start(f32[8,8,8,128]{3,2,1,0:T(8,128)S(1)} %broadcast_select_fusion.1), channel_id=1, source_target_pairs={{3,2},{2,1},{1,0},{0,3},{4,5},{5,6},{6,7},{7,4},{11,10},{10,9},{9,... | collective-permute-start | bytes 786440 | tf_op jit(solution)/shard_map/ppermute | solution.py:351
  51.6 1.4 %collective-permute-start.8 = (f32[3,4,16,128]{3,2,1,0:T(8,128)S(1)}, f32[3,4,16,128]{3,2,1,0:T(8,128)S(1)}, u32[]{:S(2)}, u32[]{:S(2)}) collective-permute-start(f32[3,4,16,128]{3,2,1,0:T(8,128)S(1)} %bitcast.1), channel_id=1, source_target_pairs={{0,1},{1,0},{2,3},{3,2},{4,5},{5,4},{6,7},{7,6},{8,9},{9,8},{10,11... | collective-permute-start | bytes 294920 | tf_op jit(solution)/shard_map/ppermute | solution.py:408

commit v9 on v8

--- a/solution.py
+++ b/solution.py
@@ -36,22 +36,23 @@
     return pltpu.CompilerParams(vmem_limit_bytes=LIMIT)
 
 
-def prepare_kernel(starts, flags, message_one, message_two, fields, kinds, sems):
+def prepare_kernel(space_size, starts, flags, one, two_x, two_y, fields, kinds, sems):
+    low = lax.axis_index("space") < turn(space_size)
     copies = [pltpu.make_async_copy(starts, fields, sems.at[0]), pltpu.make_async_copy(flags, kinds, sems.at[1])]
     for copy in copies:
         copy.start()
     for copy in copies:
         copy.wait()
-    for f in range(FIELDS):
-        message = message_one if f < 2 else message_two
-        for x in range(PLANES):
-            for t in range(TILES):
+    for t in range(TILES):
+        for f in range(FIELDS):
+            for x in range(PLANES):
                 v = fields[0, f, x, pl.ds(t, 8, stride=8), :]
-                message[f % 2 * PLANES + x, t] = v * 0.5 if f == 0 else v
-    for x in range(PLANES):
-        message = message_one if x < 2 else message_two
-        for t in range(TILES):
-            message[2 * PLANES + x % 2, t] = kinds[x, pl.ds(t, 8, stride=8), :].astype(F32)
+                for message in (one,) if f < 2 else (two_x, two_y):
+                    message[f % 2 * PLANES + x, t] = v * 0.5 if f == 0 else v
+        kind = [kinds[x, pl.ds(t, 8, stride=8), :].astype(F32) for x in range(PLANES)]
+        one[2 * PLANES, t], one[2 * PLANES + 1, t] = kind[1], kind[2]
+        two_x[2 * PLANES, t] = jnp.where(low, kind[3], kind[0])
+        two_y[2 * PLANES, t] = jnp.where(low, kind[0], kind[3])
 
 
 def fine_tile(mid, lo_x, hi_x, lo_y, hi_y, kv, ks, kc, low_lane, high_lane):
@@ -108,7 +109,8 @@
         place = lax.axis_index("space")
         self.own = own
         self.near = (near[:2], near[2:])
-        self.from_first = (place % 2 == 1, place < turn(space_size))
+        self.low = place < turn(space_size)
+        self.from_first = (place % 2 == 1, self.low)
         self.there = {0: place > 0, 2: place < space_size - 1}
 
     def row(self, j, half, k, t):
@@ -123,7 +125,7 @@
         return self.row(j, f // 2, f % 2 * PLANES + x, t)
 
     def kind(self, j, x, t):
-        return self.row(j, x // 2, 2 * PLANES + x % 2, t)
+        return self.row(j, 0, 2 * PLANES + x - 1, t) if x in (1, 2) else self.row(j, 1, 2 * PLANES, t)
 
 
 def inside(space_size, p):
@@ -155,22 +157,35 @@
         lax.fori_loop(0, 2, body, 0)
 
 
-def first_kernel(space_size, own_one, own_two, inner, outer, x, y, ended_one, ended_two, keep, even, odd):
+def first_kernel(space_size, own_one, own_two, own_other, inner, outer, x, y, ended_one, ended_two, keep, even, odd):
     slabs = Slabs(space_size, (own_one, own_two), (inner, outer, x, y))
-    for j in range(3):
-        for k in range(PLANES):
-            p = j * PLANES + k
-            scale = jnp.where(inside(space_size, p), fine_dt, 0.0).astype(F32)
-            for t in range(TILES):
-                kind = slabs.kind(j, k, t)
-                keep[0, p, t] = jnp.where(kind != 1.0, scale, 0.0)
-                keep[1, p, t] = jnp.where(kind != 2.0, scale, 0.0)
+    for p in range(1, WINDOW - 1):
+        j, k = p // PLANES, p % PLANES
+        scale = jnp.where(inside(space_size, p), fine_dt, 0.0).astype(F32)
+        for t in range(TILES):
+            kind = slabs.kind(j, k, t)
+            if j == 1 and k in (0, PLANES - 1):
+                other = own_other[2 * PLANES, t]
+                kind = jnp.where(slabs.low == (k == 0), other, kind)
+            keep[0, p, t] = jnp.where(kind != 1.0, scale, 0.0)
+            keep[1, p, t] = jnp.where(kind != 2.0, scale, 0.0)
 
     def finish(f, x, t, value):
         ended = ended_one if f < 2 else ended_two
         ended[f % 2 * PLANES + x, t] = value
 
     fine_round(space_size, slabs, even, odd, keep, finish)
+
+
+def chosen(values, picks):
+    parts, rest = [], values
+    for _ in range(3):
+        part = rest.astype(jnp.bfloat16)
+        parts.append(part)
+        rest = rest - part.astype(F32)
+    stacked = jnp.concatenate(parts, axis=1)
+    picks = jnp.concatenate([picks.astype(jnp.bfloat16)] * 3, axis=0)
+    return jnp.dot(stacked, picks, preferred_element_type=F32)
 
 
 def coarse_rows(pair_of, count):
@@ -181,7 +196,7 @@
             pieces.append(pair_of(k, 2 * i) + pair_of(k, 2 * i + 1))
     stacked = jnp.concatenate(pieces, axis=0)
     gather = (iota((NZ, NZ), 0) // 16 == iota((NZ, NZ), 1) % 8).astype(F32)
-    sums = jnp.dot(stacked, gather, precision=HIGHEST, preferred_element_type=F32)
+    sums = chosen(stacked, gather)
     sums = sums * pick_rows(sums.shape)
     sums = sums.reshape(pairs, TILES // 2, 8, NZ)
     sums = (sums[:, 0] + sums[:, 1]) + (sums[:, 2] + sums[:, 3])
@@ -273,7 +288,7 @@
         jump[k] = jumped
 
 
-def correct_kernel(jumps, others, guess, fine_end, out, grids):
+def correct_kernel(jumps, others, guess, fine_end, out, grids, result, sems):
     slices, space_size = jumps.shape[0] + 1, jumps.shape[1] * 2
     mine = lax.axis_index("tm")
     place = lax.axis_index("space")
@@ -314,12 +329,15 @@
     stacked = jnp.concatenate(pieces, axis=0)
     stacked = stacked * pick_rows(stacked.shape)
     spread = (iota((NZ, NZ), 0) % 8 == iota((NZ, NZ), 1) // 16).astype(F32)
-    wide = jnp.dot(stacked, spread, precision=HIGHEST, preferred_element_type=F32)
+    wide = chosen(stacked, spread)
     for f in range(FIELDS):
         for x in range(PLANES):
             for t in range(TILES):
                 k = ((f * 2 + x // 2) * (TILES // 2) + t // 2) * 8
-                out[0, f, x, pl.ds(t, 8, stride=8), :] = fine_end[f * PLANES + x, t] + wide[k : k + 8]
+                result[f, x, pl.ds(t, 8, stride=8), :] = fine_end[f * PLANES + x, t] + wide[k : k + 8]
+        pltpu.make_async_copy(result.at[f], out.at[0, f], sems.at[f]).start()
+    for f in range(FIELDS):
+        pltpu.make_async_copy(result.at[f], out.at[0, f], sems.at[f]).wait()
 
 
 def relayed(size):
@@ -330,7 +348,7 @@
     return size // 2 if relayed(size) else size
 
 
-def exchange(one, two, size):
+def exchange(one, two_x, two_y, size):
     inner = [(i, i ^ 1) for i in range(size)]
     outer = [(0, 0)] + [(i, (i - 1 ^ 1) + 1) for i in range(1, size - 1)] + [(size - 1, size - 1)]
     if relayed(size):
@@ -342,13 +360,13 @@
     else:
         first = [(i, (i + 1) % size) for i in range(size)]
         second = [(i, (i - 1) % size) for i in range(size)]
-    x = lax.ppermute(two, "space", first)
+    x = lax.ppermute(two_x, "space", first)
     across = lax.ppermute(one, "space", outer)
     within = lax.ppermute(one, "space", inner)
     if relayed(size):
         place = lax.axis_index("space")
-        two = jnp.where((place == 0) | (place == size - 1), x, two)
-    y = lax.ppermute(two, "space", second)
+        two_y = jnp.where((place == 0) | (place == size - 1), x, two_y)
+    y = lax.ppermute(two_y, "space", second)
     return within, across, x, y
 
 
@@ -358,14 +376,14 @@
 
 def local(slices, space_size, starts, flags):
     half = shaped(2 * PLANES, TILES, 8, NZ)
-    message = shaped(2 * PLANES + 2, TILES, 8, NZ)
+    message_one, message_two = shaped(2 * PLANES + 2, TILES, 8, NZ), shaped(2 * PLANES + 1, TILES, 8, NZ)
     keep_shape = shaped(2, WINDOW, TILES, 8, NZ)
     buffers = [pltpu.VMEM((FIELDS, WINDOW, TILES + 2, 8, NZ), F32)] * 2
     opening = pl.pallas_call(
-        prepare_kernel,
-        out_shape=(message, message),
+        functools.partial(prepare_kernel, space_size),
+        out_shape=(message_one, message_two, message_two),
         in_specs=[pl.BlockSpec(memory_space=pltpu.HBM)] * 2,
-        out_specs=(VMEM,) * 2,
+        out_specs=(VMEM,) * 3,
         scratch_shapes=[
             pltpu.VMEM(starts.shape, F32),
             pltpu.VMEM(flags.shape, flags.dtype),
@@ -378,13 +396,13 @@
     *middle, keep = pl.pallas_call(
         functools.partial(first_kernel, space_size),
         out_shape=(half, half, keep_shape),
-        in_specs=[VMEM] * 6,
+        in_specs=[VMEM] * 7,
         out_specs=(VMEM,) * 3,
         scratch_shapes=buffers,
         compiler_params=params(),
         name="first_round",
     )(*opening, *opening_near)
-    middle_near = exchange(*middle, space_size)
+    middle_near = exchange(middle[0], middle[1], middle[1], space_size)
     guess = pl.pallas_call(
         functools.partial(guess_kernel, space_size),
         out_shape=shaped(PACKED, NZ),
@@ -392,7 +410,7 @@
         out_specs=VMEM,
         compiler_params=params(),
         name="guess_old",
-    )(*opening, *opening_near)
+    )(*opening[:2], *opening_near)
     fine_end, jump = pl.pallas_call(
         functools.partial(second_kernel, space_size),
         out_shape=(shaped(PACKED, TILES, 8, NZ), shaped(slices * space_size // 2, PACKED, NZ)),
@@ -410,8 +428,12 @@
         correct_kernel,
         out_shape=shaped(1, FIELDS, PLANES, NY, NZ),
         in_specs=[VMEM] * 4,
-        out_specs=VMEM,
-        scratch_shapes=[pltpu.VMEM((slices - 1, FIELDS, 8 * slices, NZ), F32)],
+        out_specs=pl.BlockSpec(memory_space=pltpu.HBM),
+        scratch_shapes=[
+            pltpu.VMEM((slices - 1, FIELDS, 8 * slices, NZ), F32),
+            pltpu.VMEM((FIELDS, PLANES, NY, NZ), F32),
+            pltpu.SemaphoreType.DMA((FIELDS,)),
+        ],
         compiler_params=params(),
         name="correct",
     )(jumps, others, guess, fine_end)

time: 55 us -> 54.9 us (level)
  waiting for transfers between devices: 14.8 us -> 14.1 us
  starting transfers between devices: 11.5 us -> 12.2 us
    ppermute x4, waiting for transfers between devices: 13.5 us -> 12.8 us  [the longest x2 9.31 us: exchange(): y = lax.ppermute(two_y, 'space', second)]
    ppermute x4, starting transfers between devices: 4.87 us -> 5.57 us  [the longest x2 4.6 us: exchange(): x = lax.ppermute(two_x, 'space', first)]
  transfers between devices with their start and end apart: 9 -> 9, of which waited for: 5 -> 5; matrix products, arithmetic and copies ran while one was open for 0% -> 0% of each run, Pallas kernels for 3% -> 2%
where the time goes in v9:
time: 54.9 us; the launch traced here: 54.6 us
  blocking collectives  17.1 us (31%)
  waiting for transfers between devices  14.1 us (26%)
  starting transfers between devices  12.2 us (22%)
  Pallas kernels  9.05 us (16%)
  local copies, waits for them, and re-layouts  1.95 us (4%)
    all_to_all x1, blocking collectives, local(): lax.all_to_all(jump, ('tm', 'space'), 0, 0, axis_index_groups=[list(group...  17.1 us
    ppermute x2, waiting for transfers between devices, exchange(): y = lax.ppermute(two_y, 'space', second)  9.31 us
    ppermute x2, starting transfers between devices, exchange(): within = lax.ppermute(one, 'space', inner)  5.25 us
    ppermute x2, starting transfers between devices, exchange(): x = lax.ppermute(two_x, 'space', first)  4.6 us
    ppermute x2, waiting for transfers between devices, exchange(): x = lax.ppermute(two_x, 'space', first)  3.49 us
    pallas_call x1, Pallas kernels, local(): pl.pallas_call(functools.partial(second_kernel, space_size), out_shape=(s...  3.05 us
    pallas_call x1, Pallas kernels, local(): pl.pallas_call(functools.partial(first_kernel, space_size), out_shape=(ha...  2.72 us
    unnamed x4, local copies, waits for them, and re-layouts  1.94 us
  transfers between devices with their start and end apart: 9, of which 5 were waited for; matrix products, arithmetic and copies ran while one was open for 0% of the time, Pallas kernels for 2%

profile of v9, /device:TPU:0, one launch (start us, length us, event | category | flops | bytes accessed | tf_op | source)
XLA Modules:
  0.0 54.6 jit_solution(12215056616592210983)
XLA Ops:
  0.0 1.0 %copy-done = f32[1,4,4,64,128]{4,3,2,1,0:T(8,128)S(1)} copy-done((f32[1,4,4,64,128]{4,3,2,1,0:T(8,128)S(1)}, f32[1,4,4,64,128]{4,3,2,1,0:T(8,128)}, u32[]{:S(2)}) %copy-start) | copy-done | bytes 524312
  1.0 0.9 %copy-done.1 = s32[4,64,128]{2,1,0:T(8,128)S(1)} copy-done((s32[4,64,128]{2,1,0:T(8,128)S(1)}, s32[4,64,128]{2,1,0:T(8,128)}, u32[]{:S(2)}) %copy-start.1) | copy-done | bytes 131096
  1.9 0.4 prepare.1
  2.3 0.5 collective-permute-start.2
  2.8 0.7 %collective-permute-start.1 = (f32[10,8,8,128]{3,2,1,0:T(8,128)S(1)}, f32[10,8,8,128]{3,2,1,0:T(8,128)S(1)}, u32[]{:S(2)}, u32[]{:S(2)}) collective-permute-start(f32[10,8,8,128]{3,2,1,0:T(8,128)S(1)} %get-tuple-element.13.own_one), channel_id=1, source_target_pairs={{0,0},{1,2},{2,1},{3,4},{4,3},{5,6},{6,5},{7,7},{8,8},{9,10},{10,9... | collective-permute-start | bytes 983048 | tf_op jit(solution)/shard_map/ppermute | solution.py:364
  3.5 3.9 %collective-permute-start = (f32[10,8,8,128]{3,2,1,0:T(8,128)S(1)}, f32[10,8,8,128]{3,2,1,0:T(8,128)S(1)}, u32[]{:S(2)}, u32[]{:S(2)}) collective-permute-start(f32[10,8,8,128]{3,2,1,0:T(8,128)S(1)} %get-tuple-element.13.own_one), channel_id=1, source_target_pairs={{0,1},{1,0},{2,3},{3,2},{4,5},{5,4},{6,7},{7,6},{8,9},{9,8},{10,11... | collective-permute-start | bytes 983048 | tf_op jit(solution)/shard_map/ppermute | solution.py:365
  7.4 2.6 %collective-permute-done.2.x = f32[9,8,8,128]{3,2,1,0:T(8,128)S(1)} collective-permute-done((f32[9,8,8,128]{3,2,1,0:T(8,128)S(1)}, f32[9,8,8,128]{3,2,1,0:T(8,128)S(1)}, u32[]{:S(2)}, u32[]{:S(2)}) %collective-permute-start.2) | collective-permute-done | bytes 294944 | tf_op jit(solution)/shard_map/ppermute | solution.py:363
  10.1 0.1 collective-permute-start.3
  10.1 0.0 collective-permute-done.1.outer
  10.2 5.5 %collective-permute-done.3.y = f32[9,8,8,128]{3,2,1,0:T(8,128)S(1)} collective-permute-done((f32[9,8,8,128]{3,2,1,0:T(8,128)S(1)}, f32[9,8,8,128]{3,2,1,0:T(8,128)S(1)}, u32[]{:S(2)}, u32[]{:S(2)}) %collective-permute-start.3) | collective-permute-done | bytes 294944 | tf_op jit(solution)/shard_map/ppermute | solution.py:369
  15.7 2.7 %first_round.1 = (f32[8,8,8,128]{3,2,1,0:T(8,128)S(1)}, f32[8,8,8,128]{3,2,1,0:T(8,128)S(1)}, f32[2,12,8,8,128]{4,3,2,1,0:T(8,128)S(1)}) custom-call(f32[10,8,8,128]{3,2,1,0:T(8,128)S(1)} %get-tuple-element.13.own_one, f32[9,8,8,128]{3,2,1,0:T(8,128)S(1)} %get-tuple-element.14.own_two, f32[9,8,8,128]{3,2,1,0:T(8,128)S(1)} %get-tuple-element.15.own_other, ...), custom_call_target="tpu_custom_call" | custom-call | tf_op jit(solution)/shard_map/first_round/pallas_call | solution.py:396
  18.4 4.1 %collective-permute-start.6 = (f32[8,8,8,128]{3,2,1,0:T(8,128)S(1)}, f32[8,8,8,128]{3,2,1,0:T(8,128)S(1)}, u32[]{:S(2)}, u32[]{:S(2)}) collective-permute-start(f32[8,8,8,128]{3,2,1,0:T(8,128)S(1)} %get-tuple-element.17.own_two), channel_id=1, source_target_pairs={{0,1},{1,2},{2,3},{3,7},{7,6},{6,5},{5,4},{4,0},{8,9},{9,10},{10,1... | collective-permute-start | bytes 786440 | tf_op jit(solution)/shard_map/ppermute | solution.py:363
  22.5 0.7 %collective-permute-start.5 = (f32[8,8,8,128]{3,2,1,0:T(8,128)S(1)}, f32[8,8,8,128]{3,2,1,0:T(8,128)S(1)}, u32[]{:S(2)}, u32[]{:S(2)}) collective-permute-start(f32[8,8,8,128]{3,2,1,0:T(8,128)S(1)} %get-tuple-element.16.own_one), channel_id=1, source_target_pairs={{0,0},{1,2},{2,1},{3,4},{4,3},{5,6},{6,5},{7,7},{8,8},{9,10},{10,9... | collective-permute-start | bytes 786440 | tf_op jit(solution)/shard_map/ppermute | solution.py:364
  23.1 1.3 %collective-permute-start.4 = (f32[8,8,8,128]{3,2,1,0:T(8,128)S(1)}, f32[8,8,8,128]{3,2,1,0:T(8,128)S(1)}, u32[]{:S(2)}, u32[]{:S(2)}) collective-permute-start(f32[8,8,8,128]{3,2,1,0:T(8,128)S(1)} %get-tuple-element.16.own_one), channel_id=1, source_target_pairs={{0,1},{1,0},{2,3},{3,2},{4,5},{5,4},{6,7},{7,6},{8,9},{9,8},{10,11... | collective-permute-start | bytes 786440 | tf_op jit(solution)/shard_map/ppermute | solution.py:365
  24.5 0.9 %collective-permute-done.6.x = f32[8,8,8,128]{3,2,1,0:T(8,128)S(1)} collective-permute-done((f32[8,8,8,128]{3,2,1,0:T(8,128)S(1)}, f32[8,8,8,128]{3,2,1,0:T(8,128)S(1)}, u32[]{:S(2)}, u32[]{:S(2)}) %collective-permute-start.6) | collective-permute-done | bytes 262176 | tf_op jit(solution)/shard_map/ppermute | solution.py:363
  25.4 0.9 %collective-permute-start.7 = (f32[8,8,8,128]{3,2,1,0:T(8,128)S(1)}, f32[8,8,8,128]{3,2,1,0:T(8,128)S(1)}, u32[]{:S(2)}, u32[]{:S(2)}) collective-permute-start(f32[8,8,8,128]{3,2,1,0:T(8,128)S(1)} %broadcast_select_fusion.1), channel_id=1, source_target_pairs={{3,2},{2,1},{1,0},{0,3},{4,5},{5,6},{6,7},{7,4},{11,10},{10,9},{9,... | collective-permute-start | bytes 786440 | tf_op jit(solution)/shard_map/ppermute | solution.py:369
  26.3 1.1 %guess_old.1.guess = f32[16,128]{1,0:T(8,128)S(1)} custom-call(f32[10,8,8,128]{3,2,1,0:T(8,128)S(1)} %get-tuple-element.13.own_one, f32[9,8,8,128]{3,2,1,0:T(8,128)S(1)} %get-tuple-element.14.own_two, f32[10,8,8,128]{3,2,1,0:T(8,128)S(1)} %collective-permute-done.inner, f32[10,8,8,128]{3,2,1,0:T(8,128)S(1)} %collective-permute-done.1.outer, ...), custom_call_target="tpu_custom_call" | custom-call | tf_op jit(solution)/shard_map/guess_old/pallas_call | solution.py:406
  27.4 0.0 collective-permute-done.4.inner
  27.5 3.8 %collective-permute-done.7.y = f32[8,8,8,128]{3,2,1,0:T(8,128)S(1)} collective-permute-done((f32[8,8,8,128]{3,2,1,0:T(8,128)S(1)}, f32[8,8,8,128]{3,2,1,0:T(8,128)S(1)}, u32[]{:S(2)}, u32[]{:S(2)}) %collective-permute-start.7) | collective-permute-done | bytes 262176 | tf_op jit(solution)/shard_map/ppermute | solution.py:369
  31.3 3.1 %second_round.1 = (f32[16,8,8,128]{3,2,1,0:T(8,128)S(1)}, f32[16,16,128]{2,1,0:T(8,128)S(1)}) custom-call(f32[8,8,8,128]{3,2,1,0:T(8,128)S(1)} %get-tuple-element.16.own_one, f32[8,8,8,128]{3,2,1,0:T(8,128)S(1)} %get-tuple-element.17.own_two, f32[8,8,8,128]{3,2,1,0:T(8,128)S(1)} %collective-permute-done.4.inner, ...), custom_call_target="tpu_custom_call" | custom-call | tf_op jit(solution)/shard_map/second_round/pallas_call | solution.py:414
  34.3 17.1 %all_to_all.5 = f32[16,16,128]{2,1,0:T(8,128)S(1)} all-to-all(f32[16,16,128]{2,1,0:T(8,128)S(1)} %get-tuple-element.19), channel_id=1, replica_groups={{0,2,4,6,8,10,12,14,16,18,20,22,24,26,28,30},{1,3,5,7,9,11,13,15,17,19,..., dimensions={0} | all-to-all | bytes 262144 | tf_op jit(solution)/shard_map/all_to_all | solution.py:424
  51.5 0.1 collective-permute-start.8
  51.6 1.3 %collective-permute-done.8.others = f32[3,4,16,128]{3,2,1,0:T(8,128)S(1)} collective-permute-done((f32[3,4,16,128]{3,2,1,0:T(8,128)S(1)}, f32[3,4,16,128]{3,2,1,0:T(8,128)S(1)}, u32[]{:S(2)}, u32[]{:S(2)}) %collective-permute-start.8) | collective-permute-done | bytes 98336 | tf_op jit(solution)/shard_map/ppermute | solution.py:426
  52.9 1.8 %correct.1 = f32[1,4,4,64,128]{4,3,2,1,0:T(8,128)} custom-call(f32[3,4,16,128]{3,2,1,0:T(8,128)S(1)} %bitcast.2, f32[3,4,16,128]{3,2,1,0:T(8,128)S(1)} %collective-permute-done.8.others, f32[16,128]{1,0:T(8,128)S(1)} %guess_old.1.guess, f32[16,8,8,128]{3,2,1,0:T(8,128)S(1)} %get-tuple-element.20.fine_end), custom_call_target="tpu_custom_call" | custom-call | tf_op jit(solution)/shard_map/correct/pallas_call | solution.py:427
  (7 shorter events, 0.1 us)
Async XLA Ops:
  0.0 1.0 %copy-start = (f32[1,4,4,64,128]{4,3,2,1,0:T(8,128)S(1)}, f32[1,4,4,64,128]{4,3,2,1,0:T(8,128)}, u32[]{:S(2)}) copy-start(f32[1,4,4,64,128]{4,3,2,1,0:T(8,128)} %starts.1) | copy-start | bytes 1572868
  1.0 0.9 %copy-start.1 = (s32[4,64,128]{2,1,0:T(8,128)S(1)}, s32[4,64,128]{2,1,0:T(8,128)}, u32[]{:S(2)}) copy-start(s32[4,64,128]{2,1,0:T(8,128)} %flags.1) | copy-start | bytes 393220
  2.3 7.7 %collective-permute-start.2 = (f32[9,8,8,128]{3,2,1,0:T(8,128)S(1)}, f32[9,8,8,128]{3,2,1,0:T(8,128)S(1)}, u32[]{:S(2)}, u32[]{:S(2)}) collective-permute-start(f32[9,8,8,128]{3,2,1,0:T(8,128)S(1)} %get-tuple-element.14.own_two), channel_id=1, source_target_pairs={{0,1},{1,2},{2,3},{3,7},{7,6},{6,5},{5,4},{4,0},{8,9},{9,10},{10,1... | collective-permute-start | bytes 884744 | tf_op jit(solution)/shard_map/ppermute | solution.py:363
  2.8 7.3 %collective-permute-start.1 = (f32[10,8,8,128]{3,2,1,0:T(8,128)S(1)}, f32[10,8,8,128]{3,2,1,0:T(8,128)S(1)}, u32[]{:S(2)}, u32[]{:S(2)}) collective-permute-start(f32[10,8,8,128]{3,2,1,0:T(8,128)S(1)} %get-tuple-element.13.own_one), channel_id=1, source_target_pairs={{0,0},{1,2},{2,1},{3,4},{4,3},{5,6},{6,5},{7,7},{8,8},{9,10},{10,9... | collective-permute-start | bytes 983048 | tf_op jit(solution)/shard_map/ppermute | solution.py:364
  3.5 6.7 %collective-permute-start = (f32[10,8,8,128]{3,2,1,0:T(8,128)S(1)}, f32[10,8,8,128]{3,2,1,0:T(8,128)S(1)}, u32[]{:S(2)}, u32[]{:S(2)}) collective-permute-start(f32[10,8,8,128]{3,2,1,0:T(8,128)S(1)} %get-tuple-element.13.own_one), channel_id=1, source_target_pairs={{0,1},{1,0},{2,3},{3,2},{4,5},{5,4},{6,7},{7,6},{8,9},{9,8},{10,11... | collective-permute-start | bytes 983048 | tf_op jit(solution)/shard_map/ppermute | solution.py:365
  10.1 5.6 %collective-permute-start.3 = (f32[9,8,8,128]{3,2,1,0:T(8,128)S(1)}, f32[9,8,8,128]{3,2,1,0:T(8,128)S(1)}, u32[]{:S(2)}, u32[]{:S(2)}) collective-permute-start(f32[9,8,8,128]{3,2,1,0:T(8,128)S(1)} %broadcast_select_fusion), channel_id=1, source_target_pairs={{3,2},{2,1},{1,0},{0,3},{4,5},{5,6},{6,7},{7,4},{11,10},{10,9},{9,... | collective-permute-start | bytes 884744 | tf_op jit(solution)/shard_map/ppermute | solution.py:369
  18.4 7.0 %collective-permute-start.6 = (f32[8,8,8,128]{3,2,1,0:T(8,128)S(1)}, f32[8,8,8,128]{3,2,1,0:T(8,128)S(1)}, u32[]{:S(2)}, u32[]{:S(2)}) collective-permute-start(f32[8,8,8,128]{3,2,1,0:T(8,128)S(1)} %get-tuple-element.17.own_two), channel_id=1, source_target_pairs={{0,1},{1,2},{2,3},{3,7},{7,6},{6,5},{5,4},{4,0},{8,9},{9,10},{10,1... | collective-permute-start | bytes 786440 | tf_op jit(solution)/shard_map/ppermute | solution.py:363
  22.5 5.0 %collective-permute-start.5 = (f32[8,8,8,128]{3,2,1,0:T(8,128)S(1)}, f32[8,8,8,128]{3,2,1,0:T(8,128)S(1)}, u32[]{:S(2)}, u32[]{:S(2)}) collective-permute-start(f32[8,8,8,128]{3,2,1,0:T(8,128)S(1)} %get-tuple-element.16.own_one), channel_id=1, source_target_pairs={{0,0},{1,2},{2,1},{3,4},{4,3},{5,6},{6,5},{7,7},{8,8},{9,10},{10,9... | collective-permute-start | bytes 786440 | tf_op jit(solution)/shard_map/ppermute | solution.py:364
  23.1 4.3 %collective-permute-start.4 = (f32[8,8,8,128]{3,2,1,0:T(8,128)S(1)}, f32[8,8,8,128]{3,2,1,0:T(8,128)S(1)}, u32[]{:S(2)}, u32[]{:S(2)}) collective-permute-start(f32[8,8,8,128]{3,2,1,0:T(8,128)S(1)} %get-tuple-element.16.own_one), channel_id=1, source_target_pairs={{0,1},{1,0},{2,3},{3,2},{4,5},{5,4},{6,7},{7,6},{8,9},{9,8},{10,11... | collective-permute-start | bytes 786440 | tf_op jit(solution)/shard_map/ppermute | solution.py:365
  25.4 5.9 %collective-permute-start.7 = (f32[8,8,8,128]{3,2,1,0:T(8,128)S(1)}, f32[8,8,8,128]{3,2,1,0:T(8,128)S(1)}, u32[]{:S(2)}, u32[]{:S(2)}) collective-permute-start(f32[8,8,8,128]{3,2,1,0:T(8,128)S(1)} %broadcast_select_fusion.1), channel_id=1, source_target_pairs={{3,2},{2,1},{1,0},{0,3},{4,5},{5,6},{6,7},{7,4},{11,10},{10,9},{9,... | collective-permute-start | bytes 786440 | tf_op jit(solution)/shard_map/ppermute | solution.py:369
  51.5 1.4 %collective-permute-start.8 = (f32[3,4,16,128]{3,2,1,0:T(8,128)S(1)}, f32[3,4,16,128]{3,2,1,0:T(8,128)S(1)}, u32[]{:S(2)}, u32[]{:S(2)}) collective-permute-start(f32[3,4,16,128]{3,2,1,0:T(8,128)S(1)} %bitcast.1), channel_id=1, source_target_pairs={{0,1},{1,0},{2,3},{3,2},{4,5},{5,4},{6,7},{7,6},{8,9},{9,8},{10,11... | collective-permute-start | bytes 294920 | tf_op jit(solution)/shard_map/ppermute | solution.py:426

commit v10 on v9

--- a/solution.py
+++ b/solution.py
@@ -288,8 +288,8 @@
         jump[k] = jumped
 
 
-def correct_kernel(jumps, others, guess, fine_end, out, grids, result, sems):
-    slices, space_size = jumps.shape[0] + 1, jumps.shape[1] * 2
+def correct_kernel(jumps, guess, fine_end, out, grids, result, sems):
+    slices, space_size = jumps.shape[:2]
     mine = lax.axis_index("tm")
     place = lax.axis_index("space")
     rows = grids.shape[2]
@@ -301,9 +301,8 @@
         m = jnp.maximum(mine - k, 0)
         for j in range(-k, k + 1):
             s = jnp.clip(place + j, 0, space_size - 1)
-            source = jumps if j % 2 == 0 else others
             for f in range(FIELDS):
-                grids[k - 1, f, pl.ds(centre + 4 * j, 4), :] = source[m, s // 2, pl.ds(4 * f, 4), :]
+                grids[k - 1, f, pl.ds(centre + 4 * j, 4), :] = jumps[m, s, pl.ds(4 * f, 4), :]
     state = None
     for k in range(slices - 1, -1, -1):
         ended = state
@@ -413,21 +412,19 @@
     )(*opening[:2], *opening_near)
     fine_end, jump = pl.pallas_call(
         functools.partial(second_kernel, space_size),
-        out_shape=(shaped(PACKED, TILES, 8, NZ), shaped(slices * space_size // 2, PACKED, NZ)),
+        out_shape=(shaped(PACKED, TILES, 8, NZ), shaped(slices * space_size, PACKED, NZ)),
         in_specs=[VMEM] * 8,
         out_specs=(VMEM, VMEM),
         scratch_shapes=buffers,
         compiler_params=params(),
         name="second_round",
     )(*middle, *middle_near, keep, guess)
-    members = [range(core, slices * space_size, 2) for core in range(2)]
-    jumps = lax.all_to_all(jump, ("tm", "space"), 0, 0, axis_index_groups=[list(group) for group in members])
-    jumps = jumps.reshape(slices, space_size // 2, PACKED, NZ)[: slices - 1]
-    others = lax.ppermute(jumps, "space", [(i, i ^ 1) for i in range(space_size)])
+    jumps = lax.all_to_all(jump, ("tm", "space"), 0, 0)
+    jumps = jumps.reshape(slices, space_size, PACKED, NZ)
     return pl.pallas_call(
         correct_kernel,
         out_shape=shaped(1, FIELDS, PLANES, NY, NZ),
-        in_specs=[VMEM] * 4,
+        in_specs=[VMEM] * 3,
         out_specs=pl.BlockSpec(memory_space=pltpu.HBM),
         scratch_shapes=[
             pltpu.VMEM((slices - 1, FIELDS, 8 * slices, NZ), F32),
@@ -436,7 +433,7 @@
         ],
         compiler_params=params(),
         name="correct",
-    )(jumps, others, guess, fine_end)
+    )(jumps, guess, fine_end)
 
 
 def solution(mesh):

time: 54.9 us -> 55.3 us (level)
  blocking collectives: 17.1 us -> 18.9 us
  waiting for transfers between devices: 14.1 us -> 12.8 us
    all_to_all x1, blocking collectives: 17.1 us -> 18.9 us  [local(): jumps = lax.all_to_all(jump, ('tm', 'space'), 0, 0)]
    ppermute x1 -> x0, waiting for transfers between devices: 1.29 us -> none  [local(): lax.ppermute(jumps, 'space', [(i, i ^ 1) for i in range(space_size)])]
  transfers between devices with their start and end apart: 9 -> 8, of which waited for: 5 -> 4; matrix products, arithmetic and copies ran while one was open for 0% -> 0% of each run, Pallas kernels for 2% -> 2%
where the time goes in v10:
time: 55.3 us; the launch traced here: 55.1 us
  blocking collectives  18.9 us (34%)
  waiting for transfers between devices  12.8 us (23%)
  starting transfers between devices  12.2 us (22%)
  Pallas kernels  9.05 us (16%)
  local copies, waits for them, and re-layouts  1.94 us (4%)
    all_to_all x1, blocking collectives, local(): jumps = lax.all_to_all(jump, ('tm', 'space'), 0, 0)  18.9 us
    ppermute x2, waiting for transfers between devices, exchange(): y = lax.ppermute(two_y, 'space', second)  9.31 us
    ppermute x2, starting transfers between devices, exchange(): within = lax.ppermute(one, 'space', inner)  5.25 us
    ppermute x2, starting transfers between devices, exchange(): x = lax.ppermute(two_x, 'space', first)  4.6 us
    ppermute x2, waiting for transfers between devices, exchange(): x = lax.ppermute(two_x, 'space', first)  3.49 us
    pallas_call x1, Pallas kernels, local(): pl.pallas_call(functools.partial(second_kernel, space_size), out_shape=(s...  3.06 us
    pallas_call x1, Pallas kernels, local(): pl.pallas_call(functools.partial(first_kernel, space_size), out_shape=(ha...  2.72 us
    unnamed x4, local copies, waits for them, and re-layouts  1.94 us
  transfers between devices with their start and end apart: 8, of which 4 were waited for; matrix products, arithmetic and copies ran while one was open for 0% of the time, Pallas kernels for 2%

profile of v10, /device:TPU:0, one launch (start us, length us, event | category | flops | bytes accessed | tf_op | source)
XLA Modules:
  0.0 55.1 jit_solution(18102004225581098773)
XLA Ops:
  0.0 1.0 %copy-done = f32[1,4,4,64,128]{4,3,2,1,0:T(8,128)S(1)} copy-done((f32[1,4,4,64,128]{4,3,2,1,0:T(8,128)S(1)}, f32[1,4,4,64,128]{4,3,2,1,0:T(8,128)}, u32[]{:S(2)}) %copy-start) | copy-done | bytes 524312
  1.0 0.9 %copy-done.1 = s32[4,64,128]{2,1,0:T(8,128)S(1)} copy-done((s32[4,64,128]{2,1,0:T(8,128)S(1)}, s32[4,64,128]{2,1,0:T(8,128)}, u32[]{:S(2)}) %copy-start.1) | copy-done | bytes 131096
  1.9 0.4 prepare.1
  2.3 0.5 collective-permute-start.2
  2.8 0.7 %collective-permute-start.1 = (f32[10,8,8,128]{3,2,1,0:T(8,128)S(1)}, f32[10,8,8,128]{3,2,1,0:T(8,128)S(1)}, u32[]{:S(2)}, u32[]{:S(2)}) collective-permute-start(f32[10,8,8,128]{3,2,1,0:T(8,128)S(1)} %get-tuple-element.13.own_one), channel_id=1, source_target_pairs={{0,0},{1,2},{2,1},{3,4},{4,3},{5,6},{6,5},{7,7},{8,8},{9,10},{10,9... | collective-permute-start | bytes 983048 | tf_op jit(solution)/shard_map/ppermute | solution.py:363
  3.5 3.9 %collective-permute-start = (f32[10,8,8,128]{3,2,1,0:T(8,128)S(1)}, f32[10,8,8,128]{3,2,1,0:T(8,128)S(1)}, u32[]{:S(2)}, u32[]{:S(2)}) collective-permute-start(f32[10,8,8,128]{3,2,1,0:T(8,128)S(1)} %get-tuple-element.13.own_one), channel_id=1, source_target_pairs={{0,1},{1,0},{2,3},{3,2},{4,5},{5,4},{6,7},{7,6},{8,9},{9,8},{10,11... | collective-permute-start | bytes 983048 | tf_op jit(solution)/shard_map/ppermute | solution.py:364
  7.4 2.6 %collective-permute-done.2.x = f32[9,8,8,128]{3,2,1,0:T(8,128)S(1)} collective-permute-done((f32[9,8,8,128]{3,2,1,0:T(8,128)S(1)}, f32[9,8,8,128]{3,2,1,0:T(8,128)S(1)}, u32[]{:S(2)}, u32[]{:S(2)}) %collective-permute-start.2) | collective-permute-done | bytes 294944 | tf_op jit(solution)/shard_map/ppermute | solution.py:362
  10.1 0.1 collective-permute-start.3
  10.1 0.0 collective-permute-done.1.outer
  10.2 0.0 collective-permute-done.inner
  10.2 5.5 %collective-permute-done.3.y = f32[9,8,8,128]{3,2,1,0:T(8,128)S(1)} collective-permute-done((f32[9,8,8,128]{3,2,1,0:T(8,128)S(1)}, f32[9,8,8,128]{3,2,1,0:T(8,128)S(1)}, u32[]{:S(2)}, u32[]{:S(2)}) %collective-permute-start.3) | collective-permute-done | bytes 294944 | tf_op jit(solution)/shard_map/ppermute | solution.py:368
  15.7 2.7 %first_round.1 = (f32[8,8,8,128]{3,2,1,0:T(8,128)S(1)}, f32[8,8,8,128]{3,2,1,0:T(8,128)S(1)}, f32[2,12,8,8,128]{4,3,2,1,0:T(8,128)S(1)}) custom-call(f32[10,8,8,128]{3,2,1,0:T(8,128)S(1)} %get-tuple-element.13.own_one, f32[9,8,8,128]{3,2,1,0:T(8,128)S(1)} %get-tuple-element.14.own_two, f32[9,8,8,128]{3,2,1,0:T(8,128)S(1)} %get-tuple-element.15.own_other, ...), custom_call_target="tpu_custom_call" | custom-call | tf_op jit(solution)/shard_map/first_round/pallas_call | solution.py:395
  18.4 4.1 %collective-permute-start.6 = (f32[8,8,8,128]{3,2,1,0:T(8,128)S(1)}, f32[8,8,8,128]{3,2,1,0:T(8,128)S(1)}, u32[]{:S(2)}, u32[]{:S(2)}) collective-permute-start(f32[8,8,8,128]{3,2,1,0:T(8,128)S(1)} %get-tuple-element.17.own_two), channel_id=1, source_target_pairs={{0,1},{1,2},{2,3},{3,7},{7,6},{6,5},{5,4},{4,0},{8,9},{9,10},{10,1... | collective-permute-start | bytes 786440 | tf_op jit(solution)/shard_map/ppermute | solution.py:362
  22.5 0.7 %collective-permute-start.5 = (f32[8,8,8,128]{3,2,1,0:T(8,128)S(1)}, f32[8,8,8,128]{3,2,1,0:T(8,128)S(1)}, u32[]{:S(2)}, u32[]{:S(2)}) collective-permute-start(f32[8,8,8,128]{3,2,1,0:T(8,128)S(1)} %get-tuple-element.16.own_one), channel_id=1, source_target_pairs={{0,0},{1,2},{2,1},{3,4},{4,3},{5,6},{6,5},{7,7},{8,8},{9,10},{10,9... | collective-permute-start | bytes 786440 | tf_op jit(solution)/shard_map/ppermute | solution.py:363
  23.1 1.3 %collective-permute-start.4 = (f32[8,8,8,128]{3,2,1,0:T(8,128)S(1)}, f32[8,8,8,128]{3,2,1,0:T(8,128)S(1)}, u32[]{:S(2)}, u32[]{:S(2)}) collective-permute-start(f32[8,8,8,128]{3,2,1,0:T(8,128)S(1)} %get-tuple-element.16.own_one), channel_id=1, source_target_pairs={{0,1},{1,0},{2,3},{3,2},{4,5},{5,4},{6,7},{7,6},{8,9},{9,8},{10,11... | collective-permute-start | bytes 786440 | tf_op jit(solution)/shard_map/ppermute | solution.py:364
  24.5 0.9 %collective-permute-done.6.x = f32[8,8,8,128]{3,2,1,0:T(8,128)S(1)} collective-permute-done((f32[8,8,8,128]{3,2,1,0:T(8,128)S(1)}, f32[8,8,8,128]{3,2,1,0:T(8,128)S(1)}, u32[]{:S(2)}, u32[]{:S(2)}) %collective-permute-start.6) | collective-permute-done | bytes 262176 | tf_op jit(solution)/shard_map/ppermute | solution.py:362
  25.4 0.9 %collective-permute-start.7 = (f32[8,8,8,128]{3,2,1,0:T(8,128)S(1)}, f32[8,8,8,128]{3,2,1,0:T(8,128)S(1)}, u32[]{:S(2)}, u32[]{:S(2)}) collective-permute-start(f32[8,8,8,128]{3,2,1,0:T(8,128)S(1)} %broadcast_select_fusion.1), channel_id=1, source_target_pairs={{3,2},{2,1},{1,0},{0,3},{4,5},{5,6},{6,7},{7,4},{11,10},{10,9},{9,... | collective-permute-start | bytes 786440 | tf_op jit(solution)/shard_map/ppermute | solution.py:368
  26.3 1.1 %guess_old.1.guess = f32[16,128]{1,0:T(8,128)S(1)} custom-call(f32[10,8,8,128]{3,2,1,0:T(8,128)S(1)} %get-tuple-element.13.own_one, f32[9,8,8,128]{3,2,1,0:T(8,128)S(1)} %get-tuple-element.14.own_two, f32[10,8,8,128]{3,2,1,0:T(8,128)S(1)} %collective-permute-done.inner, f32[10,8,8,128]{3,2,1,0:T(8,128)S(1)} %collective-permute-done.1.outer, ...), custom_call_target="tpu_custom_call" | custom-call | tf_op jit(solution)/shard_map/guess_old/pallas_call | solution.py:405
  27.4 0.0 collective-permute-done.5.outer
  27.4 0.0 collective-permute-done.4.inner
  27.5 3.8 %collective-permute-done.7.y = f32[8,8,8,128]{3,2,1,0:T(8,128)S(1)} collective-permute-done((f32[8,8,8,128]{3,2,1,0:T(8,128)S(1)}, f32[8,8,8,128]{3,2,1,0:T(8,128)S(1)}, u32[]{:S(2)}, u32[]{:S(2)}) %collective-permute-start.7) | collective-permute-done | bytes 262176 | tf_op jit(solution)/shard_map/ppermute | solution.py:368
  31.3 3.1 %second_round.1 = (f32[16,8,8,128]{3,2,1,0:T(8,128)S(1)}, f32[32,16,128]{2,1,0:T(8,128)S(1)}) custom-call(f32[8,8,8,128]{3,2,1,0:T(8,128)S(1)} %get-tuple-element.16.own_one, f32[8,8,8,128]{3,2,1,0:T(8,128)S(1)} %get-tuple-element.17.own_two, f32[8,8,8,128]{3,2,1,0:T(8,128)S(1)} %collective-permute-done.4.inner, ...), custom_call_target="tpu_custom_call" | custom-call | tf_op jit(solution)/shard_map/second_round/pallas_call | solution.py:413
  34.4 18.9 %all_to_all.5 = f32[32,16,128]{2,1,0:T(8,128)S(1)} all-to-all(f32[32,16,128]{2,1,0:T(8,128)S(1)} %get-tuple-element.19), channel_id=1, replica_groups=mesh['tm'=4,'space'=8] {'tm','space'}, dimensions={0} | all-to-all | bytes 524288 | tf_op jit(solution)/shard_map/all_to_all | solution.py:422
  53.3 1.8 %correct.1 = f32[1,4,4,64,128]{4,3,2,1,0:T(8,128)} custom-call(f32[4,8,16,128]{3,2,1,0:T(8,128)S(1)} %bitcast.1, f32[16,128]{1,0:T(8,128)S(1)} %guess_old.1.guess, f32[16,8,8,128]{3,2,1,0:T(8,128)S(1)} %get-tuple-element.20.fine_end), custom_call_target="tpu_custom_call" | custom-call | tf_op jit(solution)/shard_map/correct/pallas_call | solution.py:424
  (4 shorter events, 0.1 us)
Async XLA Ops:
  0.0 1.0 %copy-start = (f32[1,4,4,64,128]{4,3,2,1,0:T(8,128)S(1)}, f32[1,4,4,64,128]{4,3,2,1,0:T(8,128)}, u32[]{:S(2)}) copy-start(f32[1,4,4,64,128]{4,3,2,1,0:T(8,128)} %starts.1) | copy-start | bytes 1572868
  1.0 0.9 %copy-start.1 = (s32[4,64,128]{2,1,0:T(8,128)S(1)}, s32[4,64,128]{2,1,0:T(8,128)}, u32[]{:S(2)}) copy-start(s32[4,64,128]{2,1,0:T(8,128)} %flags.1) | copy-start | bytes 393220
  2.3 7.7 %collective-permute-start.2 = (f32[9,8,8,128]{3,2,1,0:T(8,128)S(1)}, f32[9,8,8,128]{3,2,1,0:T(8,128)S(1)}, u32[]{:S(2)}, u32[]{:S(2)}) collective-permute-start(f32[9,8,8,128]{3,2,1,0:T(8,128)S(1)} %get-tuple-element.14.own_two), channel_id=1, source_target_pairs={{0,1},{1,2},{2,3},{3,7},{7,6},{6,5},{5,4},{4,0},{8,9},{9,10},{10,1... | collective-permute-start | bytes 884744 | tf_op jit(solution)/shard_map/ppermute | solution.py:362
  2.8 7.3 %collective-permute-start.1 = (f32[10,8,8,128]{3,2,1,0:T(8,128)S(1)}, f32[10,8,8,128]{3,2,1,0:T(8,128)S(1)}, u32[]{:S(2)}, u32[]{:S(2)}) collective-permute-start(f32[10,8,8,128]{3,2,1,0:T(8,128)S(1)} %get-tuple-element.13.own_one), channel_id=1, source_target_pairs={{0,0},{1,2},{2,1},{3,4},{4,3},{5,6},{6,5},{7,7},{8,8},{9,10},{10,9... | collective-permute-start | bytes 983048 | tf_op jit(solution)/shard_map/ppermute | solution.py:363
  3.5 6.7 %collective-permute-start = (f32[10,8,8,128]{3,2,1,0:T(8,128)S(1)}, f32[10,8,8,128]{3,2,1,0:T(8,128)S(1)}, u32[]{:S(2)}, u32[]{:S(2)}) collective-permute-start(f32[10,8,8,128]{3,2,1,0:T(8,128)S(1)} %get-tuple-element.13.own_one), channel_id=1, source_target_pairs={{0,1},{1,0},{2,3},{3,2},{4,5},{5,4},{6,7},{7,6},{8,9},{9,8},{10,11... | collective-permute-start | bytes 983048 | tf_op jit(solution)/shard_map/ppermute | solution.py:364
  10.1 5.6 %collective-permute-start.3 = (f32[9,8,8,128]{3,2,1,0:T(8,128)S(1)}, f32[9,8,8,128]{3,2,1,0:T(8,128)S(1)}, u32[]{:S(2)}, u32[]{:S(2)}) collective-permute-start(f32[9,8,8,128]{3,2,1,0:T(8,128)S(1)} %broadcast_select_fusion), channel_id=1, source_target_pairs={{3,2},{2,1},{1,0},{0,3},{4,5},{5,6},{6,7},{7,4},{11,10},{10,9},{9,... | collective-permute-start | bytes 884744 | tf_op jit(solution)/shard_map/ppermute | solution.py:368
  18.4 7.0 %collective-permute-start.6 = (f32[8,8,8,128]{3,2,1,0:T(8,128)S(1)}, f32[8,8,8,128]{3,2,1,0:T(8,128)S(1)}, u32[]{:S(2)}, u32[]{:S(2)}) collective-permute-start(f32[8,8,8,128]{3,2,1,0:T(8,128)S(1)} %get-tuple-element.17.own_two), channel_id=1, source_target_pairs={{0,1},{1,2},{2,3},{3,7},{7,6},{6,5},{5,4},{4,0},{8,9},{9,10},{10,1... | collective-permute-start | bytes 786440 | tf_op jit(solution)/shard_map/ppermute | solution.py:362
  22.5 5.0 %collective-permute-start.5 = (f32[8,8,8,128]{3,2,1,0:T(8,128)S(1)}, f32[8,8,8,128]{3,2,1,0:T(8,128)S(1)}, u32[]{:S(2)}, u32[]{:S(2)}) collective-permute-start(f32[8,8,8,128]{3,2,1,0:T(8,128)S(1)} %get-tuple-element.16.own_one), channel_id=1, source_target_pairs={{0,0},{1,2},{2,1},{3,4},{4,3},{5,6},{6,5},{7,7},{8,8},{9,10},{10,9... | collective-permute-start | bytes 786440 | tf_op jit(solution)/shard_map/ppermute | solution.py:363
  23.1 4.3 %collective-permute-start.4 = (f32[8,8,8,128]{3,2,1,0:T(8,128)S(1)}, f32[8,8,8,128]{3,2,1,0:T(8,128)S(1)}, u32[]{:S(2)}, u32[]{:S(2)}) collective-permute-start(f32[8,8,8,128]{3,2,1,0:T(8,128)S(1)} %get-tuple-element.16.own_one), channel_id=1, source_target_pairs={{0,1},{1,0},{2,3},{3,2},{4,5},{5,4},{6,7},{7,6},{8,9},{9,8},{10,11... | collective-permute-start | bytes 786440 | tf_op jit(solution)/shard_map/ppermute | solution.py:364
  25.4 5.9 %collective-permute-start.7 = (f32[8,8,8,128]{3,2,1,0:T(8,128)S(1)}, f32[8,8,8,128]{3,2,1,0:T(8,128)S(1)}, u32[]{:S(2)}, u32[]{:S(2)}) collective-permute-start(f32[8,8,8,128]{3,2,1,0:T(8,128)S(1)} %broadcast_select_fusion.1), channel_id=1, source_target_pairs={{3,2},{2,1},{1,0},{0,3},{4,5},{5,6},{6,7},{7,4},{11,10},{10,9},{9,... | collective-permute-start | bytes 786440 | tf_op jit(solution)/shard_map/ppermute | solution.py:368

commit v11 on v9

--- a/solution.py
+++ b/solution.py
@@ -142,19 +142,12 @@
 
     for step in range(ROUND):
         src, dst = (even, odd) if step % 2 == 0 else (odd, even)
-        many = PLANES + ROUND // 2 - 1 - step
-
-        def body(i, carry, src=src, dst=dst, step=step, many=many):
-            for k in range(many):
-                p = step + 1 + i * many + k
-                if step == ROUND - 1:
-                    store = lambda f, t, value: finish(f, p - PLANES, t, value)
-                else:
-                    store = lambda f, t, value: put_tile(dst, f, p, t, value)
-                fine_plane(src, keep, p, inside(space_size, p), store)
-            return carry
-
-        lax.fori_loop(0, 2, body, 0)
+        for p in range(step + 1, WINDOW - 1 - step):
+            if step == ROUND - 1:
+                store = lambda f, t, value: finish(f, p - PLANES, t, value)
+            else:
+                store = lambda f, t, value: put_tile(dst, f, p, t, value)
+            fine_plane(src, keep, p, inside(space_size, p), store)
 
 
 def first_kernel(space_size, own_one, own_two, own_other, inner, outer, x, y, ended_one, ended_two, keep, even, odd):

time: 54.9 us -> 53.6 us (0.976)
  Pallas kernels: 9.05 us -> 7.79 us
    pallas_call x1, Pallas kernels: 2.72 us -> 2.06 us  [local(): pl.pallas_call(functools.partial(first_kernel, space_size), out_shape=(ha...]
    pallas_call x1, Pallas kernels: 3.05 us -> 2.45 us  [local(): pl.pallas_call(functools.partial(second_kernel, space_size), out_shape=(s...]
where the time goes in v11:
time: 53.6 us; the launch traced here: 53.4 us
  blocking collectives  17.1 us (32%)
  waiting for transfers between devices  14.1 us (26%)
  starting transfers between devices  12.2 us (23%)
  Pallas kernels  7.79 us (15%)
  local copies, waits for them, and re-layouts  1.95 us (4%)
    all_to_all x1, blocking collectives, local(): lax.all_to_all(jump, ('tm', 'space'), 0, 0, axis_index_groups=[list(group...  17.1 us
    ppermute x2, waiting for transfers between devices, exchange(): y = lax.ppermute(two_y, 'space', second)  9.31 us
    ppermute x2, starting transfers between devices, exchange(): within = lax.ppermute(one, 'space', inner)  5.25 us
    ppermute x2, starting transfers between devices, exchange(): x = lax.ppermute(two_x, 'space', first)  4.6 us
    ppermute x2, waiting for transfers between devices, exchange(): x = lax.ppermute(two_x, 'space', first)  3.49 us
    pallas_call x1, Pallas kernels, local(): pl.pallas_call(functools.partial(second_kernel, space_size), out_shape=(s...  2.45 us
    pallas_call x1, Pallas kernels, local(): pl.pallas_call(functools.partial(first_kernel, space_size), out_shape=(ha...  2.06 us
    unnamed x4, local copies, waits for them, and re-layouts  1.94 us
  transfers between devices with their start and end apart: 9, of which 5 were waited for; matrix products, arithmetic and copies ran while one was open for 0% of the time, Pallas kernels for 2%

profile of v11, /device:TPU:0, one launch (start us, length us, event | category | flops | bytes accessed | tf_op | source)
XLA Modules:
  0.0 53.4 jit_solution(8957911433744317105)
XLA Ops:
  0.0 1.0 %copy-done = f32[1,4,4,64,128]{4,3,2,1,0:T(8,128)S(1)} copy-done((f32[1,4,4,64,128]{4,3,2,1,0:T(8,128)S(1)}, f32[1,4,4,64,128]{4,3,2,1,0:T(8,128)}, u32[]{:S(2)}) %copy-start) | copy-done | bytes 524312
  1.0 0.9 %copy-done.1 = s32[4,64,128]{2,1,0:T(8,128)S(1)} copy-done((s32[4,64,128]{2,1,0:T(8,128)S(1)}, s32[4,64,128]{2,1,0:T(8,128)}, u32[]{:S(2)}) %copy-start.1) | copy-done | bytes 131096
  1.9 0.4 prepare.1
  2.3 0.5 collective-permute-start.2
  2.8 0.7 %collective-permute-start.1 = (f32[10,8,8,128]{3,2,1,0:T(8,128)S(1)}, f32[10,8,8,128]{3,2,1,0:T(8,128)S(1)}, u32[]{:S(2)}, u32[]{:S(2)}) collective-permute-start(f32[10,8,8,128]{3,2,1,0:T(8,128)S(1)} %get-tuple-element.13.own_one), channel_id=1, source_target_pairs={{0,0},{1,2},{2,1},{3,4},{4,3},{5,6},{6,5},{7,7},{8,8},{9,10},{10,9... | collective-permute-start | bytes 983048 | tf_op jit(solution)/shard_map/ppermute | solution.py:357
  3.5 3.9 %collective-permute-start = (f32[10,8,8,128]{3,2,1,0:T(8,128)S(1)}, f32[10,8,8,128]{3,2,1,0:T(8,128)S(1)}, u32[]{:S(2)}, u32[]{:S(2)}) collective-permute-start(f32[10,8,8,128]{3,2,1,0:T(8,128)S(1)} %get-tuple-element.13.own_one), channel_id=1, source_target_pairs={{0,1},{1,0},{2,3},{3,2},{4,5},{5,4},{6,7},{7,6},{8,9},{9,8},{10,11... | collective-permute-start | bytes 983048 | tf_op jit(solution)/shard_map/ppermute | solution.py:358
  7.4 2.6 %collective-permute-done.2.x = f32[9,8,8,128]{3,2,1,0:T(8,128)S(1)} collective-permute-done((f32[9,8,8,128]{3,2,1,0:T(8,128)S(1)}, f32[9,8,8,128]{3,2,1,0:T(8,128)S(1)}, u32[]{:S(2)}, u32[]{:S(2)}) %collective-permute-start.2) | collective-permute-done | bytes 294944 | tf_op jit(solution)/shard_map/ppermute | solution.py:356
  10.1 0.1 collective-permute-start.3
  10.1 0.0 collective-permute-done.1.outer
  10.2 5.5 %collective-permute-done.3.y = f32[9,8,8,128]{3,2,1,0:T(8,128)S(1)} collective-permute-done((f32[9,8,8,128]{3,2,1,0:T(8,128)S(1)}, f32[9,8,8,128]{3,2,1,0:T(8,128)S(1)}, u32[]{:S(2)}, u32[]{:S(2)}) %collective-permute-start.3) | collective-permute-done | bytes 294944 | tf_op jit(solution)/shard_map/ppermute | solution.py:362
  15.7 2.1 %first_round.1 = (f32[8,8,8,128]{3,2,1,0:T(8,128)S(1)}, f32[8,8,8,128]{3,2,1,0:T(8,128)S(1)}, f32[2,12,8,8,128]{4,3,2,1,0:T(8,128)S(1)}) custom-call(f32[10,8,8,128]{3,2,1,0:T(8,128)S(1)} %get-tuple-element.13.own_one, f32[9,8,8,128]{3,2,1,0:T(8,128)S(1)} %get-tuple-element.14.own_two, f32[9,8,8,128]{3,2,1,0:T(8,128)S(1)} %get-tuple-element.15.own_other, ...), custom_call_target="tpu_custom_call" | custom-call | tf_op jit(solution)/shard_map/first_round/pallas_call | solution.py:389
  17.7 4.1 %collective-permute-start.6 = (f32[8,8,8,128]{3,2,1,0:T(8,128)S(1)}, f32[8,8,8,128]{3,2,1,0:T(8,128)S(1)}, u32[]{:S(2)}, u32[]{:S(2)}) collective-permute-start(f32[8,8,8,128]{3,2,1,0:T(8,128)S(1)} %get-tuple-element.17.own_two), channel_id=1, source_target_pairs={{0,1},{1,2},{2,3},{3,7},{7,6},{6,5},{5,4},{4,0},{8,9},{9,10},{10,1... | collective-permute-start | bytes 786440 | tf_op jit(solution)/shard_map/ppermute | solution.py:356
  21.8 0.7 %collective-permute-start.5 = (f32[8,8,8,128]{3,2,1,0:T(8,128)S(1)}, f32[8,8,8,128]{3,2,1,0:T(8,128)S(1)}, u32[]{:S(2)}, u32[]{:S(2)}) collective-permute-start(f32[8,8,8,128]{3,2,1,0:T(8,128)S(1)} %get-tuple-element.16.own_one), channel_id=1, source_target_pairs={{0,0},{1,2},{2,1},{3,4},{4,3},{5,6},{6,5},{7,7},{8,8},{9,10},{10,9... | collective-permute-start | bytes 786440 | tf_op jit(solution)/shard_map/ppermute | solution.py:357
  22.5 1.3 %collective-permute-start.4 = (f32[8,8,8,128]{3,2,1,0:T(8,128)S(1)}, f32[8,8,8,128]{3,2,1,0:T(8,128)S(1)}, u32[]{:S(2)}, u32[]{:S(2)}) collective-permute-start(f32[8,8,8,128]{3,2,1,0:T(8,128)S(1)} %get-tuple-element.16.own_one), channel_id=1, source_target_pairs={{0,1},{1,0},{2,3},{3,2},{4,5},{5,4},{6,7},{7,6},{8,9},{9,8},{10,11... | collective-permute-start | bytes 786440 | tf_op jit(solution)/shard_map/ppermute | solution.py:358
  23.8 0.9 %collective-permute-done.6.x = f32[8,8,8,128]{3,2,1,0:T(8,128)S(1)} collective-permute-done((f32[8,8,8,128]{3,2,1,0:T(8,128)S(1)}, f32[8,8,8,128]{3,2,1,0:T(8,128)S(1)}, u32[]{:S(2)}, u32[]{:S(2)}) %collective-permute-start.6) | collective-permute-done | bytes 262176 | tf_op jit(solution)/shard_map/ppermute | solution.py:356
  24.7 0.9 %collective-permute-start.7 = (f32[8,8,8,128]{3,2,1,0:T(8,128)S(1)}, f32[8,8,8,128]{3,2,1,0:T(8,128)S(1)}, u32[]{:S(2)}, u32[]{:S(2)}) collective-permute-start(f32[8,8,8,128]{3,2,1,0:T(8,128)S(1)} %broadcast_select_fusion.1), channel_id=1, source_target_pairs={{3,2},{2,1},{1,0},{0,3},{4,5},{5,6},{6,7},{7,4},{11,10},{10,9},{9,... | collective-permute-start | bytes 786440 | tf_op jit(solution)/shard_map/ppermute | solution.py:362
  25.6 1.1 %guess_old.1.guess = f32[16,128]{1,0:T(8,128)S(1)} custom-call(f32[10,8,8,128]{3,2,1,0:T(8,128)S(1)} %get-tuple-element.13.own_one, f32[9,8,8,128]{3,2,1,0:T(8,128)S(1)} %get-tuple-element.14.own_two, f32[10,8,8,128]{3,2,1,0:T(8,128)S(1)} %collective-permute-done.inner, f32[10,8,8,128]{3,2,1,0:T(8,128)S(1)} %collective-permute-done.1.outer, ...), custom_call_target="tpu_custom_call" | custom-call | tf_op jit(solution)/shard_map/guess_old/pallas_call | solution.py:399
  26.8 0.0 collective-permute-done.4.inner
  26.8 3.8 %collective-permute-done.7.y = f32[8,8,8,128]{3,2,1,0:T(8,128)S(1)} collective-permute-done((f32[8,8,8,128]{3,2,1,0:T(8,128)S(1)}, f32[8,8,8,128]{3,2,1,0:T(8,128)S(1)}, u32[]{:S(2)}, u32[]{:S(2)}) %collective-permute-start.7) | collective-permute-done | bytes 262176 | tf_op jit(solution)/shard_map/ppermute | solution.py:362
  30.6 2.5 %second_round.1 = (f32[16,8,8,128]{3,2,1,0:T(8,128)S(1)}, f32[16,16,128]{2,1,0:T(8,128)S(1)}) custom-call(f32[8,8,8,128]{3,2,1,0:T(8,128)S(1)} %get-tuple-element.16.own_one, f32[8,8,8,128]{3,2,1,0:T(8,128)S(1)} %get-tuple-element.17.own_two, f32[8,8,8,128]{3,2,1,0:T(8,128)S(1)} %collective-permute-done.4.inner, ...), custom_call_target="tpu_custom_call" | custom-call | tf_op jit(solution)/shard_map/second_round/pallas_call | solution.py:407
  33.1 17.1 %all_to_all.5 = f32[16,16,128]{2,1,0:T(8,128)S(1)} all-to-all(f32[16,16,128]{2,1,0:T(8,128)S(1)} %get-tuple-element.19), channel_id=1, replica_groups={{0,2,4,6,8,10,12,14,16,18,20,22,24,26,28,30},{1,3,5,7,9,11,13,15,17,19,..., dimensions={0} | all-to-all | bytes 262144 | tf_op jit(solution)/shard_map/all_to_all | solution.py:417
  50.2 0.1 collective-permute-start.8
  50.3 1.3 %collective-permute-done.8.others = f32[3,4,16,128]{3,2,1,0:T(8,128)S(1)} collective-permute-done((f32[3,4,16,128]{3,2,1,0:T(8,128)S(1)}, f32[3,4,16,128]{3,2,1,0:T(8,128)S(1)}, u32[]{:S(2)}, u32[]{:S(2)}) %collective-permute-start.8) | collective-permute-done | bytes 98336 | tf_op jit(solution)/shard_map/ppermute | solution.py:419
  51.6 1.8 %correct.1 = f32[1,4,4,64,128]{4,3,2,1,0:T(8,128)} custom-call(f32[3,4,16,128]{3,2,1,0:T(8,128)S(1)} %bitcast.2, f32[3,4,16,128]{3,2,1,0:T(8,128)S(1)} %collective-permute-done.8.others, f32[16,128]{1,0:T(8,128)S(1)} %guess_old.1.guess, f32[16,8,8,128]{3,2,1,0:T(8,128)S(1)} %get-tuple-element.20.fine_end), custom_call_target="tpu_custom_call" | custom-call | tf_op jit(solution)/shard_map/correct/pallas_call | solution.py:420
  (7 shorter events, 0.1 us)
Async XLA Ops:
  0.0 1.0 %copy-start = (f32[1,4,4,64,128]{4,3,2,1,0:T(8,128)S(1)}, f32[1,4,4,64,128]{4,3,2,1,0:T(8,128)}, u32[]{:S(2)}) copy-start(f32[1,4,4,64,128]{4,3,2,1,0:T(8,128)} %starts.1) | copy-start | bytes 1572868
  1.0 0.9 %copy-start.1 = (s32[4,64,128]{2,1,0:T(8,128)S(1)}, s32[4,64,128]{2,1,0:T(8,128)}, u32[]{:S(2)}) copy-start(s32[4,64,128]{2,1,0:T(8,128)} %flags.1) | copy-start | bytes 393220
  2.3 7.7 %collective-permute-start.2 = (f32[9,8,8,128]{3,2,1,0:T(8,128)S(1)}, f32[9,8,8,128]{3,2,1,0:T(8,128)S(1)}, u32[]{:S(2)}, u32[]{:S(2)}) collective-permute-start(f32[9,8,8,128]{3,2,1,0:T(8,128)S(1)} %get-tuple-element.14.own_two), channel_id=1, source_target_pairs={{0,1},{1,2},{2,3},{3,7},{7,6},{6,5},{5,4},{4,0},{8,9},{9,10},{10,1... | collective-permute-start | bytes 884744 | tf_op jit(solution)/shard_map/ppermute | solution.py:356
  2.8 7.3 %collective-permute-start.1 = (f32[10,8,8,128]{3,2,1,0:T(8,128)S(1)}, f32[10,8,8,128]{3,2,1,0:T(8,128)S(1)}, u32[]{:S(2)}, u32[]{:S(2)}) collective-permute-start(f32[10,8,8,128]{3,2,1,0:T(8,128)S(1)} %get-tuple-element.13.own_one), channel_id=1, source_target_pairs={{0,0},{1,2},{2,1},{3,4},{4,3},{5,6},{6,5},{7,7},{8,8},{9,10},{10,9... | collective-permute-start | bytes 983048 | tf_op jit(solution)/shard_map/ppermute | solution.py:357
  3.5 6.7 %collective-permute-start = (f32[10,8,8,128]{3,2,1,0:T(8,128)S(1)}, f32[10,8,8,128]{3,2,1,0:T(8,128)S(1)}, u32[]{:S(2)}, u32[]{:S(2)}) collective-permute-start(f32[10,8,8,128]{3,2,1,0:T(8,128)S(1)} %get-tuple-element.13.own_one), channel_id=1, source_target_pairs={{0,1},{1,0},{2,3},{3,2},{4,5},{5,4},{6,7},{7,6},{8,9},{9,8},{10,11... | collective-permute-start | bytes 983048 | tf_op jit(solution)/shard_map/ppermute | solution.py:358
  10.1 5.6 %collective-permute-start.3 = (f32[9,8,8,128]{3,2,1,0:T(8,128)S(1)}, f32[9,8,8,128]{3,2,1,0:T(8,128)S(1)}, u32[]{:S(2)}, u32[]{:S(2)}) collective-permute-start(f32[9,8,8,128]{3,2,1,0:T(8,128)S(1)} %broadcast_select_fusion), channel_id=1, source_target_pairs={{3,2},{2,1},{1,0},{0,3},{4,5},{5,6},{6,7},{7,4},{11,10},{10,9},{9,... | collective-permute-start | bytes 884744 | tf_op jit(solution)/shard_map/ppermute | solution.py:362
  17.7 7.0 %collective-permute-start.6 = (f32[8,8,8,128]{3,2,1,0:T(8,128)S(1)}, f32[8,8,8,128]{3,2,1,0:T(8,128)S(1)}, u32[]{:S(2)}, u32[]{:S(2)}) collective-permute-start(f32[8,8,8,128]{3,2,1,0:T(8,128)S(1)} %get-tuple-element.17.own_two), channel_id=1, source_target_pairs={{0,1},{1,2},{2,3},{3,7},{7,6},{6,5},{5,4},{4,0},{8,9},{9,10},{10,1... | collective-permute-start | bytes 786440 | tf_op jit(solution)/shard_map/ppermute | solution.py:356
  21.8 5.0 %collective-permute-start.5 = (f32[8,8,8,128]{3,2,1,0:T(8,128)S(1)}, f32[8,8,8,128]{3,2,1,0:T(8,128)S(1)}, u32[]{:S(2)}, u32[]{:S(2)}) collective-permute-start(f32[8,8,8,128]{3,2,1,0:T(8,128)S(1)} %get-tuple-element.16.own_one), channel_id=1, source_target_pairs={{0,0},{1,2},{2,1},{3,4},{4,3},{5,6},{6,5},{7,7},{8,8},{9,10},{10,9... | collective-permute-start | bytes 786440 | tf_op jit(solution)/shard_map/ppermute | solution.py:357
  22.5 4.3 %collective-permute-start.4 = (f32[8,8,8,128]{3,2,1,0:T(8,128)S(1)}, f32[8,8,8,128]{3,2,1,0:T(8,128)S(1)}, u32[]{:S(2)}, u32[]{:S(2)}) collective-permute-start(f32[8,8,8,128]{3,2,1,0:T(8,128)S(1)} %get-tuple-element.16.own_one), channel_id=1, source_target_pairs={{0,1},{1,0},{2,3},{3,2},{4,5},{5,4},{6,7},{7,6},{8,9},{9,8},{10,11... | collective-permute-start | bytes 786440 | tf_op jit(solution)/shard_map/ppermute | solution.py:358
  24.7 5.9 %collective-permute-start.7 = (f32[8,8,8,128]{3,2,1,0:T(8,128)S(1)}, f32[8,8,8,128]{3,2,1,0:T(8,128)S(1)}, u32[]{:S(2)}, u32[]{:S(2)}) collective-permute-start(f32[8,8,8,128]{3,2,1,0:T(8,128)S(1)} %broadcast_select_fusion.1), channel_id=1, source_target_pairs={{3,2},{2,1},{1,0},{0,3},{4,5},{5,6},{6,7},{7,4},{11,10},{10,9},{9,... | collective-permute-start | bytes 786440 | tf_op jit(solution)/shard_map/ppermute | solution.py:362
  50.2 1.4 %collective-permute-start.8 = (f32[3,4,16,128]{3,2,1,0:T(8,128)S(1)}, f32[3,4,16,128]{3,2,1,0:T(8,128)S(1)}, u32[]{:S(2)}, u32[]{:S(2)}) collective-permute-start(f32[3,4,16,128]{3,2,1,0:T(8,128)S(1)} %bitcast.1), channel_id=1, source_target_pairs={{0,1},{1,0},{2,3},{3,2},{4,5},{5,4},{6,7},{7,6},{8,9},{9,8},{10,11... | collective-permute-start | bytes 294920 | tf_op jit(solution)/shard_map/ppermute | solution.py:419

commit v12 on v11

--- a/solution.py
+++ b/solution.py
@@ -81,9 +81,9 @@
     kc = jnp.where(valid, fine_dt, 0.0).astype(F32)
     for begin in range(0, TILES, GROUP):
         tiles = range(begin, begin + GROUP)
-        column = [[src[f, p, t] for f in fields] for t in range(begin, begin + GROUP + 2)]
-        lo_x = [[src[f, p - 1, t + 1] for f in fields] for t in tiles]
-        hi_x = [[src[f, p + 1, t + 1] for f in fields] for t in tiles]
+        column = [[src(p)[f, p, t] for f in fields] for t in range(begin, begin + GROUP + 2)]
+        lo_x = [[src(p - 1)[f, p - 1, t + 1] for f in fields] for t in tiles]
+        hi_x = [[src(p + 1)[f, p + 1, t + 1] for f in fields] for t in tiles]
         kept = [(keep[0, p, t], keep[1, p, t]) for t in tiles]
         fresh = [
             fine_tile(column[i + 1], lo_x[i], hi_x[i], column[i], column[i + 2], *kept[i], kc, low_lane, high_lane)
@@ -116,9 +116,11 @@
     def row(self, j, half, k, t):
         if j == 1:
             return self.own[half][k, t]
-        v, other = (ref[k, t] for ref in self.near[half])
-        first = self.from_first[half]
-        v = jnp.where(first, v, other) if j == 0 else jnp.where(first, other, v)
+        refs = self.near[half]
+        v = refs[0][k, t]
+        if refs[1] is not refs[0]:
+            other, first = refs[1][k, t], self.from_first[half]
+            v = jnp.where(first, v, other) if j == 0 else jnp.where(first, other, v)
         return jnp.where(self.there[j], v, 0.0)
 
     def field(self, j, f, x, t):
@@ -133,21 +135,69 @@
     return (x >= 0) & (x < space_size * PLANES)
 
 
-def fine_round(space_size, slabs, even, odd, keep, finish):
-    for j in range(3):
+def fine_load(slabs, sides, even):
+    for j in sides:
         for x in range(PLANES):
             for f in range(FIELDS):
                 for t in range(TILES):
                     put_tile(even, f, j * PLANES + x, t, slabs.field(j, f, x, t))
 
-    for step in range(ROUND):
+
+def fine_planes(space_size, spans, even, odd, keep, finish, source=None):
+    for step, span in enumerate(spans):
         src, dst = (even, odd) if step % 2 == 0 else (odd, even)
-        for p in range(step + 1, WINDOW - 1 - step):
+
+        def read(p, src=src, step=step):
+            found = source(step, p) if source else None
+            return src if found is None else found
+
+        for p in span:
             if step == ROUND - 1:
                 store = lambda f, t, value: finish(f, p - PLANES, t, value)
             else:
                 store = lambda f, t, value: put_tile(dst, f, p, t, value)
-            fine_plane(src, keep, p, inside(space_size, p), store)
+            fine_plane(read, keep, p, inside(space_size, p), store)
+
+
+def fine_round(space_size, slabs, even, odd, keep, finish):
+    fine_load(slabs, range(3), even)
+    spans = [range(step + 1, WINDOW - 1 - step) for step in range(ROUND)]
+    fine_planes(space_size, spans, even, odd, keep, finish)
+
+
+def both_ways(space_size, run):
+    low = lax.axis_index("space") < turn(space_size)
+    pl.when(low)(lambda: run(False))
+    pl.when(jnp.logical_not(low))(lambda: run(True))
+
+
+def seen(span, mirror):
+    return [WINDOW - 1 - p for p in span] if mirror else list(span)
+
+
+def early_kernel(space_size, own_one, own_two, inner, outer, x, keep, even, odd):
+    slabs = Slabs(space_size, (own_one, own_two), (inner, outer, x, x))
+
+    def run(mirror):
+        fine_load(slabs, (2 if mirror else 0, 1), even)
+        spans = [seen(range(1 + step, 2 * PLANES - 1 - step), mirror) for step in range(ROUND - 1)]
+        fine_planes(space_size, spans, even, odd, keep, None)
+
+    both_ways(space_size, run)
+
+
+def late_round(space_size, slabs, early_even, early_odd, even, odd, keep, finish):
+    def run(mirror):
+        fine_load(slabs, (0 if mirror else 2,), even)
+        spans = [seen(range(2 * PLANES - 1 - step, WINDOW - 1 - step), mirror) for step in range(ROUND)]
+
+        def source(step, p):
+            before = seen(range(2 * PLANES - step), mirror)
+            return (early_even if step % 2 == 0 else early_odd) if p in before else None
+
+        fine_planes(space_size, spans, even, odd, keep, finish, source)
+
+    both_ways(space_size, run)
 
 
 def first_kernel(space_size, own_one, own_two, own_other, inner, outer, x, y, ended_one, ended_two, keep, even, odd):
@@ -268,13 +318,13 @@
         guess[pl.ds(4 * f, 4), :] = state[f][4:8]
 
 
-def second_kernel(space_size, own_one, own_two, inner, outer, x, y, keep, guess, fine_end, jump, even, odd):
-    slabs = Slabs(space_size, (own_one, own_two), (inner, outer, x, y))
+def second_kernel(space_size, inner, outer, y, keep, guess, early_even, early_odd, fine_end, jump, even, odd):
+    slabs = Slabs(space_size, None, (inner, outer, y, y))
 
     def finish(f, x, t, value):
         fine_end[f * PLANES + x, t] = value * 2.0 if f == 0 else value
 
-    fine_round(space_size, slabs, even, odd, keep, finish)
+    late_round(space_size, slabs, early_even, early_odd, even, odd, keep, finish)
     ended = halves(coarse_rows(lambda k, t: fine_end[2 * k, t] + fine_end[2 * k + 1, t], PACKED), PACKED)
     jumped = ended - jnp.where(lax.axis_index("tm") == 0, 0.0, guess[...])
     for k in range(jump.shape[0]):
@@ -404,15 +454,25 @@
         compiler_params=params(),
         name="guess_old",
     )(*opening[:2], *opening_near)
+    inner, outer, x, y = middle_near
+    buffer = shaped(FIELDS, WINDOW, TILES + 2, 8, NZ)
+    early = pl.pallas_call(
+        functools.partial(early_kernel, space_size),
+        out_shape=(buffer, buffer),
+        in_specs=[VMEM] * 6,
+        out_specs=(VMEM, VMEM),
+        compiler_params=params(),
+        name="second_round_early",
+    )(*middle, inner, outer, x, keep)
     fine_end, jump = pl.pallas_call(
         functools.partial(second_kernel, space_size),
         out_shape=(shaped(PACKED, TILES, 8, NZ), shaped(slices * space_size // 2, PACKED, NZ)),
-        in_specs=[VMEM] * 8,
+        in_specs=[VMEM] * 7,
         out_specs=(VMEM, VMEM),
         scratch_shapes=buffers,
         compiler_params=params(),
         name="second_round",
-    )(*middle, *middle_near, keep, guess)
+    )(inner, outer, y, keep, guess, *early)
     members = [range(core, slices * space_size, 2) for core in range(2)]
     jumps = lax.all_to_all(jump, ("tm", "space"), 0, 0, axis_index_groups=[list(group) for group in members])
     jumps = jumps.reshape(slices, space_size // 2, PACKED, NZ)[: slices - 1]

time: 53.6 us -> 52.8 us (0.985)
  waiting for transfers between devices: 14.1 us -> 13.1 us
    ppermute x2, waiting for transfers between devices: 9.31 us -> 8.33 us  [exchange(): y = lax.ppermute(two_y, 'space', second)]
    pallas_call x0 -> x1, Pallas kernels: none -> 0.98 us  [local(): pl.pallas_call(functools.partial(early_kernel, space_size), out_shape=(bu...]
    pallas_call x1, Pallas kernels: 2.45 us -> 1.61 us  [local(): pl.pallas_call(functools.partial(second_kernel, space_size), out_shape=(s...]
  transfers between devices with their start and end apart: 9 -> 9, of which waited for: 5 -> 5; matrix products, arithmetic and copies ran while one was open for 0% -> 0% of each run, Pallas kernels for 2% -> 4%
where the time goes in v12:
time: 52.8 us; the launch traced here: 52.6 us
  blocking collectives  17.1 us (32%)
  waiting for transfers between devices  13.1 us (25%)
  starting transfers between devices  12.2 us (23%)
  Pallas kernels  7.97 us (15%)
  local copies, waits for them, and re-layouts  1.95 us (4%)
    all_to_all x1, blocking collectives, local(): lax.all_to_all(jump, ('tm', 'space'), 0, 0, axis_index_groups=[list(group...  17.1 us
    ppermute x2, waiting for transfers between devices, exchange(): y = lax.ppermute(two_y, 'space', second)  8.33 us
    ppermute x2, starting transfers between devices, exchange(): within = lax.ppermute(one, 'space', inner)  5.25 us
    ppermute x2, starting transfers between devices, exchange(): x = lax.ppermute(two_x, 'space', first)  4.6 us
    ppermute x2, waiting for transfers between devices, exchange(): x = lax.ppermute(two_x, 'space', first)  3.49 us
    pallas_call x1, Pallas kernels, local(): pl.pallas_call(functools.partial(first_kernel, space_size), out_shape=(ha...  2.1 us
    unnamed x4, local copies, waits for them, and re-layouts  1.94 us
    pallas_call x1, Pallas kernels, local(): pl.pallas_call(correct_kernel, out_shape=shaped(1, FIELDS, PLANES, NY, NZ...  1.78 us
  transfers between devices with their start and end apart: 9, of which 5 were waited for; matrix products, arithmetic and copies ran while one was open for 0% of the time, Pallas kernels for 4%

profile of v12, /device:TPU:0, one launch (start us, length us, event | category | flops | bytes accessed | tf_op | source)
XLA Modules:
  0.0 52.6 jit_solution(18104103928512014799)
XLA Ops:
  0.0 1.0 %copy-done = f32[1,4,4,64,128]{4,3,2,1,0:T(8,128)S(1)} copy-done((f32[1,4,4,64,128]{4,3,2,1,0:T(8,128)S(1)}, f32[1,4,4,64,128]{4,3,2,1,0:T(8,128)}, u32[]{:S(2)}) %copy-start) | copy-done | bytes 524312
  1.0 0.9 %copy-done.1 = s32[4,64,128]{2,1,0:T(8,128)S(1)} copy-done((s32[4,64,128]{2,1,0:T(8,128)S(1)}, s32[4,64,128]{2,1,0:T(8,128)}, u32[]{:S(2)}) %copy-start.1) | copy-done | bytes 131096
  1.9 0.4 prepare.1
  2.3 0.5 collective-permute-start.2
  2.8 0.7 %collective-permute-start.1 = (f32[10,8,8,128]{3,2,1,0:T(8,128)S(1)}, f32[10,8,8,128]{3,2,1,0:T(8,128)S(1)}, u32[]{:S(2)}, u32[]{:S(2)}) collective-permute-start(f32[10,8,8,128]{3,2,1,0:T(8,128)S(1)} %get-tuple-element.15.own_one), channel_id=1, source_target_pairs={{0,0},{1,2},{2,1},{3,4},{4,3},{5,6},{6,5},{7,7},{8,8},{9,10},{10,9... | collective-permute-start | bytes 983048 | tf_op jit(solution)/shard_map/ppermute | solution.py:407
  3.5 3.9 %collective-permute-start = (f32[10,8,8,128]{3,2,1,0:T(8,128)S(1)}, f32[10,8,8,128]{3,2,1,0:T(8,128)S(1)}, u32[]{:S(2)}, u32[]{:S(2)}) collective-permute-start(f32[10,8,8,128]{3,2,1,0:T(8,128)S(1)} %get-tuple-element.15.own_one), channel_id=1, source_target_pairs={{0,1},{1,0},{2,3},{3,2},{4,5},{5,4},{6,7},{7,6},{8,9},{9,8},{10,11... | collective-permute-start | bytes 983048 | tf_op jit(solution)/shard_map/ppermute | solution.py:408
  7.4 2.6 %collective-permute-done.2.x = f32[9,8,8,128]{3,2,1,0:T(8,128)S(1)} collective-permute-done((f32[9,8,8,128]{3,2,1,0:T(8,128)S(1)}, f32[9,8,8,128]{3,2,1,0:T(8,128)S(1)}, u32[]{:S(2)}, u32[]{:S(2)}) %collective-permute-start.2) | collective-permute-done | bytes 294944 | tf_op jit(solution)/shard_map/ppermute | solution.py:406
  10.1 0.1 collective-permute-start.3
  10.1 0.0 collective-permute-done.1.outer
  10.2 5.5 %collective-permute-done.3.y = f32[9,8,8,128]{3,2,1,0:T(8,128)S(1)} collective-permute-done((f32[9,8,8,128]{3,2,1,0:T(8,128)S(1)}, f32[9,8,8,128]{3,2,1,0:T(8,128)S(1)}, u32[]{:S(2)}, u32[]{:S(2)}) %collective-permute-start.3) | collective-permute-done | bytes 294944 | tf_op jit(solution)/shard_map/ppermute | solution.py:412
  15.7 2.1 %first_round.1 = (f32[8,8,8,128]{3,2,1,0:T(8,128)S(1)}, f32[8,8,8,128]{3,2,1,0:T(8,128)S(1)}, f32[2,12,8,8,128]{4,3,2,1,0:T(8,128)S(1)}) custom-call(f32[10,8,8,128]{3,2,1,0:T(8,128)S(1)} %get-tuple-element.15.own_one, f32[9,8,8,128]{3,2,1,0:T(8,128)S(1)} %get-tuple-element.16.own_two, f32[9,8,8,128]{3,2,1,0:T(8,128)S(1)} %get-tuple-element.17.own_other, ...), custom_call_target="tpu_custom_call" | custom-call | tf_op jit(solution)/shard_map/first_round/pallas_call | solution.py:439
  17.8 4.1 %collective-permute-start.6 = (f32[8,8,8,128]{3,2,1,0:T(8,128)S(1)}, f32[8,8,8,128]{3,2,1,0:T(8,128)S(1)}, u32[]{:S(2)}, u32[]{:S(2)}) collective-permute-start(f32[8,8,8,128]{3,2,1,0:T(8,128)S(1)} %get-tuple-element.19.own_two), channel_id=1, source_target_pairs={{0,1},{1,2},{2,3},{3,7},{7,6},{6,5},{5,4},{4,0},{8,9},{9,10},{10,1... | collective-permute-start | bytes 786440 | tf_op jit(solution)/shard_map/ppermute | solution.py:406
  21.8 0.7 %collective-permute-start.5 = (f32[8,8,8,128]{3,2,1,0:T(8,128)S(1)}, f32[8,8,8,128]{3,2,1,0:T(8,128)S(1)}, u32[]{:S(2)}, u32[]{:S(2)}) collective-permute-start(f32[8,8,8,128]{3,2,1,0:T(8,128)S(1)} %get-tuple-element.18.own_one), channel_id=1, source_target_pairs={{0,0},{1,2},{2,1},{3,4},{4,3},{5,6},{6,5},{7,7},{8,8},{9,10},{10,9... | collective-permute-start | bytes 786440 | tf_op jit(solution)/shard_map/ppermute | solution.py:407
  22.5 1.3 %collective-permute-start.4 = (f32[8,8,8,128]{3,2,1,0:T(8,128)S(1)}, f32[8,8,8,128]{3,2,1,0:T(8,128)S(1)}, u32[]{:S(2)}, u32[]{:S(2)}) collective-permute-start(f32[8,8,8,128]{3,2,1,0:T(8,128)S(1)} %get-tuple-element.18.own_one), channel_id=1, source_target_pairs={{0,1},{1,0},{2,3},{3,2},{4,5},{5,4},{6,7},{7,6},{8,9},{9,8},{10,11... | collective-permute-start | bytes 786440 | tf_op jit(solution)/shard_map/ppermute | solution.py:408
  23.9 0.9 %collective-permute-done.6.x = f32[8,8,8,128]{3,2,1,0:T(8,128)S(1)} collective-permute-done((f32[8,8,8,128]{3,2,1,0:T(8,128)S(1)}, f32[8,8,8,128]{3,2,1,0:T(8,128)S(1)}, u32[]{:S(2)}, u32[]{:S(2)}) %collective-permute-start.6) | collective-permute-done | bytes 262176 | tf_op jit(solution)/shard_map/ppermute | solution.py:406
  24.8 0.9 %collective-permute-start.7 = (f32[8,8,8,128]{3,2,1,0:T(8,128)S(1)}, f32[8,8,8,128]{3,2,1,0:T(8,128)S(1)}, u32[]{:S(2)}, u32[]{:S(2)}) collective-permute-start(f32[8,8,8,128]{3,2,1,0:T(8,128)S(1)} %broadcast_select_fusion.1), channel_id=1, source_target_pairs={{3,2},{2,1},{1,0},{0,3},{4,5},{5,6},{6,7},{7,4},{11,10},{10,9},{9,... | collective-permute-start | bytes 786440 | tf_op jit(solution)/shard_map/ppermute | solution.py:412
  25.7 1.1 %guess_old.1.guess = f32[16,128]{1,0:T(8,128)S(1)} custom-call(f32[10,8,8,128]{3,2,1,0:T(8,128)S(1)} %get-tuple-element.15.own_one, f32[9,8,8,128]{3,2,1,0:T(8,128)S(1)} %get-tuple-element.16.own_two, f32[10,8,8,128]{3,2,1,0:T(8,128)S(1)} %collective-permute-done.inner, f32[10,8,8,128]{3,2,1,0:T(8,128)S(1)} %collective-permute-done.1.outer, ...), custom_call_target="tpu_custom_call" | custom-call | tf_op jit(solution)/shard_map/guess_old/pallas_call | solution.py:449
  26.8 1.0 %second_round_early.1 = (f32[4,12,10,8,128]{4,3,2,1,0:T(8,128)S(1)}, f32[4,12,10,8,128]{4,3,2,1,0:T(8,128)S(1)}) custom-call(f32[8,8,8,128]{3,2,1,0:T(8,128)S(1)} %get-tuple-element.18.own_one, f32[8,8,8,128]{3,2,1,0:T(8,128)S(1)} %get-tuple-element.19.own_two, f32[8,8,8,128]{3,2,1,0:T(8,128)S(1)} %collective-permute-done.4.inner, ...), custom_call_target="tpu_custom_call" | custom-call | tf_op jit(solution)/shard_map/second_round_early/pallas_call | solution.py:459
  27.8 2.8 %collective-permute-done.7.y = f32[8,8,8,128]{3,2,1,0:T(8,128)S(1)} collective-permute-done((f32[8,8,8,128]{3,2,1,0:T(8,128)S(1)}, f32[8,8,8,128]{3,2,1,0:T(8,128)S(1)}, u32[]{:S(2)}, u32[]{:S(2)}) %collective-permute-start.7) | collective-permute-done | bytes 262176 | tf_op jit(solution)/shard_map/ppermute | solution.py:412
  30.7 1.6 %second_round.1 = (f32[16,8,8,128]{3,2,1,0:T(8,128)S(1)}, f32[16,16,128]{2,1,0:T(8,128)S(1)}) custom-call(f32[8,8,8,128]{3,2,1,0:T(8,128)S(1)} %collective-permute-done.4.inner, f32[8,8,8,128]{3,2,1,0:T(8,128)S(1)} %collective-permute-done.5.outer, f32[8,8,8,128]{3,2,1,0:T(8,128)S(1)} %collective-permute-done.7.y, ...), custom_call_target="tpu_custom_call" | custom-call | tf_op jit(solution)/shard_map/second_round/pallas_call | solution.py:467
  32.3 17.1 %all_to_all.5 = f32[16,16,128]{2,1,0:T(8,128)S(1)} all-to-all(f32[16,16,128]{2,1,0:T(8,128)S(1)} %get-tuple-element.23), channel_id=1, replica_groups={{0,2,4,6,8,10,12,14,16,18,20,22,24,26,28,30},{1,3,5,7,9,11,13,15,17,19,..., dimensions={0} | all-to-all | bytes 262144 | tf_op jit(solution)/shard_map/all_to_all | solution.py:477
  49.4 0.1 collective-permute-start.8
  49.5 1.3 %collective-permute-done.8.others = f32[3,4,16,128]{3,2,1,0:T(8,128)S(1)} collective-permute-done((f32[3,4,16,128]{3,2,1,0:T(8,128)S(1)}, f32[3,4,16,128]{3,2,1,0:T(8,128)S(1)}, u32[]{:S(2)}, u32[]{:S(2)}) %collective-permute-start.8) | collective-permute-done | bytes 98336 | tf_op jit(solution)/shard_map/ppermute | solution.py:479
  50.8 1.8 %correct.1 = f32[1,4,4,64,128]{4,3,2,1,0:T(8,128)} custom-call(f32[3,4,16,128]{3,2,1,0:T(8,128)S(1)} %bitcast.2, f32[3,4,16,128]{3,2,1,0:T(8,128)S(1)} %collective-permute-done.8.others, f32[16,128]{1,0:T(8,128)S(1)} %guess_old.1.guess, f32[16,8,8,128]{3,2,1,0:T(8,128)S(1)} %get-tuple-element.24.fine_end), custom_call_target="tpu_custom_call" | custom-call | tf_op jit(solution)/shard_map/correct/pallas_call | solution.py:480
  (8 shorter events, 0.1 us)
Async XLA Ops:
  0.0 1.0 %copy-start = (f32[1,4,4,64,128]{4,3,2,1,0:T(8,128)S(1)}, f32[1,4,4,64,128]{4,3,2,1,0:T(8,128)}, u32[]{:S(2)}) copy-start(f32[1,4,4,64,128]{4,3,2,1,0:T(8,128)} %starts.1) | copy-start | bytes 1572868
  1.0 0.9 %copy-start.1 = (s32[4,64,128]{2,1,0:T(8,128)S(1)}, s32[4,64,128]{2,1,0:T(8,128)}, u32[]{:S(2)}) copy-start(s32[4,64,128]{2,1,0:T(8,128)} %flags.1) | copy-start | bytes 393220
  2.3 7.7 %collective-permute-start.2 = (f32[9,8,8,128]{3,2,1,0:T(8,128)S(1)}, f32[9,8,8,128]{3,2,1,0:T(8,128)S(1)}, u32[]{:S(2)}, u32[]{:S(2)}) collective-permute-start(f32[9,8,8,128]{3,2,1,0:T(8,128)S(1)} %get-tuple-element.16.own_two), channel_id=1, source_target_pairs={{0,1},{1,2},{2,3},{3,7},{7,6},{6,5},{5,4},{4,0},{8,9},{9,10},{10,1... | collective-permute-start | bytes 884744 | tf_op jit(solution)/shard_map/ppermute | solution.py:406
  2.8 7.3 %collective-permute-start.1 = (f32[10,8,8,128]{3,2,1,0:T(8,128)S(1)}, f32[10,8,8,128]{3,2,1,0:T(8,128)S(1)}, u32[]{:S(2)}, u32[]{:S(2)}) collective-permute-start(f32[10,8,8,128]{3,2,1,0:T(8,128)S(1)} %get-tuple-element.15.own_one), channel_id=1, source_target_pairs={{0,0},{1,2},{2,1},{3,4},{4,3},{5,6},{6,5},{7,7},{8,8},{9,10},{10,9... | collective-permute-start | bytes 983048 | tf_op jit(solution)/shard_map/ppermute | solution.py:407
  3.5 6.7 %collective-permute-start = (f32[10,8,8,128]{3,2,1,0:T(8,128)S(1)}, f32[10,8,8,128]{3,2,1,0:T(8,128)S(1)}, u32[]{:S(2)}, u32[]{:S(2)}) collective-permute-start(f32[10,8,8,128]{3,2,1,0:T(8,128)S(1)} %get-tuple-element.15.own_one), channel_id=1, source_target_pairs={{0,1},{1,0},{2,3},{3,2},{4,5},{5,4},{6,7},{7,6},{8,9},{9,8},{10,11... | collective-permute-start | bytes 983048 | tf_op jit(solution)/shard_map/ppermute | solution.py:408
  10.1 5.6 %collective-permute-start.3 = (f32[9,8,8,128]{3,2,1,0:T(8,128)S(1)}, f32[9,8,8,128]{3,2,1,0:T(8,128)S(1)}, u32[]{:S(2)}, u32[]{:S(2)}) collective-permute-start(f32[9,8,8,128]{3,2,1,0:T(8,128)S(1)} %broadcast_select_fusion), channel_id=1, source_target_pairs={{3,2},{2,1},{1,0},{0,3},{4,5},{5,6},{6,7},{7,4},{11,10},{10,9},{9,... | collective-permute-start | bytes 884744 | tf_op jit(solution)/shard_map/ppermute | solution.py:412
  17.8 7.0 %collective-permute-start.6 = (f32[8,8,8,128]{3,2,1,0:T(8,128)S(1)}, f32[8,8,8,128]{3,2,1,0:T(8,128)S(1)}, u32[]{:S(2)}, u32[]{:S(2)}) collective-permute-start(f32[8,8,8,128]{3,2,1,0:T(8,128)S(1)} %get-tuple-element.19.own_two), channel_id=1, source_target_pairs={{0,1},{1,2},{2,3},{3,7},{7,6},{6,5},{5,4},{4,0},{8,9},{9,10},{10,1... | collective-permute-start | bytes 786440 | tf_op jit(solution)/shard_map/ppermute | solution.py:406
  21.8 5.0 %collective-permute-start.5 = (f32[8,8,8,128]{3,2,1,0:T(8,128)S(1)}, f32[8,8,8,128]{3,2,1,0:T(8,128)S(1)}, u32[]{:S(2)}, u32[]{:S(2)}) collective-permute-start(f32[8,8,8,128]{3,2,1,0:T(8,128)S(1)} %get-tuple-element.18.own_one), channel_id=1, source_target_pairs={{0,0},{1,2},{2,1},{3,4},{4,3},{5,6},{6,5},{7,7},{8,8},{9,10},{10,9... | collective-permute-start | bytes 786440 | tf_op jit(solution)/shard_map/ppermute | solution.py:407
  22.5 4.3 %collective-permute-start.4 = (f32[8,8,8,128]{3,2,1,0:T(8,128)S(1)}, f32[8,8,8,128]{3,2,1,0:T(8,128)S(1)}, u32[]{:S(2)}, u32[]{:S(2)}) collective-permute-start(f32[8,8,8,128]{3,2,1,0:T(8,128)S(1)} %get-tuple-element.18.own_one), channel_id=1, source_target_pairs={{0,1},{1,0},{2,3},{3,2},{4,5},{5,4},{6,7},{7,6},{8,9},{9,8},{10,11... | collective-permute-start | bytes 786440 | tf_op jit(solution)/shard_map/ppermute | solution.py:408
  24.8 5.9 %collective-permute-start.7 = (f32[8,8,8,128]{3,2,1,0:T(8,128)S(1)}, f32[8,8,8,128]{3,2,1,0:T(8,128)S(1)}, u32[]{:S(2)}, u32[]{:S(2)}) collective-permute-start(f32[8,8,8,128]{3,2,1,0:T(8,128)S(1)} %broadcast_select_fusion.1), channel_id=1, source_target_pairs={{3,2},{2,1},{1,0},{0,3},{4,5},{5,6},{6,7},{7,4},{11,10},{10,9},{9,... | collective-permute-start | bytes 786440 | tf_op jit(solution)/shard_map/ppermute | solution.py:412
  49.4 1.4 %collective-permute-start.8 = (f32[3,4,16,128]{3,2,1,0:T(8,128)S(1)}, f32[3,4,16,128]{3,2,1,0:T(8,128)S(1)}, u32[]{:S(2)}, u32[]{:S(2)}) collective-permute-start(f32[3,4,16,128]{3,2,1,0:T(8,128)S(1)} %bitcast.1), channel_id=1, source_target_pairs={{0,1},{1,0},{2,3},{3,2},{4,5},{5,4},{6,7},{7,6},{8,9},{9,8},{10,11... | collective-permute-start | bytes 294920 | tf_op jit(solution)/shard_map/ppermute | solution.py:479

commit v13 on v12

--- a/solution.py
+++ b/solution.py
@@ -159,16 +159,9 @@
             fine_plane(read, keep, p, inside(space_size, p), store)
 
 
-def fine_round(space_size, slabs, even, odd, keep, finish):
-    fine_load(slabs, range(3), even)
-    spans = [range(step + 1, WINDOW - 1 - step) for step in range(ROUND)]
-    fine_planes(space_size, spans, even, odd, keep, finish)
-
-
-def both_ways(space_size, run):
-    low = lax.axis_index("space") < turn(space_size)
-    pl.when(low)(lambda: run(False))
-    pl.when(jnp.logical_not(low))(lambda: run(True))
+def both_ways(mirror, run):
+    pl.when(jnp.logical_not(mirror))(lambda: run(False))
+    pl.when(mirror)(lambda: run(True))
 
 
 def seen(span, mirror):
@@ -183,10 +176,10 @@
         spans = [seen(range(1 + step, 2 * PLANES - 1 - step), mirror) for step in range(ROUND - 1)]
         fine_planes(space_size, spans, even, odd, keep, None)
 
-    both_ways(space_size, run)
-
-
-def late_round(space_size, slabs, early_even, early_odd, even, odd, keep, finish):
+    both_ways(jnp.logical_not(slabs.low), run)
+
+
+def late_round(space_size, slabs, mirrored, early_even, early_odd, even, odd, keep, finish):
     def run(mirror):
         fine_load(slabs, (0 if mirror else 2,), even)
         spans = [seen(range(2 * PLANES - 1 - step, WINDOW - 1 - step), mirror) for step in range(ROUND)]
@@ -197,12 +190,11 @@
 
         fine_planes(space_size, spans, even, odd, keep, finish, source)
 
-    both_ways(space_size, run)
-
-
-def first_kernel(space_size, own_one, own_two, own_other, inner, outer, x, y, ended_one, ended_two, keep, even, odd):
-    slabs = Slabs(space_size, (own_one, own_two), (inner, outer, x, y))
-    for p in range(1, WINDOW - 1):
+    both_ways(mirrored, run)
+
+
+def keep_factors(space_size, slabs, own_other, planes, keep):
+    for p in planes:
         j, k = p // PLANES, p % PLANES
         scale = jnp.where(inside(space_size, p), fine_dt, 0.0).astype(F32)
         for t in range(TILES):
@@ -213,11 +205,35 @@
             keep[0, p, t] = jnp.where(kind != 1.0, scale, 0.0)
             keep[1, p, t] = jnp.where(kind != 2.0, scale, 0.0)
 
+
+def first_early_kernel(space_size, own_one, own_two, own_other, inner, x, y, keep, even, odd):
+    slabs = Slabs(space_size, (own_one, own_two), (inner, inner, x, y))
+
+    def run(mirror):
+        fine_load(slabs, (2 if mirror else 0, 1), even)
+        keep_factors(space_size, slabs, own_other, seen(range(1, 2 * PLANES), mirror), keep)
+        spans = [seen(range(1 + step, 2 * PLANES - 1 - step), mirror) for step in range(ROUND - 1)]
+        fine_planes(space_size, spans, even, odd, keep, None)
+
+    both_ways(lax.axis_index("space") % 2 == 0, run)
+
+
+def first_kernel(space_size, outer, x, y, early_keep, early_even, early_odd, ended_one, ended_two, keep, even, odd):
+    slabs = Slabs(space_size, None, (outer, outer, x, y))
+    mirrored = lax.axis_index("space") % 2 == 0
+
+    def fill(mirror):
+        for p in seen(range(1, 2 * PLANES), mirror):
+            for k in range(2):
+                keep[k, p] = early_keep[k, p]
+        keep_factors(space_size, slabs, None, seen(range(2 * PLANES, WINDOW - 1), mirror), keep)
+
     def finish(f, x, t, value):
         ended = ended_one if f < 2 else ended_two
         ended[f % 2 * PLANES + x, t] = value
 
-    fine_round(space_size, slabs, even, odd, keep, finish)
+    both_ways(mirrored, fill)
+    late_round(space_size, slabs, mirrored, early_even, early_odd, even, odd, keep, finish)
 
 
 def chosen(values, picks):
@@ -324,7 +340,7 @@
     def finish(f, x, t, value):
         fine_end[f * PLANES + x, t] = value * 2.0 if f == 0 else value
 
-    late_round(space_size, slabs, early_even, early_odd, even, odd, keep, finish)
+    late_round(space_size, slabs, jnp.logical_not(slabs.low), early_even, early_odd, even, odd, keep, finish)
     ended = halves(coarse_rows(lambda k, t: fine_end[2 * k, t] + fine_end[2 * k + 1, t], PACKED), PACKED)
     jumped = ended - jnp.where(lax.axis_index("tm") == 0, 0.0, guess[...])
     for k in range(jump.shape[0]):
@@ -436,15 +452,25 @@
         name="prepare",
     )(starts, flags)
     opening_near = exchange(*opening, space_size)
+    inner, outer, x, y = opening_near
+    buffer = shaped(FIELDS, WINDOW, TILES + 2, 8, NZ)
+    early = pl.pallas_call(
+        functools.partial(first_early_kernel, space_size),
+        out_shape=(keep_shape, buffer, buffer),
+        in_specs=[VMEM] * 6,
+        out_specs=(VMEM,) * 3,
+        compiler_params=params(),
+        name="first_round_early",
+    )(*opening, inner, x, y)
     *middle, keep = pl.pallas_call(
         functools.partial(first_kernel, space_size),
         out_shape=(half, half, keep_shape),
-        in_specs=[VMEM] * 7,
+        in_specs=[VMEM] * 6,
         out_specs=(VMEM,) * 3,
         scratch_shapes=buffers,
         compiler_params=params(),
         name="first_round",
-    )(*opening, *opening_near)
+    )(outer, x, y, *early)
     middle_near = exchange(middle[0], middle[1], middle[1], space_size)
     guess = pl.pallas_call(
         functools.partial(guess_kernel, space_size),
@@ -455,7 +481,6 @@
         name="guess_old",
     )(*opening[:2], *opening_near)
     inner, outer, x, y = middle_near
-    buffer = shaped(FIELDS, WINDOW, TILES + 2, 8, NZ)
     early = pl.pallas_call(
         functools.partial(early_kernel, space_size),
         out_shape=(buffer, buffer),

time: 52.8 us -> 54.6 us (1.034)
  Pallas kernels: 7.97 us -> 11 us
  blocking collectives: 17.1 us -> 15.4 us
  waiting for transfers between devices: 13.1 us -> 14 us
    pallas_call x0 -> x1, Pallas kernels: none -> 2.27 us  [local(): pl.pallas_call(functools.partial(first_early_kernel, space_size), out_sha...]
    all_to_all x1, blocking collectives: 17.1 us -> 15.4 us  [local(): lax.all_to_all(jump, ('tm', 'space'), 0, 0, axis_index_groups=[list(group...]
    ppermute x2, starting transfers between devices: 5.25 us -> 3.93 us  [exchange(): within = lax.ppermute(one, 'space', inner)]
    ppermute x2, waiting for transfers between devices: 3.49 us -> 4.32 us  [exchange(): x = lax.ppermute(two_x, 'space', first)]
    pallas_call x1, Pallas kernels: 2.1 us -> 2.82 us  [local(): pl.pallas_call(functools.partial(first_kernel, space_size), out_shape=(ha...]
  transfers between devices with their start and end apart: 9 -> 9, of which waited for: 5 -> 5; matrix products, arithmetic and copies ran while one was open for 0% -> 0% of each run, Pallas kernels for 4% -> 8%
where the time goes in v13:
time: 54.6 us; the launch traced here: 54.4 us
  blocking collectives  15.4 us (28%)
  waiting for transfers between devices  14 us (26%)
  starting transfers between devices  11.9 us (22%)
  Pallas kernels  11 us (20%)
  local copies, waits for them, and re-layouts  1.95 us (4%)
    all_to_all x1, blocking collectives, local(): lax.all_to_all(jump, ('tm', 'space'), 0, 0, axis_index_groups=[list(group...  15.4 us
    ppermute x2, waiting for transfers between devices, exchange(): y = lax.ppermute(two_y, 'space', second)  8.34 us
    ppermute x2, starting transfers between devices, exchange(): x = lax.ppermute(two_x, 'space', first)  5.08 us
    ppermute x2, waiting for transfers between devices, exchange(): x = lax.ppermute(two_x, 'space', first)  4.32 us
    ppermute x2, starting transfers between devices, exchange(): within = lax.ppermute(one, 'space', inner)  3.93 us
    pallas_call x1, Pallas kernels, local(): pl.pallas_call(functools.partial(first_kernel, space_size), out_shape=(ha...  2.82 us
    pallas_call x1, Pallas kernels, local(): pl.pallas_call(functools.partial(first_early_kernel, space_size), out_sha...  2.27 us
    unnamed x4, local copies, waits for them, and re-layouts  1.94 us
  transfers between devices with their start and end apart: 9, of which 5 were waited for; matrix products, arithmetic and copies ran while one was open for 0% of the time, Pallas kernels for 8%

profile of v13, /device:TPU:0, one launch (start us, length us, event | category | flops | bytes accessed | tf_op | source)
XLA Modules:
  0.0 54.4 jit_solution(16310739560522991311)
XLA Ops:
  0.0 1.0 %copy-done = f32[1,4,4,64,128]{4,3,2,1,0:T(8,128)S(1)} copy-done((f32[1,4,4,64,128]{4,3,2,1,0:T(8,128)S(1)}, f32[1,4,4,64,128]{4,3,2,1,0:T(8,128)}, u32[]{:S(2)}) %copy-start) | copy-done | bytes 524312
  1.0 0.9 %copy-done.1 = s32[4,64,128]{2,1,0:T(8,128)S(1)} copy-done((s32[4,64,128]{2,1,0:T(8,128)S(1)}, s32[4,64,128]{2,1,0:T(8,128)}, u32[]{:S(2)}) %copy-start.1) | copy-done | bytes 131096
  1.9 0.4 prepare.1
  2.3 0.5 collective-permute-start.1
  2.8 2.6 %collective-permute-start.3 = (f32[10,8,8,128]{3,2,1,0:T(8,128)S(1)}, f32[10,8,8,128]{3,2,1,0:T(8,128)S(1)}, u32[]{:S(2)}, u32[]{:S(2)}) collective-permute-start(f32[10,8,8,128]{3,2,1,0:T(8,128)S(1)} %get-tuple-element.18.own_one), channel_id=1, source_target_pairs={{0,1},{1,0},{2,3},{3,2},{4,5},{5,4},{6,7},{7,6},{8,9},{9,8},{10,11... | collective-permute-start | bytes 983048 | tf_op jit(solution)/shard_map/ppermute | solution.py:424
  5.4 0.7 %collective-permute-start = (f32[10,8,8,128]{3,2,1,0:T(8,128)S(1)}, f32[10,8,8,128]{3,2,1,0:T(8,128)S(1)}, u32[]{:S(2)}, u32[]{:S(2)}) collective-permute-start(f32[10,8,8,128]{3,2,1,0:T(8,128)S(1)} %get-tuple-element.18.own_one), channel_id=1, source_target_pairs={{0,0},{1,2},{2,1},{3,4},{4,3},{5,6},{6,5},{7,7},{8,8},{9,10},{10,9... | collective-permute-start | bytes 983048 | tf_op jit(solution)/shard_map/ppermute | solution.py:423
  6.1 3.9 %collective-permute-done.1.x = f32[9,8,8,128]{3,2,1,0:T(8,128)S(1)} collective-permute-done((f32[9,8,8,128]{3,2,1,0:T(8,128)S(1)}, f32[9,8,8,128]{3,2,1,0:T(8,128)S(1)}, u32[]{:S(2)}, u32[]{:S(2)}) %collective-permute-start.1) | collective-permute-done | bytes 294944 | tf_op jit(solution)/shard_map/ppermute | solution.py:422
  10.1 0.1 collective-permute-start.2
  10.2 5.5 %collective-permute-done.2.y = f32[9,8,8,128]{3,2,1,0:T(8,128)S(1)} collective-permute-done((f32[9,8,8,128]{3,2,1,0:T(8,128)S(1)}, f32[9,8,8,128]{3,2,1,0:T(8,128)S(1)}, u32[]{:S(2)}, u32[]{:S(2)}) %collective-permute-start.2) | collective-permute-done | bytes 294944 | tf_op jit(solution)/shard_map/ppermute | solution.py:428
  15.7 2.3 %first_round_early.1 = (f32[2,12,8,8,128]{4,3,2,1,0:T(8,128)S(1)}, f32[4,12,10,8,128]{4,3,2,1,0:T(8,128)S(1)}, f32[4,12,10,8,128]{4,3,2,1,0:T(8,128)}) custom-call(f32[10,8,8,128]{3,2,1,0:T(8,128)S(1)} %get-tuple-element.18.own_one, f32[9,8,8,128]{3,2,1,0:T(8,128)S(1)} %get-tuple-element.19.own_two, f32[9,8,8,128]{3,2,1,0:T(8,128)S(1)} %get-tuple-element.20.own_other, ...), custom_call_target="tpu_custom_call" | custom-call | tf_op jit(solution)/shard_map/first_round_early/pallas_call | solution.py:457
  17.9 2.8 %first_round.1 = (f32[8,8,8,128]{3,2,1,0:T(8,128)S(1)}, f32[8,8,8,128]{3,2,1,0:T(8,128)S(1)}, f32[2,12,8,8,128]{4,3,2,1,0:T(8,128)S(1)}) custom-call(f32[10,8,8,128]{3,2,1,0:T(8,128)S(1)} %collective-permute-done.outer, f32[9,8,8,128]{3,2,1,0:T(8,128)S(1)} %collective-permute-done.1.x, f32[9,8,8,128]{3,2,1,0:T(8,128)S(1)} %collective-permute-done.2.y, ...), custom_call_target="tpu_custom_call" | custom-call | tf_op jit(solution)/shard_map/first_round/pallas_call | solution.py:465
  20.8 4.6 %collective-permute-start.6 = (f32[8,8,8,128]{3,2,1,0:T(8,128)S(1)}, f32[8,8,8,128]{3,2,1,0:T(8,128)S(1)}, u32[]{:S(2)}, u32[]{:S(2)}) collective-permute-start(f32[8,8,8,128]{3,2,1,0:T(8,128)S(1)} %get-tuple-element.25.own_two), channel_id=1, source_target_pairs={{0,1},{1,2},{2,3},{3,7},{7,6},{6,5},{5,4},{4,0},{8,9},{9,10},{10,1... | collective-permute-start | bytes 786440 | tf_op jit(solution)/shard_map/ppermute | solution.py:422
  25.3 0.7 %collective-permute-start.5 = (f32[8,8,8,128]{3,2,1,0:T(8,128)S(1)}, f32[8,8,8,128]{3,2,1,0:T(8,128)S(1)}, u32[]{:S(2)}, u32[]{:S(2)}) collective-permute-start(f32[8,8,8,128]{3,2,1,0:T(8,128)S(1)} %get-tuple-element.24.own_one), channel_id=1, source_target_pairs={{0,0},{1,2},{2,1},{3,4},{4,3},{5,6},{6,5},{7,7},{8,8},{9,10},{10,9... | collective-permute-start | bytes 786440 | tf_op jit(solution)/shard_map/ppermute | solution.py:423
  26.0 1.3 %collective-permute-start.4 = (f32[8,8,8,128]{3,2,1,0:T(8,128)S(1)}, f32[8,8,8,128]{3,2,1,0:T(8,128)S(1)}, u32[]{:S(2)}, u32[]{:S(2)}) collective-permute-start(f32[8,8,8,128]{3,2,1,0:T(8,128)S(1)} %get-tuple-element.24.own_one), channel_id=1, source_target_pairs={{0,1},{1,0},{2,3},{3,2},{4,5},{5,4},{6,7},{7,6},{8,9},{9,8},{10,11... | collective-permute-start | bytes 786440 | tf_op jit(solution)/shard_map/ppermute | solution.py:424
  27.3 0.4 collective-permute-done.6.x
  27.8 1.4 %collective-permute-start.7 = (f32[8,8,8,128]{3,2,1,0:T(8,128)S(1)}, f32[8,8,8,128]{3,2,1,0:T(8,128)S(1)}, u32[]{:S(2)}, u32[]{:S(2)}) collective-permute-start(f32[8,8,8,128]{3,2,1,0:T(8,128)S(1)} %broadcast_select_fusion.1), channel_id=1, source_target_pairs={{3,2},{2,1},{1,0},{0,3},{4,5},{5,6},{6,7},{7,4},{11,10},{10,9},{9,... | collective-permute-start | bytes 786440 | tf_op jit(solution)/shard_map/ppermute | solution.py:428
  29.2 1.1 %guess_old.1.guess = f32[16,128]{1,0:T(8,128)S(1)} custom-call(f32[10,8,8,128]{3,2,1,0:T(8,128)S(1)} %get-tuple-element.18.own_one, f32[9,8,8,128]{3,2,1,0:T(8,128)S(1)} %get-tuple-element.19.own_two, f32[10,8,8,128]{3,2,1,0:T(8,128)S(1)} %collective-permute-done.3.inner, f32[10,8,8,128]{3,2,1,0:T(8,128)S(1)} %collective-permute-done.outer, ...), custom_call_target="tpu_custom_call" | custom-call | tf_op jit(solution)/shard_map/guess_old/pallas_call | solution.py:475
  30.3 1.0 %second_round_early.1 = (f32[4,12,10,8,128]{4,3,2,1,0:T(8,128)S(1)}, f32[4,12,10,8,128]{4,3,2,1,0:T(8,128)S(1)}) custom-call(f32[8,8,8,128]{3,2,1,0:T(8,128)S(1)} %get-tuple-element.24.own_one, f32[8,8,8,128]{3,2,1,0:T(8,128)S(1)} %get-tuple-element.25.own_two, f32[8,8,8,128]{3,2,1,0:T(8,128)S(1)} %collective-permute-done.4.inner, ...), custom_call_target="tpu_custom_call" | custom-call | tf_op jit(solution)/shard_map/second_round_early/pallas_call | solution.py:484
  31.3 2.8 %collective-permute-done.7.y = f32[8,8,8,128]{3,2,1,0:T(8,128)S(1)} collective-permute-done((f32[8,8,8,128]{3,2,1,0:T(8,128)S(1)}, f32[8,8,8,128]{3,2,1,0:T(8,128)S(1)}, u32[]{:S(2)}, u32[]{:S(2)}) %collective-permute-start.7) | collective-permute-done | bytes 262176 | tf_op jit(solution)/shard_map/ppermute | solution.py:428
  34.2 1.6 %second_round.1 = (f32[16,8,8,128]{3,2,1,0:T(8,128)S(1)}, f32[16,16,128]{2,1,0:T(8,128)S(1)}) custom-call(f32[8,8,8,128]{3,2,1,0:T(8,128)S(1)} %collective-permute-done.4.inner, f32[8,8,8,128]{3,2,1,0:T(8,128)S(1)} %collective-permute-done.5.outer, f32[8,8,8,128]{3,2,1,0:T(8,128)S(1)} %collective-permute-done.7.y, ...), custom_call_target="tpu_custom_call" | custom-call | tf_op jit(solution)/shard_map/second_round/pallas_call | solution.py:492
  35.8 15.4 %all_to_all.5 = f32[16,16,128]{2,1,0:T(8,128)S(1)} all-to-all(f32[16,16,128]{2,1,0:T(8,128)S(1)} %get-tuple-element.29), channel_id=1, replica_groups={{0,2,4,6,8,10,12,14,16,18,20,22,24,26,28,30},{1,3,5,7,9,11,13,15,17,19,..., dimensions={0} | all-to-all | bytes 262144 | tf_op jit(solution)/shard_map/all_to_all | solution.py:502
  51.2 0.1 collective-permute-start.8
  51.3 1.3 %collective-permute-done.8.others = f32[3,4,16,128]{3,2,1,0:T(8,128)S(1)} collective-permute-done((f32[3,4,16,128]{3,2,1,0:T(8,128)S(1)}, f32[3,4,16,128]{3,2,1,0:T(8,128)S(1)}, u32[]{:S(2)}, u32[]{:S(2)}) %collective-permute-start.8) | collective-permute-done | bytes 98336 | tf_op jit(solution)/shard_map/ppermute | solution.py:504
  52.6 1.8 %correct.1 = f32[1,4,4,64,128]{4,3,2,1,0:T(8,128)} custom-call(f32[3,4,16,128]{3,2,1,0:T(8,128)S(1)} %bitcast.2, f32[3,4,16,128]{3,2,1,0:T(8,128)S(1)} %collective-permute-done.8.others, f32[16,128]{1,0:T(8,128)S(1)} %guess_old.1.guess, f32[16,8,8,128]{3,2,1,0:T(8,128)S(1)} %get-tuple-element.30.fine_end), custom_call_target="tpu_custom_call" | custom-call | tf_op jit(solution)/shard_map/correct/pallas_call | solution.py:505
  (9 shorter events, 0.1 us)
Async XLA Ops:
  0.0 1.0 %copy-start = (f32[1,4,4,64,128]{4,3,2,1,0:T(8,128)S(1)}, f32[1,4,4,64,128]{4,3,2,1,0:T(8,128)}, u32[]{:S(2)}) copy-start(f32[1,4,4,64,128]{4,3,2,1,0:T(8,128)} %starts.1) | copy-start | bytes 1572868
  1.0 0.9 %copy-start.1 = (s32[4,64,128]{2,1,0:T(8,128)S(1)}, s32[4,64,128]{2,1,0:T(8,128)}, u32[]{:S(2)}) copy-start(s32[4,64,128]{2,1,0:T(8,128)} %flags.1) | copy-start | bytes 393220
  2.3 7.7 %collective-permute-start.1 = (f32[9,8,8,128]{3,2,1,0:T(8,128)S(1)}, f32[9,8,8,128]{3,2,1,0:T(8,128)S(1)}, u32[]{:S(2)}, u32[]{:S(2)}) collective-permute-start(f32[9,8,8,128]{3,2,1,0:T(8,128)S(1)} %get-tuple-element.19.own_two), channel_id=1, source_target_pairs={{0,1},{1,2},{2,3},{3,7},{7,6},{6,5},{5,4},{4,0},{8,9},{9,10},{10,1... | collective-permute-start | bytes 884744 | tf_op jit(solution)/shard_map/ppermute | solution.py:422
  2.8 7.3 %collective-permute-start.3 = (f32[10,8,8,128]{3,2,1,0:T(8,128)S(1)}, f32[10,8,8,128]{3,2,1,0:T(8,128)S(1)}, u32[]{:S(2)}, u32[]{:S(2)}) collective-permute-start(f32[10,8,8,128]{3,2,1,0:T(8,128)S(1)} %get-tuple-element.18.own_one), channel_id=1, source_target_pairs={{0,1},{1,0},{2,3},{3,2},{4,5},{5,4},{6,7},{7,6},{8,9},{9,8},{10,11... | collective-permute-start | bytes 983048 | tf_op jit(solution)/shard_map/ppermute | solution.py:424
  5.4 12.5 %collective-permute-start = (f32[10,8,8,128]{3,2,1,0:T(8,128)S(1)}, f32[10,8,8,128]{3,2,1,0:T(8,128)S(1)}, u32[]{:S(2)}, u32[]{:S(2)}) collective-permute-start(f32[10,8,8,128]{3,2,1,0:T(8,128)S(1)} %get-tuple-element.18.own_one), channel_id=1, source_target_pairs={{0,0},{1,2},{2,1},{3,4},{4,3},{5,6},{6,5},{7,7},{8,8},{9,10},{10,9... | collective-permute-start | bytes 983048 | tf_op jit(solution)/shard_map/ppermute | solution.py:423
  10.1 5.6 %collective-permute-start.2 = (f32[9,8,8,128]{3,2,1,0:T(8,128)S(1)}, f32[9,8,8,128]{3,2,1,0:T(8,128)S(1)}, u32[]{:S(2)}, u32[]{:S(2)}) collective-permute-start(f32[9,8,8,128]{3,2,1,0:T(8,128)S(1)} %broadcast_select_fusion), channel_id=1, source_target_pairs={{3,2},{2,1},{1,0},{0,3},{4,5},{5,6},{6,7},{7,4},{11,10},{10,9},{9,... | collective-permute-start | bytes 884744 | tf_op jit(solution)/shard_map/ppermute | solution.py:428
  20.8 7.0 %collective-permute-start.6 = (f32[8,8,8,128]{3,2,1,0:T(8,128)S(1)}, f32[8,8,8,128]{3,2,1,0:T(8,128)S(1)}, u32[]{:S(2)}, u32[]{:S(2)}) collective-permute-start(f32[8,8,8,128]{3,2,1,0:T(8,128)S(1)} %get-tuple-element.25.own_two), channel_id=1, source_target_pairs={{0,1},{1,2},{2,3},{3,7},{7,6},{6,5},{5,4},{4,0},{8,9},{9,10},{10,1... | collective-permute-start | bytes 786440 | tf_op jit(solution)/shard_map/ppermute | solution.py:422
  25.3 5.0 %collective-permute-start.5 = (f32[8,8,8,128]{3,2,1,0:T(8,128)S(1)}, f32[8,8,8,128]{3,2,1,0:T(8,128)S(1)}, u32[]{:S(2)}, u32[]{:S(2)}) collective-permute-start(f32[8,8,8,128]{3,2,1,0:T(8,128)S(1)} %get-tuple-element.24.own_one), channel_id=1, source_target_pairs={{0,0},{1,2},{2,1},{3,4},{4,3},{5,6},{6,5},{7,7},{8,8},{9,10},{10,9... | collective-permute-start | bytes 786440 | tf_op jit(solution)/shard_map/ppermute | solution.py:423
  26.0 4.3 %collective-permute-start.4 = (f32[8,8,8,128]{3,2,1,0:T(8,128)S(1)}, f32[8,8,8,128]{3,2,1,0:T(8,128)S(1)}, u32[]{:S(2)}, u32[]{:S(2)}) collective-permute-start(f32[8,8,8,128]{3,2,1,0:T(8,128)S(1)} %get-tuple-element.24.own_one), channel_id=1, source_target_pairs={{0,1},{1,0},{2,3},{3,2},{4,5},{5,4},{6,7},{7,6},{8,9},{9,8},{10,11... | collective-permute-start | bytes 786440 | tf_op jit(solution)/shard_map/ppermute | solution.py:424
  27.8 6.4 %collective-permute-start.7 = (f32[8,8,8,128]{3,2,1,0:T(8,128)S(1)}, f32[8,8,8,128]{3,2,1,0:T(8,128)S(1)}, u32[]{:S(2)}, u32[]{:S(2)}) collective-permute-start(f32[8,8,8,128]{3,2,1,0:T(8,128)S(1)} %broadcast_select_fusion.1), channel_id=1, source_target_pairs={{3,2},{2,1},{1,0},{0,3},{4,5},{5,6},{6,7},{7,4},{11,10},{10,9},{9,... | collective-permute-start | bytes 786440 | tf_op jit(solution)/shard_map/ppermute | solution.py:428
  51.2 1.4 %collective-permute-start.8 = (f32[3,4,16,128]{3,2,1,0:T(8,128)S(1)}, f32[3,4,16,128]{3,2,1,0:T(8,128)S(1)}, u32[]{:S(2)}, u32[]{:S(2)}) collective-permute-start(f32[3,4,16,128]{3,2,1,0:T(8,128)S(1)} %bitcast.1), channel_id=1, source_target_pairs={{0,1},{1,0},{2,3},{3,2},{4,5},{5,4},{6,7},{7,6},{8,9},{9,8},{10,11... | collective-permute-start | bytes 294920 | tf_op jit(solution)/shard_map/ppermute | solution.py:504
